TPU v7x, 32 devices: a whole 2x2x4 slice. The times are simulated.
32 devices in a mesh: task: 4 (over y, x), dp: 8 (over z, core).
Axes of the slice: x: 2, y: 2, z: 4, core: 2. Of those that a mesh axis runs over, the one named last changes fastest.
Arguments:
- images: bfloat16 [144, 96, 512], P('dp'), may hold values from -6 to 6
- conv_first: float32 [3, 3, 512, 512], P(None, None, None, 'dp'), may hold values from -0.09375 to 0.09375
- conv_second: float32 [3, 3, 512, 512], P(None, None, None, 'dp'), may hold values from -0.09375 to 0.09375
- conv_third: float32 [3, 3, 512, 512], P(None, None, None, 'dp'), may hold values from -0.09375 to 0.09375
- trunk_gains: float32 [3, 512], replicated, may hold values from 0.1 to 1.9
- trunk_biases: float32 [3, 512], replicated, may hold values from -3 to 3
- attend_in: float32 [3, 512, 512], P(None, None, 'dp'), may hold values from -0.25 to 0.25
- attend_mask: float32 [3, 512, 512], P(None, None, 'dp'), may hold values from -0.25 to 0.25
- attend_out: float32 [3, 3, 3, 512, 512], P(None, None, None, None, 'dp'), may hold values from -0.09375 to 0.09375
- branch_gains: float32 [3, 3, 512], replicated, may hold values from 0.1 to 1.9
- branch_biases: float32 [3, 3, 512], replicated, may hold values from -3 to 3
- size_class: int32 [8], replicated, may hold values from 0 to 1, as said below
- domain_tags: int32 [8, 4], replicated, may hold values 0 or 1
- trunk_cotangent: bfloat16 [72, 48, 512], P('dp'), may hold values from -6 to 6
- task_cotangent: bfloat16 [3, 72, 48, 512], P(None, 'dp'), may hold values from -6 to 6
Outputs:
- trunk_features: bfloat16 [72, 48, 512], P('dp')
- task_features: bfloat16 [3, 72, 48, 512], P(None, 'dp')
- images_grad: float32 [144, 96, 512], P('dp')
- conv_first_grad: float32 [3, 3, 512, 512], P(None, None, None, 'dp')
- conv_second_grad: float32 [3, 3, 512, 512], P(None, None, None, 'dp')
- conv_third_grad: float32 [3, 3, 512, 512], P(None, None, None, 'dp')
- trunk_gains_grad: float32 [3, 512], replicated
- trunk_biases_grad: float32 [3, 512], replicated
- attend_in_grad: float32 [3, 512, 512], P(None, None, 'dp')
- attend_mask_grad: float32 [3, 512, 512], P(None, None, 'dp')
- attend_out_grad: float32 [3, 3, 3, 512, 512], P(None, None, None, None, 'dp')
- branch_gains_grad: float32 [3, 3, 512], replicated
- branch_biases_grad: float32 [3, 3, 512], replicated
Inputs may be any that keep to these rules, and one draw needn't show every extreme that they name: Of the slots 2k and 2k + 1 exactly one has size_class 0.
All inputs are finite; a program needn't handle non-finite values.
Results may differ from a plain program's by a relative error of at most 0.025.
Values may be sent and summed in bfloat16 or wider, within the bound.
No kernel may reach another device: no remote copies, remote signals or barrier semaphores. Data moves between devices by JAX's collectives and lax.ppermute only.
A program may use at most 192 MiB of HBM per device.

v0:
```python
import jax
import jax.numpy as jnp
from jax import lax
from jax.sharding import PartitionSpec as P

HEIGHT = 36
WIDTH = 48
BAND = 18
HALF_WIDTH = 24
CANVAS = 2
TASKS = 3


EPSILON = 1e-05
OFFSETS = ((-1, -1), (-1, 0), (-1, 1), (0, -1), (0, 0), (0, 1), (1, -1), (1, 0), (1, 1))


def partner(value, axis, apart):
    mask = 2**apart
    pairs = [(source, source ^ mask) for source in range(lax.axis_size(axis))]
    return lax.ppermute(value, axis, pairs)


def edge_of(values, dim, upper):
    length = values.shape[dim]
    first_edge = lax.slice_in_dim(values, 0, 1, axis=dim)
    last_edge = lax.slice_in_dim(values, length - 1, length, axis=dim)
    return jnp.where(upper, last_edge, first_edge)


def attach(values, received, dim, upper):
    empty = jnp.zeros_like(received)
    before = jnp.where(upper, empty, received)
    after = jnp.where(upper, received, empty)
    return jnp.concatenate([before, values, after], axis=dim)


def row_halo(values):
    upper = lax.axis_index("dp") % 2 == 0
    received = partner(edge_of(values, 0, upper), "dp", 0)
    return attach(values, received, 0, upper)


def block_halo(values):
    upper = lax.axis_index("dp") % 2 == 0
    received = partner(edge_of(values, 0, upper), "dp", 0)
    tall = attach(values, received, 0, upper)
    left = lax.axis_index("task") % 2 == 0
    beside = partner(edge_of(tall, 1, left), "task", 0)
    return attach(tall, beside, 1, left)


def domain_counts(size_class, domain_tags):
    big_area = HEIGHT * WIDTH
    small_area = BAND * HALF_WIDTH
    ones_count = jnp.sum(
        jnp.where(
            size_class == 0, big_area * domain_tags[:, 0], small_area * jnp.sum(domain_tags, axis=1)
        )
    )
    all_count = size_class.shape[0] * big_area
    return jnp.maximum(jnp.stack([all_count - ones_count, ones_count]).astype(jnp.float32), 1.0)


def build_masks(up_valid, down_valid, left_valid, right_valid, mask_type):
    result_list = []
    for row_step, col_step in OFFSETS:
        current = jnp.ones(up_valid.shape, jnp.bool_)
        if row_step == -1:
            current = current & up_valid
        if row_step == 1:
            current = current & down_valid
        if col_step == -1:
            current = current & left_valid
        if col_step == 1:
            current = current & right_valid
        result_list.append(current.astype(mask_type)[:, :, None])
    return result_list


def column_layout(column, local_class, local_tags, bottom_half, row_count):
    canvas_of = column // WIDTH
    in_canvas = column % WIDTH
    picker = (canvas_of[:, None] == jnp.arange(CANVAS)[None, :]).astype(jnp.int32)
    column_class = jnp.sum(picker * local_class[None, :], axis=1)
    column_tags = jnp.sum(picker[:, :, None] * local_tags[None, :, :], axis=1)
    small_class = column_class == 1
    big_class = jnp.logical_not(small_class)
    quarter = bottom_half * 2 + (in_canvas >= HALF_WIDTH).astype(jnp.int32)
    small_tag = jnp.sum(
        column_tags * (jnp.arange(4)[None, :] == quarter[:, None]).astype(jnp.int32), axis=1
    )
    domain = jnp.where(small_class, small_tag, column_tags[:, 0]).astype(jnp.float32)[None, :, None]
    row_number = jnp.arange(row_count)[:, None]
    up_valid = jnp.where(row_number == 0, (big_class & (bottom_half == 1))[None, :], True)
    down_valid = jnp.where(
        row_number == row_count - 1, (big_class & (bottom_half == 0))[None, :], True
    )
    left_valid = jnp.broadcast_to(
        ((in_canvas > 0) & jnp.logical_not(small_class & (in_canvas == HALF_WIDTH)))[None, :],
        up_valid.shape,
    )
    right_valid = jnp.broadcast_to(
        ((in_canvas < WIDTH - 1) & jnp.logical_not(small_class & (in_canvas == HALF_WIDTH - 1)))[
            None, :
        ],
        up_valid.shape,
    )
    return (domain, build_masks(up_valid, down_valid, left_valid, right_valid, jnp.bfloat16))


def shifted(padded, row_step, col_step, row_count, col_count, wide):
    picked = lax.slice_in_dim(padded, 1 + row_step, 1 + row_step + row_count, axis=0)
    if not wide:
        picked = jnp.pad(picked, ((0, 0), (1, 1), (0, 0)))
    return lax.slice_in_dim(picked, 1 + col_step, 1 + col_step + col_count, axis=1)


def conv_apply(padded, kernel, tap_masks, transpose, col_count, wide):
    row_count = padded.shape[0] - 2
    summed = None
    for tap_index, (row_step, col_step) in enumerate(OFFSETS):
        source = (
            shifted(padded, row_step, col_step, row_count, col_count, wide) * tap_masks[tap_index]
        )
        if transpose:
            term_value = jnp.einsum(
                "rwd,cd->rwc",
                source,
                kernel[1 - row_step, 1 - col_step],
                preferred_element_type=jnp.float32,
            )
        else:
            term_value = jnp.einsum(
                "rwc,cd->rwd",
                source,
                kernel[1 + row_step, 1 + col_step],
                preferred_element_type=jnp.float32,
            )
        summed = term_value if summed is None else summed + term_value
    return summed


def kernel_grad(padded, grad_low, tap_masks, wide):
    row_count, col_count = (grad_low.shape[0], grad_low.shape[1])
    pieces = []
    for tap_index, (row_step, col_step) in enumerate(OFFSETS):
        source = (
            shifted(padded, row_step, col_step, row_count, col_count, wide) * tap_masks[tap_index]
        )
        pieces.append(
            jnp.einsum("rwc,rwd->cd", source, grad_low, preferred_element_type=jnp.float32)
        )
    stacked = jnp.stack(pieces)
    return stacked.reshape(3, 3, stacked.shape[1], stacked.shape[2])


def norm_forward(values, domain, counts, gain, bias, trunk):
    other = 1.0 - domain
    squares = values * values
    sums = jnp.stack([jnp.sum(values * other, axis=(0, 1)), jnp.sum(values * domain, axis=(0, 1))])
    square_sums = jnp.stack(
        [jnp.sum(squares * other, axis=(0, 1)), jnp.sum(squares * domain, axis=(0, 1))]
    )
    if trunk:
        sums, square_sums = lax.psum((sums, square_sums), ("task", "dp"))
    else:
        sums, square_sums = lax.psum((sums, square_sums), "dp")
    means = sums / counts[:, None]
    variance = square_sums / counts[:, None] - means * means
    scales = lax.rsqrt(variance + EPSILON)
    mean_pixel = domain * means[1] + other * means[0]
    scale_pixel = domain * scales[1] + other * scales[0]
    normed = (values - mean_pixel) * scale_pixel
    return (normed * gain + bias, normed, scale_pixel)


def norm_backward(grad_out, normed, scale_pixel, domain, counts, gain, trunk):
    other = 1.0 - domain
    product = grad_out * normed
    plain_sums = jnp.stack(
        [jnp.sum(grad_out * other, axis=(0, 1)), jnp.sum(grad_out * domain, axis=(0, 1))]
    )
    cross_sums = jnp.stack(
        [jnp.sum(product * other, axis=(0, 1)), jnp.sum(product * domain, axis=(0, 1))]
    )
    if trunk:
        plain_sums, cross_sums = lax.psum((plain_sums, cross_sums), ("task", "dp"))
    else:
        plain_sums, cross_sums = lax.psum((plain_sums, cross_sums), "dp")
    plain_pixel = domain * plain_sums[1] + other * plain_sums[0]
    cross_pixel = domain * cross_sums[1] + other * cross_sums[0]
    count_pixel = domain * counts[1] + other * counts[0]
    grad_values = (
        scale_pixel * gain * (grad_out - (plain_pixel + normed * cross_pixel) / count_pixel)
    )
    return (grad_values, jnp.sum(cross_sums, axis=0), jnp.sum(plain_sums, axis=0))


def silu_back(shaped, grad_out):
    logistic = jax.nn.sigmoid(shaped)
    return grad_out * logistic * (1.0 + shaped * (1.0 - logistic))


def pool_mean(values):
    row_count, col_count, channels = values.shape
    return jnp.mean(values.reshape(row_count // 2, 2, col_count // 2, 2, channels), axis=(1, 3))


def spread_back(values):
    return jnp.repeat(jnp.repeat(values, 2, axis=0), 2, axis=1) * 0.25


def on_device(
    images,
    conv_first,
    conv_second,
    conv_third,
    trunk_gains,
    trunk_biases,
    attend_in,
    attend_mask,
    attend_out,
    branch_gains,
    branch_biases,
    size_class,
    domain_tags,
    trunk_cotangent,
    task_cotangent,
):
    row_count, col_count, channels = images.shape
    part_cols = col_count // lax.axis_size("task")
    position = lax.axis_index("dp")
    task_index = lax.axis_index("task")
    pair_index = position // 2
    bottom_half = position % 2
    local_class = lax.dynamic_slice_in_dim(size_class, pair_index * CANVAS, CANVAS, 0)
    local_tags = lax.dynamic_slice_in_dim(domain_tags, pair_index * CANVAS, CANVAS, 0)
    col_start = task_index * part_cols
    domain, tap_masks = column_layout(
        jnp.arange(col_count), local_class, local_tags, bottom_half, row_count
    )
    part_domain, part_masks = column_layout(
        col_start + jnp.arange(part_cols), local_class, local_tags, bottom_half, row_count
    )
    counts = domain_counts(size_class, domain_tags)
    masters = (
        conv_first.astype(jnp.bfloat16),
        conv_second.astype(jnp.bfloat16),
        conv_third.astype(jnp.bfloat16),
    )
    kernels = (
        lax.all_gather(masters[0], "dp", axis=3, tiled=True),
        lax.all_gather(masters[1], "dp", axis=3, tiled=True),
        lax.all_gather(masters[2], "dp", axis=3, tiled=True),
    )
    activation = lax.dynamic_slice_in_dim(images, col_start, part_cols, 1)
    saved_layers = []
    shared = None
    for layer_index in range(3):
        padded = block_halo(activation)
        summed = conv_apply(padded, kernels[layer_index], part_masks, False, part_cols, True)
        shaped, normed, scale_pixel = norm_forward(
            summed, part_domain, counts, trunk_gains[layer_index], trunk_biases[layer_index], True
        )
        saved_layers.append((padded, shaped, normed, scale_pixel))
        shared = jax.nn.silu(shaped)
        activation = shared.astype(jnp.bfloat16)
    part_pool = pool_mean(shared).astype(jnp.bfloat16)
    shared_low, trunk_features = (
        lax.all_gather(activation, "task", axis=1, tiled=True),
        lax.all_gather(part_pool, "task", axis=1, tiled=True),
    )
    branch = jnp.minimum(task_index, TASKS - 1)
    select = (jnp.arange(TASKS) == task_index).astype(jnp.float32)
    active = (task_index < TASKS).astype(jnp.float32)
    own_in = lax.dynamic_index_in_dim(attend_in, branch, 0, keepdims=False).astype(jnp.bfloat16)
    own_mask = lax.dynamic_index_in_dim(attend_mask, branch, 0, keepdims=False).astype(jnp.bfloat16)
    own_out = lax.dynamic_index_in_dim(attend_out, branch, 0, keepdims=False).astype(jnp.bfloat16)
    in_kernel, mask_kernel, out_kernel = (
        lax.all_gather(own_in, "dp", axis=1, tiled=True),
        lax.all_gather(own_mask, "dp", axis=1, tiled=True),
        lax.all_gather(own_out, "dp", axis=3, tiled=True),
    )
    own_gains = lax.dynamic_index_in_dim(branch_gains, branch, 0, keepdims=False)
    own_biases = lax.dynamic_index_in_dim(branch_biases, branch, 0, keepdims=False)
    first_sum = jnp.einsum("rwc,cd->rwd", shared_low, in_kernel, preferred_element_type=jnp.float32)
    first_shaped, first_normed, first_scale = norm_forward(
        first_sum, domain, counts, own_gains[0], own_biases[0], False
    )
    first_low = jax.nn.silu(first_shaped).astype(jnp.bfloat16)
    mask_sum = jnp.einsum("rwc,cd->rwd", first_low, mask_kernel, preferred_element_type=jnp.float32)
    mask_shaped, mask_normed, mask_scale = norm_forward(
        mask_sum, domain, counts, own_gains[1], own_biases[1], False
    )
    gate_value = jax.nn.sigmoid(mask_shaped)
    shared_wide = shared_low.astype(jnp.float32)
    masked_low = (shared_wide * gate_value).astype(jnp.bfloat16)
    padded_masked = row_halo(masked_low)
    last_sum = conv_apply(padded_masked, out_kernel, tap_masks, False, col_count, False)
    last_shaped, last_normed, last_scale = norm_forward(
        last_sum, domain, counts, own_gains[2], own_biases[2], False
    )
    branch_pool = pool_mean(jax.nn.silu(last_shaped))
    own_cotangent = lax.dynamic_index_in_dim(task_cotangent, branch, 0, keepdims=False).astype(
        jnp.float32
    )
    grad_last = silu_back(last_shaped, spread_back(own_cotangent))
    grad_last_sum, last_gain_grad, last_bias_grad = norm_backward(
        grad_last, last_normed, last_scale, domain, counts, own_gains[2], False
    )
    grad_last_low = grad_last_sum.astype(jnp.bfloat16)
    grad_out_kernel = kernel_grad(padded_masked, grad_last_low, tap_masks, False)
    grad_masked = conv_apply(row_halo(grad_last_low), out_kernel, tap_masks, True, col_count, False)
    grad_gate = grad_masked * shared_wide
    grad_shared = grad_masked * gate_value
    grad_mask_shaped = grad_gate * gate_value * (1.0 - gate_value)
    grad_mask_sum, mask_gain_grad, mask_bias_grad = norm_backward(
        grad_mask_shaped, mask_normed, mask_scale, domain, counts, own_gains[1], False
    )
    grad_mask_low = grad_mask_sum.astype(jnp.bfloat16)
    grad_mask_kernel = jnp.einsum(
        "rwc,rwd->cd", first_low, grad_mask_low, preferred_element_type=jnp.float32
    )
    grad_first_act = jnp.einsum(
        "rwd,cd->rwc", grad_mask_low, mask_kernel, preferred_element_type=jnp.float32
    )
    grad_first = silu_back(first_shaped, grad_first_act)
    grad_first_sum, first_gain_grad, first_bias_grad = norm_backward(
        grad_first, first_normed, first_scale, domain, counts, own_gains[0], False
    )
    grad_first_low = grad_first_sum.astype(jnp.bfloat16)
    grad_in_kernel = jnp.einsum(
        "rwc,rwd->cd", shared_low, grad_first_low, preferred_element_type=jnp.float32
    )
    grad_shared = grad_shared + jnp.einsum(
        "rwd,cd->rwc", grad_first_low, in_kernel, preferred_element_type=jnp.float32
    )
    branch_part = lax.psum_scatter(
        (grad_shared * active).astype(jnp.bfloat16), "task", scatter_dimension=1, tiled=True
    ).astype(jnp.float32)
    branch_shards = (
        lax.psum_scatter(
            grad_in_kernel.astype(jnp.bfloat16), "dp", scatter_dimension=1, tiled=True
        ).astype(jnp.float32),
        lax.psum_scatter(
            grad_mask_kernel.astype(jnp.bfloat16), "dp", scatter_dimension=1, tiled=True
        ).astype(jnp.float32),
        lax.psum_scatter(
            grad_out_kernel.astype(jnp.bfloat16), "dp", scatter_dimension=3, tiled=True
        ).astype(jnp.float32),
    )
    part_cotangent = lax.dynamic_slice_in_dim(
        trunk_cotangent, task_index * (part_cols // 2), part_cols // 2, 1
    )
    grad_value = spread_back(part_cotangent.astype(jnp.float32)) + branch_part
    kernel_grads = [None, None, None]
    gain_grads = [None, None, None]
    bias_grads = [None, None, None]
    for layer_index in (2, 1, 0):
        padded, shaped, normed, scale_pixel = saved_layers[layer_index]
        grad_shaped = silu_back(shaped, grad_value)
        grad_summed, gain_grads[layer_index], bias_grads[layer_index] = norm_backward(
            grad_shaped, normed, scale_pixel, part_domain, counts, trunk_gains[layer_index], True
        )
        grad_low = grad_summed.astype(jnp.bfloat16)
        full_grad = kernel_grad(padded, grad_low, part_masks, True)
        kernel_grads[layer_index] = full_grad
        grad_value = conv_apply(
            block_halo(grad_low), kernels[layer_index], part_masks, True, part_cols, True
        )
    kernel_grads = (
        lax.psum_scatter(
            kernel_grads[0].astype(jnp.bfloat16), "dp", scatter_dimension=3, tiled=True
        ).astype(jnp.float32),
        lax.psum_scatter(
            kernel_grads[1].astype(jnp.bfloat16), "dp", scatter_dimension=3, tiled=True
        ).astype(jnp.float32),
        lax.psum_scatter(
            kernel_grads[2].astype(jnp.bfloat16), "dp", scatter_dimension=3, tiled=True
        ).astype(jnp.float32),
    )
    image_pad = lax.dynamic_update_slice_in_dim(
        jnp.zeros((row_count, col_count, channels), jnp.float32), grad_value, col_start, 1
    )
    pooled_pad = select[:, None, None, None] * branch_pool[None]
    in_pad = select[:, None, None] * branch_shards[0][None]
    mask_pad = select[:, None, None] * branch_shards[1][None]
    out_pad = select[:, None, None, None, None] * branch_shards[2][None]
    gain_pad = (
        select[:, None, None] * jnp.stack([first_gain_grad, mask_gain_grad, last_gain_grad])[None]
    )
    bias_pad = (
        select[:, None, None] * jnp.stack([first_bias_grad, mask_bias_grad, last_bias_grad])[None]
    )
    collected = (
        lax.psum(pooled_pad.astype(jnp.bfloat16), "task").astype(jnp.float32),
        lax.psum(in_pad.astype(jnp.bfloat16), "task").astype(jnp.float32),
        lax.psum(mask_pad.astype(jnp.bfloat16), "task").astype(jnp.float32),
        lax.psum(out_pad.astype(jnp.bfloat16), "task").astype(jnp.float32),
        lax.psum(gain_pad.astype(jnp.bfloat16), "task").astype(jnp.float32),
        lax.psum(bias_pad.astype(jnp.bfloat16), "task").astype(jnp.float32),
        lax.psum(image_pad.astype(jnp.bfloat16), "task").astype(jnp.float32),
        lax.psum(kernel_grads[0].astype(jnp.bfloat16), "task").astype(jnp.float32),
        lax.psum(kernel_grads[1].astype(jnp.bfloat16), "task").astype(jnp.float32),
        lax.psum(kernel_grads[2].astype(jnp.bfloat16), "task").astype(jnp.float32),
    )
    return (
        trunk_features,
        collected[0].astype(jnp.bfloat16),
        collected[6],
        collected[7],
        collected[8],
        collected[9],
        jnp.stack(gain_grads),
        jnp.stack(bias_grads),
        collected[1],
        collected[2],
        collected[3],
        collected[4],
        collected[5],
    )


def solution(mesh):
    in_specs = (
        P("dp", None, None),
        P(None, None, None, "dp"),
        P(None, None, None, "dp"),
        P(None, None, None, "dp"),
        P(),
        P(),
        P(None, None, "dp"),
        P(None, None, "dp"),
        P(None, None, None, None, "dp"),
        P(),
        P(),
        P(),
        P(),
        P("dp", None, None),
        P(None, "dp", None, None),
    )
    out_specs = (
        P("dp", None, None),
        P(None, "dp", None, None),
        P("dp", None, None),
        P(None, None, None, "dp"),
        P(None, None, None, "dp"),
        P(None, None, None, "dp"),
        P(),
        P(),
        P(None, None, "dp"),
        P(None, None, "dp"),
        P(None, None, None, None, "dp"),
        P(),
        P(),
    )
    return jax.shard_map(
        on_device, mesh=mesh, in_specs=in_specs, out_specs=out_specs, check_vma=False
    )
```

profile of v0, /device:TPU:0, one launch (start us, length us, event | category | flops | bytes accessed | tf_op | source)
XLA Modules:
  0.0 1143.2 jit_solution(5399603395539435636)
XLA Ops:
  30.6 2.5 collective-permute-start.1
  35.5 2.6 pad_maximum_fusion.4
  38.0 26.6 %all-gather.9.cloned.1.call-done = bf16[3,3,512,512]{2,3,1,0:T(8,128)(2,1)} async-done(((bf16[3,3,512,64]{2,3,1,0:T(8,128)(2,1)}), bf16[3,3,512,512]{2,3,1,0:T(8,128)(2,1)}) %all-gather.9.cloned.1.call-update) | async-done | bytes 4718608 | tf_op jit(solution)/shard_map/all_gather | solution.py:253
  75.0 42.8 %all-reduce.13 = (f32[2,512]{1,0:T(2,128)}, f32[2,512]{1,0:T(2,128)}) all-reduce(f32[2,512]{1,0:T(2,128)} %pad_maximum_fusion.38, f32[2,512]{1,0:T(2,128)} %pad_maximum_fusion.39), channel_id=1, replica_groups=mesh['task'=4,'dp'=8] {'task','dp'}, use_global_device_ids=true, to_apply=%region_5.6 | all-reduce | flops 2048 | bytes 16384 | tf_op jit(solution)/shard_map/psum | solution.py:166
  141.9 51.6 %all-reduce.12 = (f32[2,512]{1,0:T(2,128)S(1)}, f32[2,512]{1,0:T(2,128)S(1)}) all-reduce(f32[2,512]{1,0:T(2,128)S(1)} %pad_maximum_fusion.40, f32[2,512]{1,0:T(2,128)S(1)} %pad_maximum_fusion.41), channel_id=1, replica_groups=mesh['task'=4,'dp'=8] {'task','dp'}, use_global_device_ids=true, to_apply=%region_13.14 | all-reduce | flops 2048 | bytes 16384 | tf_op jit(solution)/shard_map/psum | solution.py:166
  199.6 3.0 broadcast_in_dim.98
  202.7 5.4 mul.2522
  219.8 38.9 %all-reduce.11 = (f32[2,512]{1,0:T(2,128)S(1)}, f32[2,512]{1,0:T(2,128)S(1)}) all-reduce(f32[2,512]{1,0:T(2,128)S(1)} %pad_maximum_fusion.42, f32[2,512]{1,0:T(2,128)S(1)} %pad_maximum_fusion.43), channel_id=1, replica_groups=mesh['task'=4,'dp'=8] {'task','dp'}, use_global_device_ids=true, to_apply=%region_19.20 | all-reduce | flops 2048 | bytes 16384 | tf_op jit(solution)/shard_map/psum | solution.py:166
  268.7 15.7 %all-gather = bf16[1,512,512]{1,2,0:T(8,128)(2,1)} all-gather(bf16[1,512,64]{1,2,0:T(8,128)(2,1)S(1)} %dynamic-slice_convert_fusion.2), channel_id=2, replica_groups=mesh['task'=4,'dp'=8] {'dp'}, dimensions={2}, use_global_device_ids=true | all-gather | bytes 589824 | tf_op jit(solution)/shard_map/all_gather | solution.py:281
  284.5 15.8 %all-gather.1 = bf16[1,512,512]{1,2,0:T(8,128)(2,1)} all-gather(bf16[1,512,64]{1,2,0:T(8,128)(2,1)S(1)} %dynamic-slice_convert_fusion.1), channel_id=3, replica_groups=mesh['task'=4,'dp'=8] {'dp'}, dimensions={2}, use_global_device_ids=true | all-gather | bytes 589824 | tf_op jit(solution)/shard_map/all_gather | solution.py:282
  300.3 6.7 copy.190
  307.0 3.4 multiply_reduce_fusion.21
  312.1 16.3 %all-reduce.19 = (f32[2,512]{1,0:T(2,128)}, f32[2,512]{1,0:T(2,128)}) all-reduce(f32[2,512]{1,0:T(2,128)} %pad_maximum_fusion.44, f32[2,512]{1,0:T(2,128)} %pad_maximum_fusion.45), channel_id=1, replica_groups=mesh['task'=4,'dp'=8] {'dp'}, use_global_device_ids=true, to_apply=%region_29.30 | all-reduce | flops 2048 | bytes 16384 | tf_op jit(solution)/shard_map/psum | solution.py:168
  332.5 2.5 multiply_reduce_fusion.17
  336.2 15.0 %all-reduce.18 = (f32[2,512]{1,0:T(2,128)}, f32[2,512]{1,0:T(2,128)}) all-reduce(f32[2,512]{1,0:T(2,128)} %pad_maximum_fusion.46, f32[2,512]{1,0:T(2,128)} %pad_maximum_fusion.47), channel_id=1, replica_groups=mesh['task'=4,'dp'=8] {'dp'}, use_global_device_ids=true, to_apply=%region_35.36 | all-reduce | flops 2048 | bytes 16384 | tf_op jit(solution)/shard_map/psum | solution.py:168
  353.6 2.9 fusion
  356.6 2.5 fusion.221
  359.1 2.9 fusion.176
  362.1 3.0 fusion.177
  365.8 2.9 fusion.174
  368.7 2.9 fusion.175
  372.7 2.9 fusion.178
  375.7 2.9 fusion.179
  378.7 10.6 multiply_reduce_fusion.13
  390.5 14.8 %all-reduce.17 = (f32[2,512]{1,0:T(2,128)}, f32[2,512]{1,0:T(2,128)}) all-reduce(f32[2,512]{1,0:T(2,128)} %pad_maximum_fusion.48, f32[2,512]{1,0:T(2,128)} %pad_maximum_fusion.49), channel_id=1, replica_groups=mesh['task'=4,'dp'=8] {'dp'}, use_global_device_ids=true, to_apply=%region_41.42 | all-reduce | flops 2048 | bytes 16384 | tf_op jit(solution)/shard_map/psum | solution.py:168
  407.6 6.7 multiply_reduce_fusion.9
  415.5 14.6 %all-reduce.16 = (f32[2,512]{1,0:T(2,128)}, f32[2,512]{1,0:T(2,128)}) all-reduce(f32[2,512]{1,0:T(2,128)} %pad_maximum_fusion.51, f32[2,512]{1,0:T(2,128)} %pad_maximum_fusion.50), channel_id=1, replica_groups=mesh['task'=4,'dp'=8] {'dp'}, use_global_device_ids=true, to_apply=%region_52.53 | all-reduce | flops 2048 | bytes 16384 | tf_op jit(solution)/shard_map/psum | solution.py:190
  432.4 4.4 multiply_convert_fusion.4
  436.9 4.5 fusion.14
  441.4 3.9 fusion.220
  445.3 2.9 fusion.17
  448.9 2.9 fusion.20
  453.0 3.0 fusion.25
  456.0 2.9 fusion.11
  459.0 2.9 fusion.7
  462.0 14.1 %multiply_reduce_fusion.5 = (f32[512]{0:T(512)S(1)}, f32[512]{0:T(512)S(1)}, f32[512]{0:T(512)S(1)}, f32[512]{0:T(512)S(1)}, f32[18,96,512]{2,1,0:T(8,128)}, /*index=5*/f32[18,96,512]{2,1,0:T(8,128)}) fusion(f32[96]{0:T(128)S(1)} %copy-done.127, f32[96,512]{1,0:T(8,128)S(1)} %copy-done.50, f32[18,96,512]{2,1,0:T(8,128)S(1)} %get-tuple-element.357, ...), kind=kOutput, calls=%fused_computation.15 | convolution fusion | flops 932509696 | bytes 43401344 | tf_op jit(solution)/shard_map/rwd,cd->rwc/dot_general | solution.py:127
  477.3 15.0 %all-reduce.15 = (f32[2,512]{1,0:T(2,128)}, f32[2,512]{1,0:T(2,128)}) all-reduce(f32[2,512]{1,0:T(2,128)} %pad_maximum_fusion.53, f32[2,512]{1,0:T(2,128)} %pad_maximum_fusion.52), channel_id=1, replica_groups=mesh['task'=4,'dp'=8] {'dp'}, use_global_device_ids=true, to_apply=%region_58.59 | all-reduce | flops 2048 | bytes 16384 | tf_op jit(solution)/shard_map/psum | solution.py:190
  494.7 3.5 multiply_convert_fusion.3
  498.2 4.6 multiply_reduce_fusion.1
  504.0 14.6 %all-reduce.14 = (f32[2,512]{1,0:T(2,128)}, f32[2,512]{1,0:T(2,128)}) all-reduce(f32[2,512]{1,0:T(2,128)} %pad_maximum_fusion.55, f32[2,512]{1,0:T(2,128)} %pad_maximum_fusion.54), channel_id=1, replica_groups=mesh['task'=4,'dp'=8] {'dp'}, use_global_device_ids=true, to_apply=%region_64.65 | all-reduce | flops 2048 | bytes 16384 | tf_op jit(solution)/shard_map/psum | solution.py:190
  521.0 4.4 multiply_convert_fusion.2
  526.7 3.3 multiply_convert_fusion.1
  530.5 4.4 fusion.173
  545.2 2.8 fusion.165
  550.3 2.8 fusion.163
  557.2 11.0 copy.194
  568.4 24.9 %all-reduce.26.cloned.1.call-done = bf16[18,96,512]{2,1,0:T(8,128)(2,1)} async-done(((bf16[18,96,512]{2,1,0:T(8,128)(2,1)}), bf16[18,96,512]{2,1,0:T(8,128)(2,1)}) %all-reduce.26.cloned.1.call-update) | async-done | bytes 1769488
  593.4 2.6 multiply_reduce_fusion.33
  596.1 39.7 %all-reduce.10 = (f32[2,512]{1,0:T(2,128)S(1)}, f32[2,512]{1,0:T(2,128)S(1)}) all-reduce(f32[2,512]{1,0:T(2,128)S(1)} %pad_maximum_fusion.57, f32[2,512]{1,0:T(2,128)S(1)} %pad_maximum_fusion.56), channel_id=1, replica_groups=mesh['task'=4,'dp'=8] {'task','dp'}, use_global_device_ids=true, to_apply=%region_71.72 | all-reduce | flops 2048 | bytes 16384 | tf_op jit(solution)/shard_map/psum | solution.py:188
  650.2 6.7 copy.193
  675.6 3.1 multiply_reduce_fusion.29
  678.7 42.3 %all-reduce.9 = (f32[2,512]{1,0:T(2,128)S(1)}, f32[2,512]{1,0:T(2,128)S(1)}) all-reduce(f32[2,512]{1,0:T(2,128)S(1)} %pad_maximum_fusion.59, f32[2,512]{1,0:T(2,128)S(1)} %pad_maximum_fusion.58), channel_id=1, replica_groups=mesh['task'=4,'dp'=8] {'task','dp'}, use_global_device_ids=true, to_apply=%region_77.78 | all-reduce | flops 2048 | bytes 16384 | tf_op jit(solution)/shard_map/psum | solution.py:188
  735.5 6.7 copy.192
  761.2 3.1 multiply_reduce_fusion.25
  764.3 40.0 %all-reduce.8 = (f32[2,512]{1,0:T(2,128)S(1)}, f32[2,512]{1,0:T(2,128)S(1)}) all-reduce(f32[2,512]{1,0:T(2,128)S(1)} %pad_maximum_fusion.61, f32[2,512]{1,0:T(2,128)S(1)} %pad_maximum_fusion.60), channel_id=1, replica_groups=mesh['task'=4,'dp'=8] {'task','dp'}, use_global_device_ids=true, to_apply=%region_83.84 | all-reduce | flops 2048 | bytes 16384 | tf_op jit(solution)/shard_map/psum | solution.py:188
  818.9 6.7 copy.191
  827.5 5.3 reshape.2693
  832.8 4.7 reduce_sum.663
  863.6 46.8 %reduce-scatter.9.cloned.1.call-done = bf16[3,3,512,64]{2,3,1,0:T(8,128)(2,1)} async-done(((bf16[3,3,512,512]{2,3,1,0:T(8,128)(2,1)}), bf16[3,3,512,64]{2,3,1,0:T(8,128)(2,1)}) %reduce-scatter.9.cloned.1.call-update) | async-done | bytes 589840 | tf_op jit(solution)/shard_map/reduce_scatter | solution.py:376
  910.4 55.5 %reduce-scatter.7.cloned.1.call-done = bf16[3,3,512,64]{2,3,1,0:T(8,128)(2,1)} async-done(((bf16[3,3,512,512]{2,3,1,0:T(8,128)(2,1)}), bf16[3,3,512,64]{2,3,1,0:T(8,128)(2,1)}) %reduce-scatter.7.cloned.1.call-update) | async-done | bytes 589840 | tf_op jit(solution)/shard_map/reduce_scatter | solution.py:373
  967.3 16.5 %all_gather.27 = bf16[9,48,512]{2,0,1:T(8,128)(2,1)S(1)} all-gather(bf16[9,12,512]{2,0,1:T(8,128)(2,1)S(1)} %copy.186), channel_id=1, replica_groups=mesh['task'=4,'dp'=8] {'task'}, dimensions={1}, use_global_device_ids=true | all-gather | bytes 552960 | tf_op jit(solution)/shard_map/all_gather | solution.py:272
  985.1 16.2 %all-reduce.20 = (bf16[3,3,512]{2,1,0:T(4,128)(2,1)S(1)}, bf16[3,3,512]{2,1,0:T(4,128)(2,1)S(1)}) all-reduce(bf16[3,3,512]{2,1,0:T(4,128)(2,1)S(1)} %get-tuple-element.339, bf16[3,3,512]{2,1,0:T(4,128)(2,1)S(1)} %get-tuple-element.338), channel_id=1, replica_groups=mesh['task'=4,'dp'=8] {'task'}, use_global_device_ids=true, to_apply=%region_106.107 | all-reduce | flops 9216 | bytes 36864 | tf_op jit(solution)/shard_map/psum | solution.py:401
  1003.8 120.3 %all-reduce.30.cloned.1.call-done = (bf16[3,9,48,512]{3,2,1,0:T(8,128)(2,1)}, bf16[18,96,512]{2,1,0:T(8,128)(2,1)}, bf16[3,3,512,64]{2,3,1,0:T(8,128)(2,1)}, bf1...) async-done(((bf16[3,9,48,512]{3,2,1,0:T(8,128)(2,1)}, ...) | async-done | bytes 7028752 | tf_op jit(solution)/shard_map/psum | solution.py:397
  1124.2 3.9 convert_element_type.426
  (845 shorter events, 252.2 us)
Async XLA Ops:
  7.2 122.7 %copy-start = (f32[3,3,3,512,64]{3,4,2,1,0:T(8,128)S(1)}, f32[3,3,3,512,64]{3,4,2,1,0:T(8,128)}, u32[]{:S(2)}) copy-start(f32[3,3,3,512,64]{3,4,2,1,0:T(8,128)} %param.23) | copy-start | bytes 10616836
  7.2 57.4 %all-gather.9.cloned.1.call-start = ((), (), s32[]{:S(2)}) async-start(), calls=%async_computation.5 | async-start | bytes 5308416 | tf_op jit(solution)/shard_map/all_gather | solution.py:253
  9.6 125.0 %all-gather.11.cloned.1.call-start = ((), (), s32[]{:S(2)}) async-start(), calls=%async_computation.6 | async-start | bytes 5308416 | tf_op jit(solution)/shard_map/all_gather | solution.py:254
  11.8 200.7 %all-gather.13.cloned.1.call-start = ((), (), s32[]{:S(2)}) async-start(), calls=%async_computation.7 | async-start | bytes 5308416 | tf_op jit(solution)/shard_map/all_gather | solution.py:255
  14.1 286.2 %all-gather.17.cloned.1.call-start = ((), (), s32[]{:S(2)}) async-start(), calls=%async_computation.14 | async-start | bytes 5308416 | tf_op jit(solution)/shard_map/all_gather | solution.py:283
  15.5 13.2 %collective-permute-start = (bf16[1,24,512]{2,1,0:T(8,128)(2,1)}, bf16[1,24,512]{2,1,0:T(8,128)(2,1)}, u32[]{:S(2)}, u32[]{:S(2)}) collective-permute-start(bf16[1,24,512]{2,1,0:T(8,128)(2,1)} %dynamic-slice_select_fusion), channel_id=1, source_target_pairs={{0,1},{1,0},{2,3},{3,2},{4,5},{5,4},{6,7},{7,6},{8,9},{9,8},{10,11... | collective-permute-start | bytes 73736 | tf_op jit(solution)/shard_map/ppermute | solution.py:21
  30.6 4.8 collective-permute-start.1
  123.0 1.5 collective-permute-start.2
  127.6 4.6 collective-permute-start.3
  130.8 176.1 %all-gather.15.cloned.1.call-start = ((), (), s32[]{:S(2)}) async-start(), calls=%async_computation.8 | async-start | bytes 2211840 | tf_op jit(solution)/shard_map/all_gather | solution.py:271
  141.1 52.4 %copy-start.143 = (f32[2]{0:T(128)S(1)}, f32[2]{0:T(128)}, u32[]{:S(2)}) copy-start(f32[2]{0:T(128)} %copy-done.142) | copy-start | bytes 28
  141.1 52.5 %copy-start.131 = (f32[24]{0:T(128)S(1)}, f32[24]{0:T(128)}, u32[]{:S(2)}) copy-start(f32[24]{0:T(128)} %get-tuple-element.161) | copy-start | bytes 292
  141.1 52.5 %copy-start.147 = (f32[24]{0:T(128)S(1)}, f32[24]{0:T(128)}, u32[]{:S(2)}) copy-start(f32[24]{0:T(128)} %broadcast_subtract_fusion.1) | copy-start | bytes 292
  141.1 52.5 %copy-start.182 = (f32[1,512]{1,0:T(1,128)S(1)}, f32[1,512]{1,0:T(1,128)}, u32[]{:S(2)}) copy-start(f32[1,512]{1,0:T(1,128)} %get-tuple-element.239) | copy-start | bytes 6148
  141.1 53.2 %copy-start.209 = (f32[1,512]{1,0:T(1,128)S(1)}, f32[1,512]{1,0:T(1,128)}, u32[]{:S(2)}) copy-start(f32[1,512]{1,0:T(1,128)} %get-tuple-element.242) | copy-start | bytes 6148
  141.8 57.6 %copy-start.46 = (f32[18,24,512]{2,1,0:T(8,128)}, f32[18,24,512]{2,1,0:T(8,128)S(1)}, u32[]{:S(2)}) copy-start(f32[18,24,512]{2,1,0:T(8,128)S(1)} %get-tuple-element.354) | copy-start | bytes 2654212
  194.6 1.3 collective-permute-start.4
  196.1 15.2 %collective-permute-start.5 = (bf16[20,1,512]{2,1,0:T(2,128)(2,1)S(1)}, bf16[20,1,512]{2,1,0:T(2,128)(2,1)}, u32[]{:S(2)}, u32[]{:S(2)}) collective-permute-start(bf16[20,1,512]{2,1,0:T(2,128)(2,1)S(1)} %broadcast_select_fusion.15), channel_id=1, source_target_pairs={{0,8},{8,0},{16,24},{24,16},{1,9},{9,1},{17,25},{25,17},{2,10},{10... | collective-permute-start | bytes 61448 | tf_op jit(solution)/shard_map/ppermute | solution.py:21
  219.1 43.4 %copy-start.244 = (s32[2]{0:T(128)S(1)}, s32[2]{0:T(128)}, u32[]{:S(2)}) copy-start(s32[2]{0:T(128)} %dynamic_slice.35) | copy-start | bytes 28
  219.1 48.3 %copy-start.235 = (pred[18]{0:T(512)(128)(4,1)S(1)}, pred[18]{0:T(512)(128)(4,1)}, u32[]{:S(2)}) copy-start(pred[18]{0:T(512)(128)(4,1)} %copy-done.234) | copy-start | bytes 58
  219.1 48.9 %copy-start.233 = (pred[18]{0:T(512)(128)(4,1)S(1)}, pred[18]{0:T(512)(128)(4,1)}, u32[]{:S(2)}) copy-start(pred[18]{0:T(512)(128)(4,1)} %copy-done.232) | copy-start | bytes 58
  219.8 87.2 %copy-start.18 = (f32[18,24,512]{2,1,0:T(8,128)}, f32[18,24,512]{2,1,0:T(8,128)S(1)}, u32[]{:S(2)}) copy-start(f32[18,24,512]{2,1,0:T(8,128)S(1)} %get-tuple-element.355) | copy-start | bytes 2654212
  259.5 47.4 %copy-start.69 = (f32[24,512]{1,0:T(8,128)}, f32[24,512]{1,0:T(8,128)S(1)}, u32[]{:S(2)}) copy-start(f32[24,512]{1,0:T(8,128)S(1)} %get-tuple-element.250) | copy-start | bytes 147460
  259.5 47.4 %copy-start.71 = (f32[24,512]{1,0:T(8,128)}, f32[24,512]{1,0:T(8,128)S(1)}, u32[]{:S(2)}) copy-start(f32[24,512]{1,0:T(8,128)S(1)} %get-tuple-element.311) | copy-start | bytes 147460
  260.9 332.4 %all-reduce.26.cloned.1.call-start = ((), (), s32[]{:S(2)}) async-start(), calls=%async_computation.15 | async-start | bytes 3538944
  356.5 8.6 collective-permute-start.6
  445.3 2.9 collective-permute-start.7
  530.0 309.0 %reduce-scatter.15.cloned.1.call-start = ((), (), s32[]{:S(2)}) async-start(), calls=%async_computation.13 | async-start | bytes 589824 | tf_op jit(solution)/shard_map/reduce_scatter | solution.py:346
  543.2 296.7 %reduce-scatter.13.cloned.1.call-start = ((), (), s32[]{:S(2)}) async-start(), calls=%async_computation.12 | async-start | bytes 589824 | tf_op jit(solution)/shard_map/reduce_scatter | solution.py:343
  550.1 309.6 %all-reduce.28.cloned.1.call-start = ((), (), s32[]{:S(2)}) async-start(), calls=%async_computation.16 | async-start | bytes 12582912
  568.3 68.1 %copy-start.115 = (f32[24,512]{1,0:T(8,128)S(1)}, f32[24,512]{1,0:T(8,128)}, u32[]{:S(2)}) copy-start(f32[24,512]{1,0:T(8,128)} %get-tuple-element.249) | copy-start | bytes 147460
  568.3 68.1 %copy-start.213 = (f32[24]{0:T(128)S(1)}, f32[24]{0:T(128)}, u32[]{:S(2)}) copy-start(f32[24]{0:T(128)} %get-tuple-element.160) | copy-start | bytes 292
  568.3 69.5 %copy-start.40 = (bf16[20,25,512]{2,1,0:T(8,128)(2,1)S(1)}, bf16[20,25,512]{2,1,0:T(8,128)(2,1)}, u32[]{:S(2)}) copy-start(bf16[20,25,512]{2,1,0:T(8,128)(2,1)} %copy-done.39) | copy-start | bytes 1536004
  568.3 69.5 %copy-start.217 = (bf16[18,24]{1,0:T(8,128)(2,1)S(1)}, bf16[18,24]{1,0:T(8,128)(2,1)}, u32[]{:S(2)}) copy-start(bf16[18,24]{1,0:T(8,128)(2,1)} %get-tuple-element.334) | copy-start | bytes 2596
  568.4 295.2 %reduce-scatter.11.cloned.1.call-start = ((), (), s32[]{:S(2)}) async-start(), calls=%async_computation.11 | async-start | bytes 5308416 | tf_op jit(solution)/shard_map/reduce_scatter | solution.py:379
  656.9 253.5 %reduce-scatter.9.cloned.1.call-start = ((), (), s32[]{:S(2)}) async-start(), calls=%async_computation.10 | async-start | bytes 5308416 | tf_op jit(solution)/shard_map/reduce_scatter | solution.py:376
  657.1 1.3 collective-permute-start.8
  658.5 4.3 collective-permute-start.9
  675.5 46.1 %copy-start.135 = (f32[24]{0:T(128)S(1)}, f32[24]{0:T(128)}, u32[]{:S(2)}) copy-start(f32[24]{0:T(128)} %get-tuple-element.161) | copy-start | bytes 292
  675.5 46.1 %copy-start.151 = (f32[24]{0:T(128)S(1)}, f32[24]{0:T(128)}, u32[]{:S(2)}) copy-start(f32[24]{0:T(128)} %broadcast_subtract_fusion.1) | copy-start | bytes 292
  675.5 46.2 %copy-start.48 = (f32[18,24,512]{2,1,0:T(8,128)S(1)}, f32[18,24,512]{2,1,0:T(8,128)}, u32[]{:S(2)}) copy-start(f32[18,24,512]{2,1,0:T(8,128)} %copy-done.46) | copy-start | bytes 2654212
  675.6 46.2 %copy-start.87 = (f32[24,512]{1,0:T(8,128)S(1)}, f32[24,512]{1,0:T(8,128)}, u32[]{:S(2)}) copy-start(f32[24,512]{1,0:T(8,128)} %copy-done.85) | copy-start | bytes 147460
  675.6 46.2 %copy-start.90 = (f32[24,512]{1,0:T(8,128)S(1)}, f32[24,512]{1,0:T(8,128)}, u32[]{:S(2)}) copy-start(f32[24,512]{1,0:T(8,128)} %copy-done.88) | copy-start | bytes 147460
  675.6 46.2 %copy-start.114 = (f32[24,512]{1,0:T(8,128)S(1)}, f32[24,512]{1,0:T(8,128)}, u32[]{:S(2)}) copy-start(f32[24,512]{1,0:T(8,128)} %get-tuple-element.247) | copy-start | bytes 147460
  675.6 46.2 %copy-start.214 = (f32[24]{0:T(128)S(1)}, f32[24]{0:T(128)}, u32[]{:S(2)}) copy-start(f32[24]{0:T(128)} %get-tuple-element.160) | copy-start | bytes 292
  675.6 47.6 %copy-start.36 = (bf16[20,25,512]{2,1,0:T(8,128)(2,1)S(1)}, bf16[20,25,512]{2,1,0:T(8,128)(2,1)}, u32[]{:S(2)}) copy-start(bf16[20,25,512]{2,1,0:T(8,128)(2,1)} %copy-done.35) | copy-start | bytes 1536004
  675.6 47.6 %copy-start.219 = (bf16[18,24]{1,0:T(8,128)(2,1)S(1)}, bf16[18,24]{1,0:T(8,128)(2,1)}, u32[]{:S(2)}) copy-start(bf16[18,24]{1,0:T(8,128)(2,1)} %get-tuple-element.334) | copy-start | bytes 2596
  742.2 223.6 %reduce-scatter.7.cloned.1.call-start = ((), (), s32[]{:S(2)}) async-start(), calls=%async_computation.9 | async-start | bytes 5308416 | tf_op jit(solution)/shard_map/reduce_scatter | solution.py:373
  742.7 1.3 collective-permute-start.10
  744.1 4.3 collective-permute-start.11
  761.1 43.8 %copy-start.137 = (f32[24]{0:T(128)S(1)}, f32[24]{0:T(128)}, u32[]{:S(2)}) copy-start(f32[24]{0:T(128)} %get-tuple-element.161) | copy-start | bytes 292
  761.1 43.8 %copy-start.153 = (f32[24]{0:T(128)S(1)}, f32[24]{0:T(128)}, u32[]{:S(2)}) copy-start(f32[24]{0:T(128)} %broadcast_subtract_fusion.1) | copy-start | bytes 292
  761.1 43.9 %copy-start.45 = (f32[18,24,512]{2,1,0:T(8,128)S(1)}, f32[18,24,512]{2,1,0:T(8,128)}, u32[]{:S(2)}) copy-start(f32[18,24,512]{2,1,0:T(8,128)} %get-tuple-element.353) | copy-start | bytes 2654212
  761.2 43.9 %copy-start.81 = (f32[24,512]{1,0:T(8,128)S(1)}, f32[24,512]{1,0:T(8,128)}, u32[]{:S(2)}) copy-start(f32[24,512]{1,0:T(8,128)} %copy-done.79) | copy-start | bytes 147460
  761.2 43.9 %copy-start.84 = (f32[24,512]{1,0:T(8,128)S(1)}, f32[24,512]{1,0:T(8,128)}, u32[]{:S(2)}) copy-start(f32[24,512]{1,0:T(8,128)} %copy-done.82) | copy-start | bytes 147460
  761.2 43.9 %copy-start.113 = (f32[24,512]{1,0:T(8,128)S(1)}, f32[24,512]{1,0:T(8,128)}, u32[]{:S(2)}) copy-start(f32[24,512]{1,0:T(8,128)} %get-tuple-element.245) | copy-start | bytes 147460
  761.2 43.9 %copy-start.215 = (f32[24]{0:T(128)S(1)}, f32[24]{0:T(128)}, u32[]{:S(2)}) copy-start(f32[24]{0:T(128)} %get-tuple-element.160) | copy-start | bytes 292
  761.2 45.4 %copy-start.32 = (bf16[20,25,512]{2,1,0:T(8,128)(2,1)S(1)}, bf16[20,25,512]{2,1,0:T(8,128)(2,1)}, u32[]{:S(2)}) copy-start(bf16[20,25,512]{2,1,0:T(8,128)(2,1)} %get-tuple-element.204) | copy-start | bytes 1536004
  761.2 45.4 %copy-start.221 = (bf16[18,24]{1,0:T(8,128)(2,1)S(1)}, bf16[18,24]{1,0:T(8,128)(2,1)}, u32[]{:S(2)}) copy-start(bf16[18,24]{1,0:T(8,128)(2,1)} %get-tuple-element.334) | copy-start | bytes 2596
  825.6 298.6 %all-reduce.30.cloned.1.call-start = ((), (), s32[]{:S(2)}) async-start(), calls=%async_computation.17 | async-start | bytes 14057472 | tf_op jit(solution)/shard_map/psum | solution.py:397
  837.6 3.3 collective-permute-start.12
  840.9 4.6 collective-permute-start.13
  859.6 106.3 %copy-start.23 = (bf16[18,96,512]{2,1,0:T(8,128)(2,1)}, bf16[18,96,512]{2,1,0:T(8,128)(2,1)S(1)}, u32[]{:S(2)}) copy-start(bf16[18,96,512]{2,1,0:T(8,128)(2,1)S(1)} %fusion.47) | copy-start | bytes 5308420
  863.6 102.4 %copy-start.42 = (f32[18,24,512]{2,1,0:T(8,128)S(1)}, f32[18,24,512]{2,1,0:T(8,128)}, u32[]{:S(2)}) copy-start(f32[18,24,512]{2,1,0:T(8,128)} %get-tuple-element.177) | copy-start | bytes 2654212
  (212 other events, 1505.3 us)
Sparse Core Ops, SparseCore 0:
  10.2 54.3 all-gather.8
  66.8 51.4 all-gather.10
  120.5 50.4 all-gather.12
  173.0 50.5 all-gather.16
  261.0 32.5 all-gather.14
  530.1 63.1 all-reduce.25
  596.2 31.1 reduce-scatter.14
  629.7 28.9 reduce-scatter.12
  661.2 136.2 all-reduce.27
  799.6 55.0 reduce-scatter.10
  857.0 53.3 reduce-scatter.8
  912.5 53.2 reduce-scatter.6
  971.5 152.6 all-reduce.29
where the time goes:
time: 1150 us; the launch traced here: 1140 us
  blocking collectives  410 us (36%)
  waiting for transfers between devices  286 us (25%)
  matrix products  213 us (19%)
  other arithmetic  117 us (10%)
  local copies, waits for them, and re-layouts  81 us (7%)
  between operations  19.8 us (2%)
  starting transfers between devices  16.9 us (1%)
    psum x3, blocking collectives, norm_forward(): sums, square_sums = lax.psum((sums, square_sums), ('task', 'dp'))  133 us
    psum x3, blocking collectives, norm_backward(): plain_sums, cross_sums = lax.psum((plain_sums, cross_sums), ('task', 'dp'))  122 us
    psum x1, waiting for transfers between devices, on_device(): lax.psum(pooled_pad.astype(jnp.bfloat16), 'task').astype(jnp.float32)  120 us
    dot_general x36, matrix products, conv_apply(): jnp.einsum('rwd,cd->rwc', source, kernel[1 - row_step, 1 - col_step], pre...  81.9 us
    dot_general x36, matrix products, kernel_grad(): jnp.einsum('rwc,rwd->cd', source, grad_low, preferred_element_type=jnp.fl...  58.9 us
    reduce_scatter x1, waiting for transfers between devices, on_device(): lax.psum_scatter(kernel_grads[0].astype(jnp.bfloat16), 'dp', scatter_dime...  55.5 us
    dot_general x36, matrix products, conv_apply(): jnp.einsum('rwc,cd->rwd', source, kernel[1 + row_step, 1 + col_step], pre...  54.6 us
    reduce_scatter x1, waiting for transfers between devices, on_device(): lax.psum_scatter(kernel_grads[1].astype(jnp.bfloat16), 'dp', scatter_dime...  46.8 us
  transfers between devices with their start and end apart: 27, of which 13 were waited for; matrix products, arithmetic and copies ran while one was open for 24% of the time, Pallas kernels for 0%

commit v1 on v0

v1 whole, which is shorter than its diff:
```python
import functools

import jax
import jax.numpy as jnp
from jax import lax
from jax.experimental import pallas as pl
from jax.experimental.pallas import tpu as pltpu
from jax.sharding import PartitionSpec as P

HEIGHT = 36
WIDTH = 48
BAND = 18
HALF_WIDTH = 24
CANVAS = 2
TASKS = 3
COLS = CANVAS * WIDTH
GROUPS = COLS // HALF_WIDTH
EPSILON = 1e-05
TAPS = 9
TILE_ROWS = 6
MIB = 2**20
BF = jnp.bfloat16
F32 = jnp.float32
NT = (((1,), (1,)), ((), ()))
TN = (((0,), (0,)), ((), ()))

VMEM = pl.BlockSpec(memory_space=pltpu.VMEM)
SMEM = pl.BlockSpec(memory_space=pltpu.SMEM)


def affine(row, co, scale, shift):
    step = row.shape[0] // GROUPS
    return jnp.concatenate(
        [
            row[step * j : step * (j + 1)] * co[4 * scale + j : 4 * scale + j + 1, :]
            + co[4 * shift + j : 4 * shift + j + 1, :]
            for j in range(GROUPS)
        ],
        axis=0,
    )


def scaled(row, co, scale):
    step = row.shape[0] // GROUPS
    return jnp.concatenate(
        [
            row[step * j : step * (j + 1)] * co[4 * scale + j : 4 * scale + j + 1, :]
            for j in range(GROUPS)
        ],
        axis=0,
    )


def sigmoid(v):
    return 0.5 * jnp.tanh(0.5 * v) + 0.5


def silu(v):
    return v * sigmoid(v)


def silu_slope(v):
    s = sigmoid(v)
    return s * (1.0 + v * (1.0 - s))


def norm_coefs(co, base, stats, gain, bias, cnt, info):
    means, scales = [], []
    for d in range(2):
        mean = stats[d : d + 1, :] / cnt[d]
        var = stats[2 + d : 3 + d, :] / cnt[d] - mean * mean
        means.append(mean)
        scales.append(lax.rsqrt(var + EPSILON))
    for j in range(GROUPS):
        one = info[j] == 1
        mean = jnp.where(one, means[1], means[0])
        scale = jnp.where(one, scales[1], scales[0])
        full = scale * gain[...]
        co[4 * base + j : 4 * base + j + 1, :] = full
        co[4 * base + 4 + j : 4 * base + 5 + j, :] = bias[...] - mean * full
        co[4 * base + 8 + j : 4 * base + 9 + j, :] = scale
        co[4 * base + 12 + j : 4 * base + 13 + j, :] = -mean * scale


def grad_coefs(co, base, norm, sums, cnt, info):
    for j in range(GROUPS):
        one = info[j] == 1
        count = jnp.where(one, cnt[1], cnt[0])
        plain = jnp.where(one, sums[1:2, :], sums[0:1, :]) / count
        cross = jnp.where(one, sums[3:4, :], sums[2:3, :]) / count
        full = co[4 * norm + j : 4 * norm + j + 1, :]
        scale = co[4 * norm + 8 + j : 4 * norm + 9 + j, :]
        shift = co[4 * norm + 12 + j : 4 * norm + 13 + j, :]
        co[4 * base + j : 4 * base + j + 1, :] = -full * cross * scale
        co[4 * base + 4 + j : 4 * base + 5 + j, :] = -full * (plain + cross * shift)


def grad_row(g, z, co, norm, base):
    return scaled(g, co, norm) + affine(z, co, base, base + 1)


def add_sums(acc, slot, values):
    step = HALF_WIDTH // 8
    count = values.shape[0] // COLS
    channels = values.shape[1]
    acc[slot] += jnp.sum(
        values.reshape(count, GROUPS, step, 8, channels), axis=(0, 2)
    )


def put_sums(acc, info, out, start):
    for slot in range(2):
        groups = [jnp.sum(acc[slot, j], axis=0, keepdims=True) for j in range(GROUPS)]
        for d in range(2):
            total = jnp.zeros_like(groups[0])
            for j in range(GROUPS):
                total = total + jnp.where(info[j] == d, groups[j], 0.0)
            row = start + 2 * slot + d
            out[row : row + 1, :] = total
    out[start + 4 : start + 8, :] = jnp.zeros((4, out.shape[1]), F32)


def put_edge(out, ref, info, rows):
    start = jnp.where(info[6] == 1, 0, (rows - 1) * COLS)
    out[0:COLS, :] = ref[pl.ds(pl.multiple_of(start, 8), COLS), :].astype(out.dtype)


def make_masks(mk, info):
    col = lax.broadcasted_iota(jnp.int32, mk.shape[1:], 0)
    small = (info[4] == 1, info[5] == 1)
    left = (col == 0) | (col == WIDTH)
    right = (col == WIDTH - 1) | (col == COLS - 1)
    for s in range(2):
        left = left | ((col == s * WIDTH + HALF_WIDTH) & small[s])
        right = right | ((col == s * WIDTH + HALF_WIDTH - 1) & small[s])
    mk[0] = jnp.where(left, 0.0, 1.0)
    mk[1] = jnp.where(right, 0.0, 1.0)


def put_row(taps, at, row, mk):
    parts = row.shape[1] // mk.shape[2]
    left = jnp.concatenate([mk[0]] * parts, axis=1)
    right = jnp.concatenate([mk[1]] * parts, axis=1)
    here = pl.ds(pl.multiple_of(at * COLS, COLS), COLS)
    taps[0, here, :] = (pltpu.roll(row, 1, 0) * left).astype(BF)
    taps[1, here, :] = row.astype(BF)
    taps[2, here, :] = (pltpu.roll(row, COLS - 1, 0) * right).astype(BF)


def put_halo(taps, row, mk, info, rows):
    step = COLS // GROUPS
    keep = [jnp.where(info[4 + j // 2] == 1, 0.0, 1.0) for j in range(GROUPS)]
    row = jnp.concatenate(
        [row[step * j : step * (j + 1)] * keep[j] for j in range(GROUPS)], axis=0
    )
    put_row(taps, jnp.where(info[6] == 1, 0, rows + 1), row, mk)
    put_row(taps, jnp.where(info[6] == 1, rows + 1, 0), jnp.zeros_like(row), mk)


def conv_tile(taps, w, at, rows, transpose):
    acc = None
    channels = taps.shape[2]
    for t in range(TAPS):
        di, dj = divmod(t, 3)
        a = taps[dj, pl.ds(pl.multiple_of((at + di) * COLS, COLS), rows * COLS), :]
        if transpose:
            k = w[:, (8 - t) * channels : (9 - t) * channels]
            r = jnp.dot(a, k, preferred_element_type=F32)
        else:
            k = w[:, t * channels : (t + 1) * channels]
            r = lax.dot_general(a, k, NT, preferred_element_type=F32)
        acc = r if acc is None else acc + r
    return acc


def row_at(r):
    return pl.ds(pl.multiple_of(r * COLS, COLS), COLS)


def tile_at(m, rows):
    return pl.ds(pl.multiple_of(m * rows * COLS, COLS), rows * COLS)


def loop(count, body):
    def step(i, carry):
        body(i)
        return carry

    lax.fori_loop(0, count, step, 0)


def pooled(buf, values):
    half = COLS // 2
    parts, _, lanes = buf.shape
    out = []
    for c in range(parts):
        buf[c] = values[:, c * lanes : (c + 1) * lanes]
        out.append(buf[c, pl.ds(0, half, stride=2), :] + buf[c, pl.ds(1, half, stride=2), :])
    return jnp.concatenate(out, axis=1) * 0.25


def spread(buf, values):
    half = COLS // 2
    parts, _, lanes = buf.shape
    quarter = values.astype(F32) * 0.25
    out = []
    for c in range(parts):
        part = quarter[:, c * lanes : (c + 1) * lanes]
        buf[c, pl.ds(0, half, stride=2), :] = part
        buf[c, pl.ds(1, half, stride=2), :] = part
        out.append(buf[c])
    return jnp.concatenate(out, axis=1)


def first_conv_kernel(rows, info, x, halo, w, z, pay, quarter, taps, mk, acc):
    make_masks(mk, info)
    acc[...] = jnp.zeros_like(acc)
    loop(rows, lambda r: put_row(taps, r + 1, x[row_at(r), :].astype(F32), mk))
    put_halo(taps, halo[...].astype(F32), mk, info, rows)
    conv_finish(rows, info, w, z, pay, quarter, taps, acc)


def conv_finish(rows, info, w, z, pay, quarter, taps, acc):
    def tile(m):
        out = conv_tile(taps, w, m * TILE_ROWS, TILE_ROWS, False)
        z[tile_at(m, TILE_ROWS), :] = out
        add_sums(acc, 0, out)
        add_sums(acc, 1, out * out)

    loop(rows // TILE_ROWS, tile)
    if quarter is not None:
        width = quarter.shape[2]
        quarter[...] = taps[:, :, pl.ds(pl.multiple_of(info[7] * width, width), width)]
    put_edge(pay, z, info, rows)
    put_sums(acc, info, pay, COLS)


def conv_kernel(
    rows, info, cnt, x, recv, stats, gain, bias, w, z, pay, quarter, taps, mk, acc, co
):
    make_masks(mk, info)
    acc[...] = jnp.zeros_like(acc)
    norm_coefs(co, 0, stats, gain, bias, cnt, info)
    loop(rows, lambda r: put_row(taps, r + 1, silu(affine(x[row_at(r), :], co, 0, 1)), mk))
    put_halo(taps, silu(affine(recv[0:COLS, :], co, 0, 1)), mk, info, rows)
    conv_finish(rows, info, w, z, pay, quarter, taps, acc)


def enter_kernel(
    rows, info, cnt, x, recv, stats, gain, bias, w, low, pool, u, pay, acc, co, buf
):
    acc[...] = jnp.zeros_like(acc)
    norm_coefs(co, 0, stats, gain, bias, cnt, info)

    def pair(i):
        first = silu(affine(x[row_at(2 * i), :], co, 0, 1))
        second = silu(affine(x[row_at(2 * i + 1), :], co, 0, 1))
        low[row_at(2 * i), :] = first.astype(BF)
        low[row_at(2 * i + 1), :] = second.astype(BF)
        half = COLS // 2
        pool[pl.ds(pl.multiple_of(i * half, half), half), :] = pooled(
            buf, first + second
        ).astype(BF)

    loop(rows // 2, pair)
    low[rows * COLS : (rows + 1) * COLS, :] = silu(
        affine(recv[0:COLS, :], co, 0, 1)
    ).astype(BF)

    def tile(m):
        here = tile_at(m, TILE_ROWS)
        out = lax.dot_general(low[here, :], w[...], NT, preferred_element_type=F32)
        u[here, :] = out
        add_sums(acc, 0, out)
        add_sums(acc, 1, out * out)

    loop(rows // TILE_ROWS, tile)
    put_sums(acc, info, pay, 0)


def mask_kernel(rows, info, cnt, u, stats, gain, bias, w, p, q, pay, acc, co):
    acc[...] = jnp.zeros_like(acc)
    norm_coefs(co, 0, stats, gain, bias, cnt, info)

    def each(r):
        p[row_at(r), :] = silu(affine(u[row_at(r), :], co, 0, 1)).astype(BF)

    loop(rows, each)

    def tile(m):
        here = tile_at(m, TILE_ROWS)
        out = lax.dot_general(p[here, :], w[...], NT, preferred_element_type=F32)
        q[here, :] = out
        add_sums(acc, 0, out)
        add_sums(acc, 1, out * out)

    loop(rows // TILE_ROWS, tile)
    put_edge(pay, q, info, rows)
    put_sums(acc, info, pay, COLS)


def branch_conv_kernel(
    rows, info, cnt, low, q, recv, stats, gain, bias, w, y, pay, taps, mk, acc, co
):
    make_masks(mk, info)
    acc[...] = jnp.zeros_like(acc)
    norm_coefs(co, 0, stats, gain, bias, cnt, info)

    def masked(source, gated):
        return source.astype(F32) * sigmoid(affine(gated, co, 0, 1))

    loop(rows, lambda r: put_row(taps, r + 1, masked(low[row_at(r), :], q[row_at(r), :]), mk))
    put_halo(
        taps, masked(low[rows * COLS : (rows + 1) * COLS, :], recv[0:COLS, :]), mk, info, rows
    )
    conv_finish(rows, info, w, y, pay, None, taps, acc)


def turn_kernel(
    rows, info, cnt, y, stats, gain, bias, cot, pool, g, pay, acc, co, buf
):
    acc[...] = jnp.zeros_like(acc)
    norm_coefs(co, 0, stats, gain, bias, cnt, info)
    half = COLS // 2

    def pair(i):
        part = pl.ds(pl.multiple_of(i * half, half), half)
        ct = spread(buf, cot[part, :])
        total = None
        for k in range(2):
            here = row_at(2 * i + k)
            row = y[here, :]
            v = affine(row, co, 0, 1)
            s = sigmoid(v)
            f = v * s
            total = f if total is None else total + f
            gr = ct * (s * (1.0 + v * (1.0 - s)))
            g[here, :] = gr
            add_sums(acc, 0, gr)
            add_sums(acc, 1, gr * affine(row, co, 2, 3))
        pool[part, :] = pooled(buf, total).astype(BF)

    loop(rows // 2, pair)
    put_edge(pay, g, info, rows)
    put_sums(acc, info, pay, COLS)


def branch_back_kernel(
    rows, info, cnt, g, y, recv_g, recv_y, stats, sums, gain, bias, w, low, q, qstats, qgain, qbias,
    e, gq, gs, pay, taps, mk, acc, co,
):
    make_masks(mk, info)
    acc[...] = jnp.zeros_like(acc)
    norm_coefs(co, 0, stats, gain, bias, cnt, info)
    grad_coefs(co, 4, 0, sums, cnt, info)
    norm_coefs(co, 6, qstats, qgain, qbias, cnt, info)

    def each(r):
        row = grad_row(g[row_at(r), :], y[row_at(r), :], co, 0, 4)
        e[row_at(r), :] = row.astype(BF)
        put_row(taps, r + 1, row, mk)

    loop(rows, each)
    put_halo(taps, grad_row(recv_g[0:COLS, :], recv_y[0:COLS, :], co, 0, 4), mk, info, rows)

    def tile(m):
        gq[tile_at(m, TILE_ROWS), :] = conv_tile(taps, w, m * TILE_ROWS, TILE_ROWS, True)

    loop(rows // TILE_ROWS, tile)

    def post(r):
        here = row_at(r)
        grad = gq[here, :]
        row = q[here, :]
        gate = sigmoid(affine(row, co, 6, 7))
        gs[here, :] = grad * gate
        out = grad * low[here, :].astype(F32) * gate * (1.0 - gate)
        gq[here, :] = out
        add_sums(acc, 0, out)
        add_sums(acc, 1, out * affine(row, co, 8, 9))

    loop(rows, post)
    put_sums(acc, info, pay, 0)


def mask_back_kernel(
    rows, info, cnt, g, q, stats, sums, gain, bias, w, u, ustats, ugain, ubias, e, gu, pay, acc, co
):
    acc[...] = jnp.zeros_like(acc)
    norm_coefs(co, 0, stats, gain, bias, cnt, info)
    grad_coefs(co, 4, 0, sums, cnt, info)
    norm_coefs(co, 6, ustats, ugain, ubias, cnt, info)

    def each(r):
        e[row_at(r), :] = grad_row(g[row_at(r), :], q[row_at(r), :], co, 0, 4).astype(BF)

    loop(rows, each)

    def tile(m):
        here = tile_at(m, TILE_ROWS)
        gu[here, :] = jnp.dot(e[here, :], w[...], preferred_element_type=F32)

    loop(rows // TILE_ROWS, tile)

    def post(r):
        here = row_at(r)
        row = u[here, :]
        out = gu[here, :] * silu_slope(affine(row, co, 6, 7))
        gu[here, :] = out
        add_sums(acc, 0, out)
        add_sums(acc, 1, out * affine(row, co, 8, 9))

    loop(rows, post)
    put_sums(acc, info, pay, 0)


def leave_kernel(
    rows, info, cnt, g, u, stats, sums, gain, bias, w, gs, z, zstats, zgain, zbias, cot,
    e, out, pay, acc, co, buf, wide,
):
    acc[...] = jnp.zeros_like(acc)
    norm_coefs(co, 0, stats, gain, bias, cnt, info)
    grad_coefs(co, 4, 0, sums, cnt, info)
    norm_coefs(co, 6, zstats, zgain, zbias, cnt, info)

    def each(r):
        e[row_at(r), :] = grad_row(g[row_at(r), :], u[row_at(r), :], co, 0, 4).astype(BF)

    loop(rows, each)

    def tile(m):
        here = tile_at(m, TILE_ROWS)
        wide[here, :] = gs[here, :] + jnp.dot(e[here, :], w[...], preferred_element_type=F32)

    loop(rows // TILE_ROWS, tile)
    half = COLS // 2
    active = info[8] == 1

    def post(i):
        ct = spread(buf, cot[pl.ds(pl.multiple_of(i * half, half), half), :])
        for k in range(2):
            here = row_at(2 * i + k)
            grad = jnp.where(active, wide[here, :], ct)
            out[here, :] = grad.astype(BF)
            row = z[here, :]
            grad = grad * silu_slope(affine(row, co, 6, 7))
            add_sums(acc, 0, grad)
            add_sums(acc, 1, grad * affine(row, co, 8, 9))

    loop(rows // 2, post)
    put_sums(acc, info, pay, 0)


def trunk_back_kernel(
    rows, top, last, info, cnt, g, z, recv_g, recv_z, stats, sums, gain, bias, w, *rest
):
    if last:
        e, out, taps, mk, co = rest
    else:
        x, xstats, xgain, xbias, e, out, pay, taps, mk, co, acc = rest
        acc[...] = jnp.zeros_like(acc)
        norm_coefs(co, 6, xstats, xgain, xbias, cnt, info)
    make_masks(mk, info)
    norm_coefs(co, 0, stats, gain, bias, cnt, info)
    grad_coefs(co, 4, 0, sums, cnt, info)

    def grad(g_row, z_row):
        if top:
            g_row = g_row.astype(F32) * silu_slope(affine(z_row, co, 0, 1))
        return grad_row(g_row, z_row, co, 0, 4)

    def each(r):
        row = grad(g[row_at(r), :], z[row_at(r), :])
        e[row_at(r), :] = row.astype(BF)
        put_row(taps, r + 1, row, mk)

    loop(rows, each)
    put_halo(taps, grad(recv_g[0:COLS, :], recv_z[0:COLS, :]), mk, info, rows)

    def tile(m):
        out[tile_at(m, TILE_ROWS), :] = conv_tile(taps, w, m * TILE_ROWS, TILE_ROWS, True)

    loop(rows // TILE_ROWS, tile)
    if last:
        return

    def post(r):
        here = row_at(r)
        row = x[here, :]
        value = out[here, :] * silu_slope(affine(row, co, 6, 7))
        out[here, :] = value
        add_sums(acc, 0, value)
        add_sums(acc, 1, value * affine(row, co, 8, 9))

    loop(rows, post)
    put_edge(pay, out, info, rows)
    put_sums(acc, info, pay, COLS)


def trunk_wgrad_kernel(rows, quarter, e, out):
    width = rows * COLS
    wide = jnp.concatenate(
        [quarter[t % 3, (t // 3) * COLS : (t // 3) * COLS + width, :] for t in range(TAPS)], axis=1
    )
    out[...] = lax.dot_general(e[...], wide, TN, preferred_element_type=F32).astype(BF)


def branch_wgrad_kernel(rows, taps, ey, p, eq, low, eu, out):
    width = rows * COLS
    channels = ey.shape[1]
    for t in range(TAPS):
        di, dj = divmod(t, 3)
        a = taps[dj, di * COLS : di * COLS + width, :]
        out[:, t * channels : (t + 1) * channels] = lax.dot_general(
            ey[...], a, TN, preferred_element_type=F32
        ).astype(BF)
    out[:, 9 * channels : 10 * channels] = lax.dot_general(
        eu[...], low[0:width, :], TN, preferred_element_type=F32
    ).astype(BF)
    out[:, 10 * channels : 11 * channels] = lax.dot_general(
        eq[...], p[...], TN, preferred_element_type=F32
    ).astype(BF)


def run(kernel, ins, outs, scratch, limit, flops=0):
    specs = [SMEM if a.ndim == 1 else VMEM for a in ins]
    size = sum(a.size * a.dtype.itemsize for a in ins) + sum(
        o.size * o.dtype.itemsize for o in outs
    )
    return pl.pallas_call(
        kernel,
        out_shape=outs,
        in_specs=specs,
        out_specs=[VMEM] * len(outs),
        scratch_shapes=scratch,
        compiler_params=pltpu.CompilerParams(vmem_limit_bytes=limit * MIB),
        cost_estimate=pl.CostEstimate(flops=flops, bytes_accessed=size, transcendentals=0),
    )(*ins)


def swap(value, axis, mask):
    pairs = [(i, i ^ mask) for i in range(lax.axis_size(axis))]
    return lax.ppermute(value, axis, pairs)


def sum_over(value, axis, start=1):
    mask = start
    while mask < lax.axis_size(axis):
        value = value + swap(value, axis, mask)
        mask *= 2
    return value


def exchange(pay):
    recv = swap(pay, "dp", 1)
    return recv, sum_over(pay[COLS:] + recv[COLS:], "dp", 2)


def domain_counts(size_class, domain_tags):
    big_area = HEIGHT * WIDTH
    small_area = BAND * HALF_WIDTH
    ones_count = jnp.sum(
        jnp.where(
            size_class == 0, big_area * domain_tags[:, 0], small_area * jnp.sum(domain_tags, axis=1)
        )
    )
    all_count = size_class.shape[0] * big_area
    return jnp.maximum(jnp.stack([all_count - ones_count, ones_count]).astype(F32), 1.0)


def on_device(
    images,
    conv_first,
    conv_second,
    conv_third,
    trunk_gains,
    trunk_biases,
    attend_in,
    attend_mask,
    attend_out,
    branch_gains,
    branch_biases,
    size_class,
    domain_tags,
    trunk_cotangent,
    task_cotangent,
):
    rows, cols, ch = images.shape
    pixels = rows * cols
    position = lax.axis_index("dp")
    task_index = lax.axis_index("task")
    task_count = lax.axis_size("task")
    quarter = ch // task_count
    pair_index = position // 2
    bottom = position % 2
    local_class = lax.dynamic_slice_in_dim(size_class, pair_index * CANVAS, CANVAS, 0)
    local_tags = lax.dynamic_slice_in_dim(domain_tags, pair_index * CANVAS, CANVAS, 0)
    side = jnp.arange(GROUPS) % 2
    slot_class = jnp.repeat(local_class, 2)
    slot_tags = jnp.repeat(local_tags, 2, axis=0)
    which = jnp.where(slot_class == 1, bottom * 2 + side, 0)
    groups = jnp.sum(slot_tags * (jnp.arange(4)[None, :] == which[:, None]), axis=1)
    active = (task_index < TASKS).astype(jnp.int32)
    info = jnp.concatenate(
        [groups, local_class, jnp.stack([bottom, task_index, active])]
    ).astype(jnp.int32)
    cnt = domain_counts(size_class, domain_tags)

    def own(kernel):
        return jnp.transpose(kernel.reshape(-1, kernel.shape[-1])).astype(BF)

    branch = jnp.minimum(task_index, TASKS - 1)

    def pick(values):
        return lax.dynamic_index_in_dim(values, branch, 0, keepdims=False)

    gather = functools.partial(lax.all_gather, axis_name="dp", axis=0, tiled=True)
    weights = [gather(own(k)) for k in (conv_first, conv_second, conv_third)]
    w_in = gather(own(pick(attend_in)))
    w_mask = gather(own(pick(attend_mask)))
    w_out = gather(own(pick(attend_out)))
    gains = [trunk_gains[i : i + 1] for i in range(3)]
    biases = [trunk_biases[i : i + 1] for i in range(3)]
    own_gains = pick(branch_gains)
    own_biases = pick(branch_biases)
    b_gains = [own_gains[i : i + 1] for i in range(3)]
    b_biases = [own_biases[i : i + 1] for i in range(3)]

    def shape(dims, dtype=F32):
        return jax.ShapeDtypeStruct(dims, dtype)

    wide = shape((pixels, ch))
    low_wide = shape((pixels, ch), BF)
    pay_shape = shape((COLS + 8, ch))
    sums_shape = shape((8, ch))
    taps_dims = (3, pixels + 2 * COLS, ch)
    taps = pltpu.VMEM(taps_dims, BF)
    masks = pltpu.VMEM((2, COLS, 128), F32)
    acc = pltpu.VMEM((2, GROUPS, 8, ch), F32)
    buf = pltpu.VMEM((ch // 128, COLS, 128), F32)

    def coefs(blocks):
        return pltpu.VMEM((4 * blocks, ch), F32)

    conv_flops = 2 * TAPS * pixels * ch * ch
    dot_flops = 2 * pixels * ch * ch

    flat = images.reshape(pixels, ch)
    edge = jnp.where(bottom == 1, flat[:COLS], flat[pixels - COLS :])
    halo = swap(edge, "dp", 1)
    quarter_shape = shape((3, pixels + 2 * COLS, quarter), BF)
    z, recv, stats, quarters = [], [], [], []
    for layer in range(3):
        outs = [wide, pay_shape, quarter_shape]
        if layer == 0:
            values, pay, part = run(
                functools.partial(first_conv_kernel, rows),
                [info, flat, halo, weights[0]],
                outs, [taps, masks, acc], 30, conv_flops,
            )
        else:
            values, pay, part = run(
                functools.partial(conv_kernel, rows),
                [info, cnt, z[-1], recv[-1], stats[-1], gains[layer - 1], biases[layer - 1], weights[layer]],
                outs, [taps, masks, acc, coefs(4)], 30, conv_flops,
            )
        got, total = exchange(pay)
        z.append(values)
        recv.append(got)
        stats.append(total)
        quarters.append(part)

    low, trunk_pool, u, pay = run(
        functools.partial(enter_kernel, rows),
        [info, cnt, z[2], recv[2], stats[2], gains[2], biases[2], w_in],
        [shape((pixels + COLS, ch), BF), shape((pixels // 4, ch), BF), wide, sums_shape],
        [acc, coefs(4), buf], 24, dot_flops,
    )
    u_stats = sum_over(pay, "dp")
    p, q, pay = run(
        functools.partial(mask_kernel, rows),
        [info, cnt, u, u_stats, b_gains[0], b_biases[0], w_mask],
        [low_wide, wide, pay_shape], [acc, coefs(4)], 24, dot_flops,
    )
    q_recv, q_stats = exchange(pay)
    y, pay, masked_taps = run(
        functools.partial(branch_conv_kernel, rows),
        [info, cnt, low, q, q_recv, q_stats, b_gains[1], b_biases[1], w_out],
        [wide, pay_shape, shape(taps_dims, BF)], [masks, acc, coefs(4)], 34, conv_flops,
    )
    y_recv, y_stats = exchange(pay)

    cot = pick(task_cotangent).reshape(pixels // 4, ch)
    branch_pool, g_y, pay = run(
        functools.partial(turn_kernel, rows),
        [info, cnt, y, y_stats, b_gains[2], b_biases[2], cot],
        [shape((pixels // 4, ch), BF), wide, pay_shape], [acc, coefs(4), buf], 24,
    )
    gy_recv, y_sums = exchange(pay)
    e_y, g_q, gs, pay = run(
        functools.partial(branch_back_kernel, rows),
        [info, cnt, g_y, y, gy_recv, y_recv, y_stats, y_sums, b_gains[2], b_biases[2], w_out, low, q, q_stats,
         b_gains[1], b_biases[1]],
        [low_wide, wide, wide, sums_shape], [taps, masks, acc, coefs(10)], 44, conv_flops,
    )
    q_sums = sum_over(pay, "dp")
    e_q, g_u, pay = run(
        functools.partial(mask_back_kernel, rows),
        [info, cnt, g_q, q, q_stats, q_sums, b_gains[1], b_biases[1], w_mask, u, u_stats, b_gains[0], b_biases[0]],
        [low_wide, wide, sums_shape], [acc, coefs(10)], 28, dot_flops,
    )
    u_sums = sum_over(pay, "dp")
    trunk_cot = trunk_cotangent.reshape(pixels // 4, ch)
    e_u, grad_shared, pay = run(
        functools.partial(leave_kernel, rows),
        [info, cnt, g_u, u, u_stats, u_sums, b_gains[0], b_biases[0], w_in, gs, z[2], stats[2], gains[2],
         biases[2], trunk_cot],
        [low_wide, low_wide, sums_shape], [acc, coefs(10), buf, pltpu.VMEM((pixels, ch), F32)], 34, dot_flops,
    )
    sums = sum_over(sum_over(pay, "dp"), "task")
    grad_shared = lax.psum(grad_shared, "task")
    (branch_kernel_grad,) = run(
        functools.partial(branch_wgrad_kernel, rows),
        [masked_taps, e_y, p, e_q, low, e_u],
        [shape((ch, 11 * ch), BF)], [], 40, conv_flops,
    )

    edge = jnp.where(bottom == 1, grad_shared[:COLS], grad_shared[pixels - COLS :])
    g, g_recv = grad_shared, swap(edge, "dp", 1)
    kernel_parts = [None, None, None]
    trunk_sums = [None, None, None]
    for layer in (2, 1, 0):
        trunk_sums[layer] = sums
        last = layer == 0
        ins = [info, cnt, g, z[layer], g_recv, recv[layer], stats[layer], sums, gains[layer], biases[layer],
               weights[layer]]
        outs = [low_wide, wide]
        scratch = [taps, masks, coefs(10)]
        if not last:
            ins += [z[layer - 1], stats[layer - 1], gains[layer - 1], biases[layer - 1]]
            outs += [pay_shape]
            scratch += [acc]
        got = run(
            functools.partial(trunk_back_kernel, rows, layer == 2, last),
            ins, outs, scratch, 38, conv_flops,
        )
        e, g = got[0], got[1]
        (kernel_parts[layer],) = run(
            functools.partial(trunk_wgrad_kernel, rows),
            [quarters[layer], e], [shape((ch, TAPS * quarter), BF)], [], 24, conv_flops // 4,
        )
        if not last:
            g_recv, sums = exchange(got[2])

    def scatter(values):
        return lax.psum_scatter(values, "dp", scatter_dimension=0, tiled=True)

    def collect(values):
        return lax.all_gather(values, "task", axis=0, tiled=False)

    task_features = collect(branch_pool)[:TASKS].reshape(TASKS, rows // 2, cols // 2, ch)
    trunk_kernel_grads = []
    for part in kernel_parts:
        whole = collect(scatter(part))
        outc = whole.shape[1]
        whole = whole.reshape(task_count, outc, TAPS, quarter).transpose(2, 0, 3, 1)
        trunk_kernel_grads.append(whole.astype(F32).reshape(3, 3, ch, outc))
    whole = collect(scatter(branch_kernel_grad))[:TASKS]
    outc = whole.shape[1]
    whole = whole.reshape(TASKS, outc, 11, ch).transpose(0, 2, 3, 1).astype(F32)
    out_grad = whole[:, :TAPS].reshape(TASKS, 3, 3, ch, outc)
    in_grad = whole[:, TAPS]
    mask_grad = whole[:, TAPS + 1]
    branch_sums = collect(jnp.stack([u_sums[:4], q_sums[:4], y_sums[:4]]))[:TASKS]
    trunk_sums = jnp.stack([s[:4] for s in trunk_sums])
    return (
        trunk_pool.reshape(rows // 2, cols // 2, ch),
        task_features,
        g.reshape(rows, cols, ch),
        trunk_kernel_grads[0],
        trunk_kernel_grads[1],
        trunk_kernel_grads[2],
        trunk_sums[:, 2] + trunk_sums[:, 3],
        trunk_sums[:, 0] + trunk_sums[:, 1],
        in_grad,
        mask_grad,
        out_grad,
        branch_sums[:, :, 2] + branch_sums[:, :, 3],
        branch_sums[:, :, 0] + branch_sums[:, :, 1],
    )


def solution(mesh):
    in_specs = (
        P("dp", None, None),
        P(None, None, None, "dp"),
        P(None, None, None, "dp"),
        P(None, None, None, "dp"),
        P(),
        P(),
        P(None, None, "dp"),
        P(None, None, "dp"),
        P(None, None, None, None, "dp"),
        P(),
        P(),
        P(),
        P(),
        P("dp", None, None),
        P(None, "dp", None, None),
    )
    out_specs = (
        P("dp", None, None),
        P(None, "dp", None, None),
        P("dp", None, None),
        P(None, None, None, "dp"),
        P(None, None, None, "dp"),
        P(None, None, None, "dp"),
        P(),
        P(),
        P(None, None, "dp"),
        P(None, None, "dp"),
        P(None, None, None, None, "dp"),
        P(),
        P(),
    )
    return jax.shard_map(
        on_device, mesh=mesh, in_specs=in_specs, out_specs=out_specs, check_vma=False
    )
```

time: 1150 us -> 718 us (0.62)
  blocking collectives: 410 us -> 74.9 us
  matrix products: 213 us -> 0 us
  Pallas kernels: 0 us -> 156 us
  other arithmetic: 117 us -> 18.6 us
  local copies, waits for them, and re-layouts: 81 us -> 141 us
    psum x13 -> x0, blocking collectives: 362 us -> none  [the longest x3 133 us: norm_forward(): sums, square_sums = lax.psum((sums, square_sums), ('task', 'dp'))]
    dot_general x114 -> x0, matrix products: 213 us -> none  [the longest x36 81.9 us: conv_apply(): jnp.einsum('rwd,cd->rwc', source, kernel[1 - row_step, 1 - col_step], pre...]
    pallas_call x0 -> x17, Pallas kernels: none -> 156 us  [run(): pl.pallas_call(kernel, out_shape=outs, in_specs=specs, out_specs=[VMEM] *...]
    ppermute x14 -> x40, waiting for transfers between devices: 11.5 us -> 96.8 us  [swap(): return lax.ppermute(value, axis, pairs)]
    unnamed x503 -> x272, local copies, waits for them, and re-layouts: 11.8 us -> 94.4 us
    psum x1, waiting for transfers between devices: 120 us -> 39.5 us  [on_device(): grad_shared = lax.psum(grad_shared, 'task')]
    all_gather x5 -> x6, waiting for transfers between devices: 26.7 us -> 103 us  [the longest x3 75.7 us: on_device(): weights = [gather(own(k)) for k in (conv_first, conv_second, conv_third)]]
    reduce_scatter x5 -> x4, waiting for transfers between devices: 102 us -> 40.5 us  [scatter(): return lax.psum_scatter(values, 'dp', scatter_dimension=0, tiled=True)]
  transfers between devices with their start and end apart: 27 -> 51, of which waited for: 13 -> 42; matrix products, arithmetic and copies ran while one was open for 24% -> 6% of each run, Pallas kernels for 0% -> 16%
where the time goes in v1:
time: 718 us; the launch traced here: 712 us
  waiting for transfers between devices  281 us (39%)
  Pallas kernels  156 us (22%)
  local copies, waits for them, and re-layouts  141 us (20%)
  blocking collectives  74.9 us (10%)
  starting transfers between devices  24.8 us (3%)
  other arithmetic  18.6 us (3%)
  between operations  16 us (2%)
    pallas_call x17, Pallas kernels, run(): pl.pallas_call(kernel, out_shape=outs, in_specs=specs, out_specs=[VMEM] *...  156 us
    ppermute x40, waiting for transfers between devices, swap(): return lax.ppermute(value, axis, pairs)  96.8 us
    unnamed x272, local copies, waits for them, and re-layouts  94.4 us
    all_gather x3, waiting for transfers between devices, on_device(): weights = [gather(own(k)) for k in (conv_first, conv_second, conv_third)]  75.7 us
    all_gather x4, blocking collectives, collect(): return lax.all_gather(values, 'task', axis=0, tiled=False)  41 us
    reduce_scatter x4, waiting for transfers between devices, scatter(): return lax.psum_scatter(values, 'dp', scatter_dimension=0, tiled=True)  40.5 us
    psum x1, waiting for transfers between devices, on_device(): grad_shared = lax.psum(grad_shared, 'task')  39.5 us
    all_gather x2, waiting for transfers between devices, collect(): return lax.all_gather(values, 'task', axis=0, tiled=False)  27.3 us
  transfers between devices with their start and end apart: 51, of which 42 were waited for; matrix products, arithmetic and copies ran while one was open for 6% of the time, Pallas kernels for 16%

profile of v1, /device:TPU:0, one launch (start us, length us, event | category | flops | bytes accessed | tf_op | source)
XLA Modules:
  0.0 712.2 jit_solution(9413136158680607314)
XLA Ops:
  10.1 2.5 convert_element_type.91
  15.5 2.5 convert_element_type.94
  20.8 2.5 convert_element_type.97
  29.3 37.9 %all-gather.13.cloned.1.call-done.w = bf16[512,4608]{1,0:T(8,128)(2,1)} async-done(((bf16[64,4608]{1,0:T(8,128)(2,1)}), bf16[512,4608]{1,0:T(8,128)(2,1)}) %all-gather.13.cloned.1.call-update) | async-done | bytes 4718608 | tf_op jit(solution)/shard_map/all_gather | solution.py:618
  68.7 2.3 copy-done.89
  72.0 10.8 %shard_map.246 = (f32[1728,512]{1,0:T(8,128)S(1)}, f32[104,512]{1,0:T(8,128)S(1)}, bf16[3,1920,128]{2,1,0:T(8,128)(2,1)S(1)}) custom-call(s32[9]{0:T(128)S(1)} %concatenate.3.info, bf16[1728,512]{1,0:T(8,128)(2,1)S(1)} %bitcast.90, bf16[96,512]{1,0:T(8,128)(2,1)S(1)} %copy-done.106, bf16[512,4608]{1,0:T(8,128)(2,1)S(1)} %copy-done.89), custom_call_target="tpu_custom_call" | custom-call | flops 8153726976 | bytes 11812900 | tf_op jit(solution)/shard_map/pallas_call | solution.py:530
  89.2 4.4 collective-permute-done.2
  94.3 5.2 collective-permute-done.3
  100.1 20.5 %all-gather.15.cloned.1.call-done.w = bf16[512,4608]{1,0:T(8,128)(2,1)} async-done(((bf16[64,4608]{1,0:T(8,128)(2,1)}), bf16[512,4608]{1,0:T(8,128)(2,1)}) %all-gather.15.cloned.1.call-update) | async-done | bytes 4718608 | tf_op jit(solution)/shard_map/all_gather | solution.py:618
  128.0 11.6 %shard_map.247 = (f32[1728,512]{1,0:T(8,128)S(1)}, f32[104,512]{1,0:T(8,128)S(1)}, bf16[3,1920,128]{2,1,0:T(8,128)(2,1)S(1)}) custom-call(s32[9]{0:T(128)S(1)} %concatenate.3.info, f32[2]{0:T(128)S(1)} %fusion.14.cnt, f32[1728,512]{1,0:T(8,128)S(1)} %copy-done.117, f32[104,512]{1,0:T(8,128)S(1)} %copy-done.80, f32[8,512]{1,0:T(8,128)S(1)} %copy-done.51, ...), custom_call_target="tpu_custom_call" | custom-call | flops 8153726976 | bytes 13717548 | tf_op jit(solution)/shard_map/pallas_call | solution.py:530
  144.7 5.8 collective-permute-done.5
  150.6 5.6 collective-permute-done.6
  156.7 17.3 %all-gather.17.cloned.1.call-done.w = bf16[512,4608]{1,0:T(8,128)(2,1)} async-done(((bf16[64,4608]{1,0:T(8,128)(2,1)}), bf16[512,4608]{1,0:T(8,128)(2,1)}) %all-gather.17.cloned.1.call-update) | async-done | bytes 4718608 | tf_op jit(solution)/shard_map/all_gather | solution.py:618
  181.4 11.6 %shard_map.248 = (f32[1728,512]{1,0:T(8,128)S(1)}, f32[104,512]{1,0:T(8,128)S(1)}, bf16[3,1920,128]{2,1,0:T(8,128)(2,1)S(1)}) custom-call(s32[9]{0:T(128)S(1)} %concatenate.3.info, f32[2]{0:T(128)S(1)} %fusion.14.cnt, f32[1728,512]{1,0:T(8,128)S(1)} %copy-done.121, f32[104,512]{1,0:T(8,128)S(1)} %copy-done.83, f32[8,512]{1,0:T(8,128)S(1)} %copy-done.53, ...), custom_call_target="tpu_custom_call" | custom-call | flops 8153726976 | bytes 13717548 | tf_op jit(solution)/shard_map/pallas_call | solution.py:530
  196.6 4.6 collective-permute-done.8
  201.2 17.6 %all_gather.57.w = bf16[512,512]{1,0:T(8,128)(2,1)S(1)} all-gather(bf16[64,512]{1,0:T(8,128)(2,1)S(1)} %fusion), channel_id=1, replica_groups=mesh['task'=4,'dp'=8] {'dp'}, dimensions={0}, use_global_device_ids=true | all-gather | bytes 589824 | tf_op jit(solution)/shard_map/all_gather | solution.py:619
  218.9 3.7 shard_map.249
  225.3 16.3 %all_gather.58.w = bf16[512,512]{1,0:T(8,128)(2,1)} all-gather(bf16[64,512]{1,0:T(8,128)(2,1)S(1)} %fusion.1), channel_id=1, replica_groups=mesh['task'=4,'dp'=8] {'dp'}, dimensions={0}, use_global_device_ids=true | all-gather | bytes 589824 | tf_op jit(solution)/shard_map/all_gather | solution.py:620
  244.4 2.7 collective-permute-done.12
  249.3 3.2 shard_map.250
  258.1 3.4 collective-permute-done.14
  262.3 3.8 collective-permute-done.15
  276.9 11.5 %shard_map.251 = (f32[1728,512]{1,0:T(8,128)S(1)}, f32[104,512]{1,0:T(8,128)S(1)}, bf16[3,1920,512]{2,1,0:T(8,128)(2,1)S(1)}) custom-call(s32[9]{0:T(128)S(1)} %copy-done.41, f32[2]{0:T(128)S(1)} %copy-done.59, bf16[1824,512]{1,0:T(8,128)(2,1)S(1)} %copy-done.96, f32[1728,512]{1,0:T(8,128)S(1)} %copy-done.11, f32[104,512]{1,0:T(8,128)S(1)} %copy-done.86, ...), custom_call_target="tpu_custom_call" | custom-call | flops 8153726976 | bytes 20009004 | tf_op jit(solution)/shard_map/pallas_call | solution.py:530
  288.4 2.6 copy-done.113
  292.8 3.4 collective-permute-done.17
  298.1 2.7 collective-permute-done.18
  300.9 3.5 shard_map.252
  308.8 3.4 collective-permute-done.20
  313.0 3.8 collective-permute-done.21
  316.9 19.7 %shard_map.253 = (bf16[1728,512]{1,0:T(8,128)(2,1)S(1)}, f32[1728,512]{1,0:T(8,128)S(1)}, f32[1728,512]{1,0:T(8,128)}, f32[8,512]{1,0:T(8,128)S(1)}) custom-call(s32[9]{0:T(128)S(1)} %copy-done.42, f32[2]{0:T(128)S(1)} %copy-done.60, f32[1728,512]{1,0:T(8,128)} %copy-done.94, f32[1728,512]{1,0:T(8,128)} %copy-done.13, ...), custom_call_target="tpu_custom_call" | custom-call | flops 8153726976 | bytes 26550316 | tf_op jit(solution)/shard_map/pallas_call | solution.py:530
  338.2 3.4 collective-permute-done.23
  342.4 3.8 collective-permute-done.24
  348.3 4.7 shard_map.254
  355.8 3.4 collective-permute-done.26
  359.9 3.8 collective-permute-done.27
  363.8 5.4 shard_map.255
  380.3 15.8 %shard_map.262 = bf16[512,5632]{1,0:T(8,128)(2,1)} custom-call(bf16[3,1920,512]{2,1,0:T(8,128)(2,1)} %copy-done.113, bf16[1728,512]{1,0:T(8,128)(2,1)S(1)} %copy-done.115, bf16[1728,512]{1,0:T(8,128)(2,1)S(1)} %copy-done.100, bf16[1728,512]{1,0:T(8,128)(2,1)S(1)} %copy-done.102, bf16[1824,512]{1,0:T(8,128)(2,1)S(1)} %copy-done.98, ...), custom_call_target="tpu_custom_call" | custom-call | flops 8153726976 | bytes 20611072 | tf_op jit(solution)/shard_map/pallas_call | solution.py:530
  396.9 39.5 %all-reduce.2.cloned.1.call-done.g = bf16[1728,512]{1,0:T(8,128)(2,1)} async-done(((bf16[1728,512]{1,0:T(8,128)(2,1)}), bf16[1728,512]{1,0:T(8,128)(2,1)}) %all-reduce.2.cloned.1.call-update) | async-done | bytes 1769488 | tf_op jit(solution)/shard_map/psum | solution.py:721
  443.4 2.4 collective-permute-start.31
  445.8 2.4 collective-permute-done.31
  453.3 2.4 collective-permute-done.33
  464.9 16.3 %shard_map.256 = (bf16[1728,512]{1,0:T(8,128)(2,1)S(1)}, f32[1728,512]{1,0:T(8,128)S(1)}, f32[104,512]{1,0:T(8,128)S(1)}) custom-call(s32[9]{0:T(128)S(1)} %copy-done.43, f32[2]{0:T(128)S(1)} %copy-done.61, bf16[1728,512]{1,0:T(8,128)(2,1)S(1)} %copy-done.38, f32[1728,512]{1,0:T(8,128)S(1)} %copy-done.4, bf16[96,512]{1,0:T(8,128)(2,1)S(1)} %collective-permute-done.28.recv_g, ...), custom_call_target="tpu_custom_call" | custom-call | flops 8153726976 | bytes 19456044 | tf_op jit(solution)/shard_map/pallas_call | solution.py:530
  483.8 3.6 shard_map.261
  491.6 2.7 collective-permute-done.35
  494.4 2.6 collective-permute-start.36
  497.0 2.9 collective-permute-done.36
  506.0 14.8 %shard_map.257 = (bf16[1728,512]{1,0:T(8,128)(2,1)S(1)}, f32[1728,512]{1,0:T(8,128)S(1)}, f32[104,512]{1,0:T(8,128)S(1)}) custom-call(s32[9]{0:T(128)S(1)} %copy-done.44, f32[2]{0:T(128)S(1)} %copy-done.62, f32[1728,512]{1,0:T(8,128)S(1)} %copy-done.127, f32[1728,512]{1,0:T(8,128)S(1)} %copy-done.123, f32[104,512]{1,0:T(8,128)S(1)} %collective-permute-done.34.recv_g, ...), custom_call_target="tpu_custom_call" | custom-call | flops 8153726976 | bytes 21340204 | tf_op jit(solution)/shard_map/pallas_call | solution.py:530
  523.3 3.6 shard_map.260
  530.6 2.5 collective-permute-done.38
  533.1 2.5 collective-permute-start.39
  544.1 12.6 %shard_map.258 = (bf16[1728,512]{1,0:T(8,128)(2,1)S(1)}, f32[1728,512]{1,0:T(8,128)}) custom-call(s32[9]{0:T(128)S(1)} %copy-done.44, f32[2]{0:T(128)S(1)} %copy-done.62, f32[1728,512]{1,0:T(8,128)S(1)} %copy-done.125, f32[1728,512]{1,0:T(8,128)S(1)} %copy-done.119, f32[104,512]{1,0:T(8,128)S(1)} %collective-permute-done.37.recv_g, ...), custom_call_target="tpu_custom_call" | custom-call | flops 8153726976 | bytes 17567788 | tf_op jit(solution)/shard_map/pallas_call | solution.py:530
  556.8 3.6 shard_map.259
  561.3 8.4 %all-gather.5 = f32[12,4,512]{2,1,0:T(4,128)S(1)} all-gather(f32[3,4,512]{2,1,0:T(4,128)S(1)} %pad_maximum_fusion.1), channel_id=7, replica_groups=mesh['task'=4,'dp'=8] {'task'}, dimensions={0}, use_global_device_ids=true | all-gather | bytes 122880 | tf_op jit(solution)/shard_map/all_gather | solution.py:759
  570.9 2.5 slice.246
  574.7 10.1 %all-gather.3 = bf16[256,1152]{1,0:T(8,128)(2,1)S(1)} all-gather(bf16[64,1152]{1,0:T(8,128)(2,1)} %reduce-scatter.9.cloned.1.call-done), channel_id=5, replica_groups=mesh['task'=4,'dp'=8] {'task'}, dimensions={0}, use_global_device_ids=true | all-gather | bytes 737280 | tf_op jit(solution)/shard_map/all_gather | solution.py:759
  587.4 19.8 %reduce-scatter.7.cloned.1.call-done = bf16[64,1152]{1,0:T(8,128)(2,1)} async-done(((bf16[512,1152]{1,0:T(8,128)(2,1)}), bf16[64,1152]{1,0:T(8,128)(2,1)}) %reduce-scatter.7.cloned.1.call-update) | async-done | bytes 147472 | tf_op jit(solution)/shard_map/reduce_scatter | solution.py:756
  607.1 10.6 %all-gather.2 = bf16[256,1152]{1,0:T(8,128)(2,1)S(1)} all-gather(bf16[64,1152]{1,0:T(8,128)(2,1)} %reduce-scatter.7.cloned.1.call-done), channel_id=4, replica_groups=mesh['task'=4,'dp'=8] {'task'}, dimensions={0}, use_global_device_ids=true | all-gather | bytes 737280 | tf_op jit(solution)/shard_map/all_gather | solution.py:759
  620.3 20.7 %reduce-scatter.5.cloned.1.call-done = bf16[64,1152]{1,0:T(8,128)(2,1)} async-done(((bf16[512,1152]{1,0:T(8,128)(2,1)}), bf16[64,1152]{1,0:T(8,128)(2,1)}) %reduce-scatter.5.cloned.1.call-update) | async-done | bytes 147472 | tf_op jit(solution)/shard_map/reduce_scatter | solution.py:756
  641.0 11.9 %all-gather.1 = bf16[256,1152]{1,0:T(8,128)(2,1)S(1)} all-gather(bf16[64,1152]{1,0:T(8,128)(2,1)} %reduce-scatter.5.cloned.1.call-done), channel_id=3, replica_groups=mesh['task'=4,'dp'=8] {'task'}, dimensions={0}, use_global_device_ids=true | all-gather | bytes 737280 | tf_op jit(solution)/shard_map/all_gather | solution.py:759
  655.5 27.3 %all-gather.23.cloned.1.call-done = bf16[256,5632]{1,0:T(8,128)(2,1)} async-done(((bf16[64,5632]{1,0:T(8,128)(2,1)}), bf16[256,5632]{1,0:T(8,128)(2,1)}) %all-gather.23.cloned.1.call-update) | async-done | bytes 2883600 | tf_op jit(solution)/shard_map/all_gather | solution.py:759
  682.7 4.1 slice_convert_fusion
  686.9 6.5 reshape.154
  693.4 3.6 fusion.15
  697.1 6.8 copy.86
  (437 shorter events, 162.9 us)
Async XLA Ops:
  7.2 60.0 %all-gather.13.cloned.1.call-start = ((), (), s32[]{:S(2)}) async-start(), calls=%async_computation.4 | async-start | bytes 5308416 | tf_op jit(solution)/shard_map/all_gather | solution.py:618
  12.7 107.9 %all-gather.15.cloned.1.call-start = ((), (), s32[]{:S(2)}) async-start(), calls=%async_computation.5 | async-start | bytes 5308416 | tf_op jit(solution)/shard_map/all_gather | solution.py:618
  18.0 156.0 %all-gather.17.cloned.1.call-start = ((), (), s32[]{:S(2)}) async-start(), calls=%async_computation.6 | async-start | bytes 5308416 | tf_op jit(solution)/shard_map/all_gather | solution.py:618
  23.3 243.4 %all-gather.19.cloned.1.call-start = ((), (), s32[]{:S(2)}) async-start(), calls=%async_computation.7 | async-start | bytes 5308416 | tf_op jit(solution)/shard_map/all_gather | solution.py:621
  25.6 410.8 %all-reduce.2.cloned.1.call-start = ((), (), s32[]{:S(2)}) async-start(), calls=%async_computation.8 | async-start | bytes 3538944 | tf_op jit(solution)/shard_map/psum | solution.py:721
  26.9 1.8 collective-permute-start
  28.7 190.2 %copy-start.39 = (s32[9]{0:T(128)}, s32[9]{0:T(128)S(1)}, u32[]{:S(2)}) copy-start(s32[9]{0:T(128)S(1)} %concatenate.3.info) | copy-start | bytes 112
  85.8 1.5 collective-permute-start.1
  86.6 132.3 %copy-start.45 = (f32[1,512]{1,0:T(1,128)}, f32[1,512]{1,0:T(1,128)S(1)}, u32[]{:S(2)}) copy-start(f32[1,512]{1,0:T(1,128)S(1)} %get-tuple-element.122.bias.zbias) | copy-start | bytes 6148
  86.6 132.3 %copy-start.48 = (f32[1,512]{1,0:T(1,128)}, f32[1,512]{1,0:T(1,128)S(1)}, u32[]{:S(2)}) copy-start(f32[1,512]{1,0:T(1,128)S(1)} %get-tuple-element.130.gain.zgain) | copy-start | bytes 6148
  87.9 5.7 collective-permute-start.2
  93.6 5.9 collective-permute-start.3
  94.3 124.5 %copy-start.57 = (f32[2]{0:T(128)}, f32[2]{0:T(128)S(1)}, u32[]{:S(2)}) copy-start(f32[2]{0:T(128)S(1)} %fusion.14.cnt) | copy-start | bytes 28
  142.5 1.5 collective-permute-start.4
  144.6 5.9 collective-permute-start.5
  150.6 5.6 collective-permute-start.6
  194.1 28.4 %copy-start.2 = (f32[1728,512]{1,0:T(8,128)}, f32[1728,512]{1,0:T(8,128)S(1)}, u32[]{:S(2)}) copy-start(f32[1728,512]{1,0:T(8,128)S(1)} %get-tuple-element.57.x.z) | copy-start | bytes 10616836
  194.1 1.5 collective-permute-start.7
  195.6 27.0 %copy-start.17 = (f32[104,512]{1,0:T(8,128)}, f32[104,512]{1,0:T(8,128)S(1)}, u32[]{:S(2)}) copy-start(f32[104,512]{1,0:T(8,128)S(1)} %collective-permute-done.7.recv.recv_z) | copy-start | bytes 638980
  195.6 5.6 collective-permute-start.8
  201.2 17.6 %collective-permute-start.9 = (f32[8,512]{1,0:T(8,128)S(1)}, f32[8,512]{1,0:T(8,128)S(1)}, u32[]{:S(2)}, u32[]{:S(2)}) collective-permute-start(f32[8,512]{1,0:T(8,128)S(1)} %add.202), channel_id=1, source_target_pairs={{0,4},{1,5},{2,6},{3,7},{4,0},{5,1},{6,2},{7,3},{8,12},{9,13},{10,... | collective-permute-start | bytes 49160 | tf_op jit(solution)/shard_map/ppermute | solution.py:543
  223.9 1.3 collective-permute-start.10
  225.2 16.4 %collective-permute-start.11 = (f32[8,512]{1,0:T(8,128)S(1)}, f32[8,512]{1,0:T(8,128)}, u32[]{:S(2)}, u32[]{:S(2)}) collective-permute-start(f32[8,512]{1,0:T(8,128)S(1)} %add.205), channel_id=1, source_target_pairs={{0,2},{1,3},{2,0},{3,1},{4,6},{5,7},{6,4},{7,5},{8,10},{9,11},{10,... | collective-permute-start | bytes 49160 | tf_op jit(solution)/shard_map/ppermute | solution.py:543
  242.3 4.8 collective-permute-start.12
  255.6 1.5 collective-permute-start.13
  257.7 3.7 collective-permute-start.14
  261.5 4.7 collective-permute-start.15
  276.9 24.0 %copy-start.68 = (f32[1,512]{1,0:T(1,128)S(1)}, f32[1,512]{1,0:T(1,128)}, u32[]{:S(2)}) copy-start(f32[1,512]{1,0:T(1,128)} %get-tuple-element.133.bias) | copy-start | bytes 6148
  291.0 1.5 collective-permute-start.16
  292.5 3.7 collective-permute-start.17
  296.2 4.6 collective-permute-start.18
  307.0 1.5 collective-permute-start.19
  308.4 3.7 collective-permute-start.20
  312.2 4.6 collective-permute-start.21
  316.9 29.4 %copy-start.8 = (bf16[512,512]{1,0:T(8,128)(2,1)S(1)}, bf16[512,512]{1,0:T(8,128)(2,1)}, u32[]{:S(2)}) copy-start(bf16[512,512]{1,0:T(8,128)(2,1)} %all_gather.58.w) | copy-start | bytes 1572868
  316.9 29.4 %copy-start.34 = (f32[1,512]{1,0:T(1,128)S(1)}, f32[1,512]{1,0:T(1,128)}, u32[]{:S(2)}) copy-start(f32[1,512]{1,0:T(1,128)} %copy-done.33) | copy-start | bytes 6148
  316.9 29.4 %copy-start.36 = (f32[1,512]{1,0:T(1,128)S(1)}, f32[1,512]{1,0:T(1,128)}, u32[]{:S(2)}) copy-start(f32[1,512]{1,0:T(1,128)} %copy-done.35) | copy-start | bytes 6148
  336.7 1.2 collective-permute-start.22
  337.8 3.7 collective-permute-start.23
  341.6 4.6 collective-permute-start.24
  354.2 1.2 collective-permute-start.25
  355.4 3.7 collective-permute-start.26
  359.1 4.6 collective-permute-start.27
  372.3 188.2 %reduce-scatter.11.cloned.1.call-start = ((), (), s32[]{:S(2)}) async-start(), calls=%async_computation.12 | async-start | bytes 6488064 | tf_op jit(solution)/shard_map/reduce_scatter | solution.py:756
  396.1 59.6 %copy-start.4 = (f32[1728,512]{1,0:T(8,128)S(1)}, f32[1728,512]{1,0:T(8,128)}, u32[]{:S(2)}) copy-start(f32[1728,512]{1,0:T(8,128)} %copy-done.2) | copy-start | bytes 10616836
  396.1 59.6 %copy-start.21 = (f32[8,512]{1,0:T(8,128)S(1)}, f32[8,512]{1,0:T(8,128)}, u32[]{:S(2)}) copy-start(f32[8,512]{1,0:T(8,128)} %copy-done.19) | copy-start | bytes 49156
  396.1 174.8 %all-gather.21.cloned.1.call-start = ((), (), s32[]{:S(2)}) async-start(), calls=%async_computation.13 | async-start | bytes 2211840 | tf_op jit(solution)/shard_map/all_gather | solution.py:759
  396.8 177.8 %reduce-scatter.9.cloned.1.call-start = ((), (), s32[]{:S(2)}) async-start(), calls=%async_computation.11 | async-start | bytes 1327104 | tf_op jit(solution)/shard_map/reduce_scatter | solution.py:756
  437.3 18.4 %collective-permute-start.28 = (bf16[96,512]{1,0:T(8,128)(2,1)S(1)}, bf16[96,512]{1,0:T(8,128)(2,1)S(1)}, u32[]{:S(2)}, u32[]{:S(2)}) collective-permute-start(bf16[96,512]{1,0:T(8,128)(2,1)S(1)} %slice_select_fusion), channel_id=1, source_target_pairs={{0,1},{1,0},{2,3},{3,2},{4,5},{5,4},{6,7},{7,6},{8,9},{9,8},{10,11... | collective-permute-start | bytes 294920 | tf_op jit(solution)/shard_map/ppermute | solution.py:543
  437.4 1.5 collective-permute-start.29
  439.7 3.7 collective-permute-start.30
  443.4 4.8 collective-permute-start.31
  448.2 3.7 collective-permute-start.32
  452.0 3.7 collective-permute-start.33
  455.7 25.5 %copy-start.29 = (f32[8,512]{1,0:T(8,128)}, f32[8,512]{1,0:T(8,128)S(1)}, u32[]{:S(2)}) copy-start(f32[8,512]{1,0:T(8,128)S(1)} %add.227.sums) | copy-start | bytes 49156
  487.4 119.7 %reduce-scatter.7.cloned.1.call-start = ((), (), s32[]{:S(2)}) async-start(), calls=%async_computation.10 | async-start | bytes 1327104 | tf_op jit(solution)/shard_map/reduce_scatter | solution.py:756
  487.6 1.7 collective-permute-start.34
  490.1 4.3 collective-permute-start.35
  494.4 5.4 collective-permute-start.36
  526.9 114.1 %reduce-scatter.5.cloned.1.call-start = ((), (), s32[]{:S(2)}) async-start(), calls=%async_computation.9 | async-start | bytes 1327104 | tf_op jit(solution)/shard_map/reduce_scatter | solution.py:756
  526.9 1.7 collective-permute-start.37
  529.4 3.7 collective-permute-start.38
  533.1 4.6 collective-permute-start.39
  560.4 122.3 %all-gather.23.cloned.1.call-start = ((), (), s32[]{:S(2)}) async-start(), calls=%async_computation.14 | async-start | bytes 3604480 | tf_op jit(solution)/shard_map/all_gather | solution.py:759
  (121 other events, 779.1 us)
Sparse Core Ops, SparseCore 0:
  12.8 54.3 all-gather.12
  69.4 51.1 all-gather.14
  122.8 51.1 all-gather.16
  176.1 55.2 all-gather.18
  372.4 63.8 all-reduce.1
  438.5 65.7 reduce-scatter.10
  506.7 30.9 all-gather.20
  540.5 32.8 reduce-scatter.8
  576.3 30.7 reduce-scatter.6
  609.8 31.1 reduce-scatter.4
  642.8 39.8 all-gather.22

commit v2 on v1

v2 whole, which is shorter than its diff:
```python
import functools
import math

import jax
import jax.numpy as jnp
from jax import lax
from jax.experimental import pallas as pl
from jax.experimental.pallas import tpu as pltpu
from jax.sharding import PartitionSpec as P

HEIGHT = 36
WIDTH = 48
BAND = 18
HALF_WIDTH = 24
CANVAS = 2
TASKS = 3
COLS = CANVAS * WIDTH
GROUPS = COLS // HALF_WIDTH
EPSILON = 1e-05
TAPS = 9
TILE_ROWS = 6
PIECE = 16
MIB = 2**20
BF = jnp.bfloat16
F32 = jnp.float32
NT = (((1,), (1,)), ((), ()))
TN = (((0,), (0,)), ((), ()))

ANY = pl.BlockSpec(memory_space=pl.ANY)
HBM = pl.BlockSpec(memory_space=pltpu.HBM)
SMEM = pl.BlockSpec(memory_space=pltpu.SMEM)


def affine(row, co, scale, shift):
    step = row.shape[0] // GROUPS
    return jnp.concatenate(
        [
            row[step * j : step * (j + 1)] * co[4 * scale + j : 4 * scale + j + 1, :]
            + co[4 * shift + j : 4 * shift + j + 1, :]
            for j in range(GROUPS)
        ],
        axis=0,
    )


def scaled(row, co, scale):
    step = row.shape[0] // GROUPS
    return jnp.concatenate(
        [
            row[step * j : step * (j + 1)] * co[4 * scale + j : 4 * scale + j + 1, :]
            for j in range(GROUPS)
        ],
        axis=0,
    )


def sigmoid(v):
    return 0.5 * jnp.tanh(0.5 * v) + 0.5


def silu(v):
    return v * sigmoid(v)


def silu_slope(v):
    s = sigmoid(v)
    return s * (1.0 + v * (1.0 - s))


def norm_coefs(co, base, stats, params, which, cnt, info):
    gain = params[which : which + 1, :]
    bias = params[which + 6 : which + 7, :]
    means, scales = [], []
    for d in range(2):
        mean = stats[d : d + 1, :] / cnt[d]
        var = stats[2 + d : 3 + d, :] / cnt[d] - mean * mean
        means.append(mean)
        scales.append(lax.rsqrt(var + EPSILON))
    for j in range(GROUPS):
        one = info[j] == 1
        mean = jnp.where(one, means[1], means[0])
        scale = jnp.where(one, scales[1], scales[0])
        full = scale * gain
        co[4 * base + j : 4 * base + j + 1, :] = full
        co[4 * base + 4 + j : 4 * base + 5 + j, :] = bias - mean * full
        co[4 * base + 8 + j : 4 * base + 9 + j, :] = scale
        co[4 * base + 12 + j : 4 * base + 13 + j, :] = -mean * scale


def grad_coefs(co, base, norm, sums, cnt, info):
    for j in range(GROUPS):
        one = info[j] == 1
        count = jnp.where(one, cnt[1], cnt[0])
        plain = jnp.where(one, sums[1:2, :], sums[0:1, :]) / count
        cross = jnp.where(one, sums[3:4, :], sums[2:3, :]) / count
        full = co[4 * norm + j : 4 * norm + j + 1, :]
        scale = co[4 * norm + 8 + j : 4 * norm + 9 + j, :]
        shift = co[4 * norm + 12 + j : 4 * norm + 13 + j, :]
        co[4 * base + j : 4 * base + j + 1, :] = -full * cross * scale
        co[4 * base + 4 + j : 4 * base + 5 + j, :] = -full * (plain + cross * shift)


def grad_row(g, z, co, norm, base):
    return scaled(g, co, norm) + affine(z, co, base, base + 1)


def add_sums(acc, slot, values):
    step = HALF_WIDTH // 8
    count = values.shape[0] // COLS
    channels = values.shape[1]
    acc[slot] += jnp.sum(
        values.reshape(count, GROUPS, step, 8, channels), axis=(0, 2)
    )


def put_sums(acc, info, out, start):
    for slot in range(2):
        groups = [jnp.sum(acc[slot, j], axis=0, keepdims=True) for j in range(GROUPS)]
        for d in range(2):
            total = jnp.zeros_like(groups[0])
            for j in range(GROUPS):
                total = total + jnp.where(info[j] == d, groups[j], 0.0)
            row = start + 2 * slot + d
            out[row : row + 1, :] = total
    out[start + 4 : start + 8, :] = jnp.zeros((4, out.shape[1]), F32)


def put_edge(out, ref, info, rows):
    start = jnp.where(info[6] == 1, 0, (rows - 1) * COLS)
    out[0:COLS, :] = ref[pl.ds(pl.multiple_of(start, COLS), COLS), :].astype(out.dtype)


def make_masks(mk, info):
    col = lax.broadcasted_iota(jnp.int32, mk.shape[1:], 0)
    small = (info[4] == 1, info[5] == 1)
    left = (col == 0) | (col == WIDTH)
    right = (col == WIDTH - 1) | (col == COLS - 1)
    for s in range(2):
        left = left | ((col == s * WIDTH + HALF_WIDTH) & small[s])
        right = right | ((col == s * WIDTH + HALF_WIDTH - 1) & small[s])
    mk[0] = jnp.where(left, 0.0, 1.0)
    mk[1] = jnp.where(right, 0.0, 1.0)


def put_row(taps, at, row, mk):
    parts = row.shape[1] // mk.shape[2]
    left = jnp.concatenate([mk[0]] * parts, axis=1)
    right = jnp.concatenate([mk[1]] * parts, axis=1)
    here = pl.ds(pl.multiple_of(at * COLS, COLS), COLS)
    taps[0, here, :] = (pltpu.roll(row, 1, 0) * left).astype(BF)
    taps[1, here, :] = row.astype(BF)
    taps[2, here, :] = (pltpu.roll(row, COLS - 1, 0) * right).astype(BF)


def put_halo(taps, row, mk, info, rows):
    step = COLS // GROUPS
    keep = [jnp.where(info[4 + j // 2] == 1, 0.0, 1.0) for j in range(GROUPS)]
    row = jnp.concatenate(
        [row[step * j : step * (j + 1)] * keep[j] for j in range(GROUPS)], axis=0
    )
    put_row(taps, jnp.where(info[6] == 1, 0, rows + 1), row, mk)
    put_row(taps, jnp.where(info[6] == 1, rows + 1, 0), jnp.zeros_like(row), mk)


def conv_tile(taps, w, at, rows, transpose):
    acc = None
    channels = taps.shape[2]
    for t in range(TAPS):
        di, dj = divmod(t, 3)
        a = taps[dj, (at + di) * COLS : (at + di + rows) * COLS, :]
        if transpose:
            k = w[:, (8 - t) * channels : (9 - t) * channels]
            r = jnp.dot(a, k, preferred_element_type=F32)
        else:
            k = w[:, t * channels : (t + 1) * channels]
            r = lax.dot_general(a, k, NT, preferred_element_type=F32)
        acc = r if acc is None else acc + r
    return acc


def row_at(r):
    return pl.ds(pl.multiple_of(r * COLS, COLS), COLS)


def tile_at(m):
    return slice(m * TILE_ROWS * COLS, (m + 1) * TILE_ROWS * COLS)


def loop(count, body):
    def step(i, carry):
        body(i)
        return carry

    lax.fori_loop(0, count, step, 0)


def pooled(buf, values):
    half = COLS // 2
    parts, _, lanes = buf.shape
    out = []
    for c in range(parts):
        buf[c] = values[:, c * lanes : (c + 1) * lanes]
        out.append(buf[c, pl.ds(0, half, stride=2), :] + buf[c, pl.ds(1, half, stride=2), :])
    return jnp.concatenate(out, axis=1) * 0.25


def spread(buf, values):
    half = COLS // 2
    parts, _, lanes = buf.shape
    quarter = values.astype(F32) * 0.25
    out = []
    for c in range(parts):
        part = quarter[:, c * lanes : (c + 1) * lanes]
        buf[c, pl.ds(0, half, stride=2), :] = part
        buf[c, pl.ds(1, half, stride=2), :] = part
        out.append(buf[c])
    return jnp.concatenate(out, axis=1)


class Copies:
    def __init__(self, sems):
        self.sems = sems
        self.used = 0
        self.open = []

    def start(self, src, dst):
        copy = pltpu.make_async_copy(src, dst, self.sems.at[self.used])
        self.used += 1
        copy.start()
        return copy

    def put(self, src, dst):
        self.open.append(self.start(src, dst))

    def tiles(self, src, dst, rows):
        return [
            self.start(src.at[pl.ds(m * TILE_ROWS * COLS, TILE_ROWS * COLS)],
                       dst.at[pl.ds(m * TILE_ROWS * COLS, TILE_ROWS * COLS)])
            for m in range(rows // TILE_ROWS)
        ]

    def put_tile(self, src, dst, m):
        here = pl.ds(m * TILE_ROWS * COLS, TILE_ROWS * COLS)
        self.put(src.at[here], dst.at[here])

    def weights(self, pieces, place, dst):
        if len(pieces) == 1:
            return [self.start(pieces[0], dst)]
        copies = []
        count = pieces[0].shape[0] // PIECE
        for i, piece in enumerate(pieces):
            for k in range(count):
                row = pl.multiple_of(place[i * count + k], PIECE)
                copies.append(
                    self.start(piece.at[pl.ds(k * PIECE, PIECE)], dst.at[pl.ds(row, PIECE)])
                )
        return copies

    def finish(self):
        for copy in self.open:
            copy.wait()


def fetch_sums(io, sums, dst):
    return [io.start(part, dst.at[k]) for k, part in enumerate(sums)]


def settle(dst, count):
    if count == 4:
        dst[0] = (dst[0] + dst[1]) + (dst[2] + dst[3])
    return dst.at[0]


def wait(*copies):
    for copy in copies:
        copy.wait()


def tile_rows(m):
    return range(m * TILE_ROWS, (m + 1) * TILE_ROWS)


def each_row(m, body):
    loop(TILE_ROWS, lambda r: body(m * TILE_ROWS + r))


def cast_kernel(pick, count, spot, *refs):
    sources, out, wide, sems = refs[:count], refs[-count - 2], refs[-count - 1 : -1], refs[-1]
    io = Copies(sems)
    rows, channels = out.shape[0], wide[0].shape[2]
    first = pl.multiple_of(spot[0] * rows, rows) if pick else 0
    reads = []
    for src, dst in zip(sources, wide):
        if len(src.shape) == 4:
            src = src.at[spot[1]]
        reads.append(io.start(src.at[:, pl.ds(first, rows), :], dst))
    start = 0
    for src, read in zip(wide, reads):
        read.wait()
        for t in range(src.shape[0]):
            out[:, start : start + channels] = src[t].astype(BF)
            start += channels


def conv_outputs(rows, info, w, z, zv, pay, payv, quarter, taps, acc, io, w_reads):
    if quarter is not None:
        width = quarter.shape[2]
        io.put(taps.at[:, :, pl.ds(pl.multiple_of(info[7] * width, 128), width)], quarter)
    wait(*w_reads)
    for m in range(rows // TILE_ROWS):
        out = conv_tile(taps, w, m * TILE_ROWS, TILE_ROWS, False)
        zv[tile_at(m), :] = out
        io.put_tile(zv, z, m)
        add_sums(acc, 0, out)
        add_sums(acc, 1, out * out)
    put_edge(payv, zv, info, rows)
    put_sums(acc, info, payv, COLS)
    io.put(payv, pay)


def first_conv_kernel(rows, info, place, x, halo, pieces, z, zv, pay, quarter, xv, hv, payv, wv, taps, mk, acc, sems):
    io = Copies(sems)
    reads = io.tiles(x, xv, rows)
    halo_read = io.start(halo, hv)
    w_reads = io.weights(pieces, place, wv)
    make_masks(mk, info)
    acc[...] = jnp.zeros_like(acc)
    for m, read in enumerate(reads):
        read.wait()
        each_row(m, lambda r: put_row(taps, r + 1, xv[row_at(r), :].astype(F32), mk))
    halo_read.wait()
    put_halo(taps, hv[...].astype(F32), mk, info, rows)
    conv_outputs(rows, info, wv, z, zv, pay, payv, quarter, taps, acc, io, w_reads)
    io.finish()


def conv_kernel(
    rows, which, info, cnt, place, params, x, recv, stats, pieces, z, zv, pay, quarter,
    pv, hv, sv, payv, wv, taps, mk, acc, co, sems,
):
    io = Copies(sems)
    small = [*fetch_sums(io, stats, sv), io.start(params, pv)]
    halo_read = io.start(recv, hv)
    w_reads = io.weights(pieces, place, wv)
    make_masks(mk, info)
    acc[...] = jnp.zeros_like(acc)
    wait(*small)
    norm_coefs(co, 0, settle(sv, len(stats)), pv, which, cnt, info)
    loop(rows, lambda r: put_row(taps, r + 1, silu(affine(x[row_at(r), :], co, 0, 1)), mk))
    halo_read.wait()
    put_halo(taps, silu(affine(hv[0:COLS, :], co, 0, 1)), mk, info, rows)
    conv_outputs(rows, info, wv, z, zv, pay, payv, quarter, taps, acc, io, w_reads)
    io.finish()


def enter_kernel(
    rows, which, info, cnt, params, x, recv, stats, w, low, pool, u, uv, pay,
    pv, hv, sv, wv, lowv, poolv, payv, acc, co, buf, sems,
):
    io = Copies(sems)
    small = [*fetch_sums(io, stats, sv), io.start(params, pv)]
    halo_read = io.start(recv, hv)
    w_read = io.start(w.at[:, pl.ds(0, wv.shape[1])], wv)
    acc[...] = jnp.zeros_like(acc)
    wait(*small)
    norm_coefs(co, 0, settle(sv, len(stats)), pv, which, cnt, info)
    half = COLS // 2

    def pair(i):
        first = silu(affine(x[row_at(2 * i), :], co, 0, 1))
        second = silu(affine(x[row_at(2 * i + 1), :], co, 0, 1))
        lowv[row_at(2 * i), :] = first.astype(BF)
        lowv[row_at(2 * i + 1), :] = second.astype(BF)
        poolv[pl.ds(pl.multiple_of(i * half, half), half), :] = pooled(
            buf, first + second
        ).astype(BF)

    halo_read.wait()
    lowv[rows * COLS : (rows + 1) * COLS, :] = silu(affine(hv[0:COLS, :], co, 0, 1)).astype(BF)
    for m in range(rows // TILE_ROWS):
        loop(TILE_ROWS // 2, lambda i: pair(m * (TILE_ROWS // 2) + i))
        if m == 0:
            w_read.wait()
        out = lax.dot_general(lowv[tile_at(m), :], wv[...], NT, preferred_element_type=F32)
        uv[tile_at(m), :] = out
        io.put_tile(uv, u, m)
        add_sums(acc, 0, out)
        add_sums(acc, 1, out * out)
    io.put(lowv, low)
    io.put(poolv, pool)
    put_sums(acc, info, payv, 0)
    io.put(payv, pay)
    io.finish()


def mask_kernel(
    rows, which, info, cnt, params, u, stats, w, p, q, qv, pay, pv, sv, wv, ev, payv, acc, co, sems
):
    io = Copies(sems)
    small = [*fetch_sums(io, stats, sv), io.start(params, pv)]
    w_read = io.start(w.at[:, pl.ds(wv.shape[1], wv.shape[1])], wv)
    acc[...] = jnp.zeros_like(acc)
    wait(*small)
    norm_coefs(co, 0, settle(sv, len(stats)), pv, which, cnt, info)

    def each(r):
        ev[row_at(r), :] = silu(affine(u[row_at(r), :], co, 0, 1)).astype(BF)

    for m in range(rows // TILE_ROWS):
        each_row(m, each)
        io.put_tile(ev, p, m)
        if m == 0:
            w_read.wait()
        out = lax.dot_general(ev[tile_at(m), :], wv[...], NT, preferred_element_type=F32)
        qv[tile_at(m), :] = out
        io.put_tile(qv, q, m)
        add_sums(acc, 0, out)
        add_sums(acc, 1, out * out)
    put_edge(payv, qv, info, rows)
    put_sums(acc, info, payv, COLS)
    io.put(payv, pay)
    io.finish()


def branch_conv_kernel(
    rows, which, info, cnt, params, low, q, recv, stats, w, y, yv, pay, wide_taps,
    pv, lv, hv, sv, payv, wv, taps, mk, acc, co, sems,
):
    io = Copies(sems)
    small = [*fetch_sums(io, stats, sv), io.start(params, pv)]
    low_read = io.start(low, lv)
    halo_read = io.start(recv, hv)
    w_read = io.start(w, wv)
    make_masks(mk, info)
    acc[...] = jnp.zeros_like(acc)
    wait(*small)
    norm_coefs(co, 0, settle(sv, len(stats)), pv, which, cnt, info)

    def masked(source, gated):
        return source.astype(F32) * sigmoid(affine(gated, co, 0, 1))

    low_read.wait()
    loop(rows, lambda r: put_row(taps, r + 1, masked(lv[row_at(r), :], q[row_at(r), :]), mk))
    halo_read.wait()
    put_halo(taps, masked(lv[rows * COLS : (rows + 1) * COLS, :], hv[0:COLS, :]), mk, info, rows)
    io.put(taps, wide_taps)
    conv_outputs(rows, info, wv, y, yv, pay, payv, None, taps, acc, io, [w_read])
    io.finish()


def turn_kernel(
    rows, which, info, cnt, params, y, stats, cot, pool, gv, pay, pv, sv, cv, poolv, payv, acc, co, buf, sems
):
    io = Copies(sems)
    small = [*fetch_sums(io, stats, sv), io.start(params, pv)]
    cot_read = io.start(cot.at[info[9]], cv)
    acc[...] = jnp.zeros_like(acc)
    wait(*small)
    norm_coefs(co, 0, settle(sv, len(stats)), pv, which, cnt, info)
    half = COLS // 2

    def pair(i):
        part = pl.ds(pl.multiple_of(i * half, half), half)
        ct = spread(buf, cv[part, :])
        total = None
        for k in range(2):
            here = row_at(2 * i + k)
            row = y[here, :]
            v = affine(row, co, 0, 1)
            s = sigmoid(v)
            f = v * s
            total = f if total is None else total + f
            gr = ct * (s * (1.0 + v * (1.0 - s)))
            gv[here, :] = gr
            add_sums(acc, 0, gr)
            add_sums(acc, 1, gr * affine(row, co, 2, 3))
        poolv[part, :] = pooled(buf, total).astype(BF)

    cot_read.wait()
    loop(rows // 2, pair)
    io.put(poolv, pool)
    put_edge(payv, gv, info, rows)
    put_sums(acc, info, payv, COLS)
    io.put(payv, pay)
    io.finish()


def branch_back_kernel(
    rows, info, cnt, params, g, y, recv_g, recv_y, stats, sums, w, low, q, qstats,
    e, gv, gs, pay,
    pv, yv, hv, kv, sv, tv, qsv, lv, qv, ev, payv, wv, taps, mk, acc, co, sems,
):
    io = Copies(sems)
    small = [*fetch_sums(io, stats, sv), *fetch_sums(io, sums, tv), *fetch_sums(io, qstats, qsv),
             io.start(params, pv)]
    reads = io.tiles(y, yv, rows)
    halo_reads = [io.start(recv_g, hv), io.start(recv_y, kv)]
    w_read = io.start(w, wv)
    low_read = io.start(low.at[pl.ds(0, rows * COLS)], lv)
    q_read = io.start(q, qv)
    make_masks(mk, info)
    acc[...] = jnp.zeros_like(acc)
    wait(*small)
    norm_coefs(co, 0, settle(sv, len(stats)), pv, 5, cnt, info)
    grad_coefs(co, 4, 0, settle(tv, len(sums)), cnt, info)
    norm_coefs(co, 6, settle(qsv, len(qstats)), pv, 4, cnt, info)

    def each(r):
        row = grad_row(g[row_at(r), :], yv[row_at(r), :], co, 0, 4)
        ev[row_at(r), :] = row.astype(BF)
        put_row(taps, r + 1, row, mk)

    for m, read in enumerate(reads):
        read.wait()
        each_row(m, each)
        io.put_tile(ev, e, m)
    wait(*halo_reads)
    put_halo(taps, grad_row(hv[0:COLS, :], kv[0:COLS, :], co, 0, 4), mk, info, rows)
    wait(w_read, low_read, q_read)

    def post(r):
        here = row_at(r)
        grad = gv[here, :]
        row = qv[here, :]
        gate = sigmoid(affine(row, co, 6, 7))
        yv[here, :] = grad * gate
        out = grad * lv[here, :].astype(F32) * gate * (1.0 - gate)
        gv[here, :] = out
        add_sums(acc, 0, out)
        add_sums(acc, 1, out * affine(row, co, 8, 9))

    for m in range(rows // TILE_ROWS):
        gv[tile_at(m), :] = conv_tile(taps, wv, m * TILE_ROWS, TILE_ROWS, True)
        each_row(m, post)
        io.put_tile(yv, gs, m)
    put_sums(acc, info, payv, 0)
    io.put(payv, pay)
    io.finish()


def mask_back_kernel(
    rows, info, cnt, params, g, q, stats, sums, w, u, ustats, e, gv, pay,
    pv, qv, uv, sv, tv, usv, wv, ev, payv, acc, co, sems,
):
    io = Copies(sems)
    small = [*fetch_sums(io, stats, sv), *fetch_sums(io, sums, tv), *fetch_sums(io, ustats, usv),
             io.start(params, pv)]
    reads = io.tiles(q, qv, rows)
    w_read = io.start(w.at[:, pl.ds(wv.shape[1], wv.shape[1])], wv)
    u_reads = io.tiles(u, uv, rows)
    acc[...] = jnp.zeros_like(acc)
    wait(*small)
    norm_coefs(co, 0, settle(sv, len(stats)), pv, 4, cnt, info)
    grad_coefs(co, 4, 0, settle(tv, len(sums)), cnt, info)
    norm_coefs(co, 6, settle(usv, len(ustats)), pv, 3, cnt, info)

    def each(r):
        ev[row_at(r), :] = grad_row(g[row_at(r), :], qv[row_at(r), :], co, 0, 4).astype(BF)

    def post(r):
        here = row_at(r)
        row = uv[here, :]
        out = gv[here, :] * silu_slope(affine(row, co, 6, 7))
        gv[here, :] = out
        add_sums(acc, 0, out)
        add_sums(acc, 1, out * affine(row, co, 8, 9))

    for m, read in enumerate(reads):
        read.wait()
        each_row(m, each)
        io.put_tile(ev, e, m)
        if m == 0:
            w_read.wait()
        gv[tile_at(m), :] = jnp.dot(ev[tile_at(m), :], wv[...], preferred_element_type=F32)
        u_reads[m].wait()
        each_row(m, post)
    put_sums(acc, info, payv, 0)
    io.put(payv, pay)
    io.finish()


def leave_kernel(
    rows, info, cnt, params, g, u, stats, sums, w, gs, z, zstats, cot, e, out, pay,
    pv, gv, uv, sv, tv, zsv, wv, gsv, zv, cv, ev, ov, payv, acc, co, buf, sems,
):
    io = Copies(sems)
    small = [*fetch_sums(io, stats, sv), *fetch_sums(io, sums, tv), *fetch_sums(io, zstats, zsv),
             io.start(params, pv)]
    reads = io.tiles(u, uv, rows)
    w_read = io.start(w.at[:, pl.ds(0, wv.shape[1])], wv)
    later = list(zip(io.tiles(gs, gsv, rows), io.tiles(z, zv, rows)))
    cot_read = io.start(cot, cv)
    acc[...] = jnp.zeros_like(acc)
    wait(*small)
    norm_coefs(co, 0, settle(sv, len(stats)), pv, 3, cnt, info)
    grad_coefs(co, 4, 0, settle(tv, len(sums)), cnt, info)
    norm_coefs(co, 6, settle(zsv, len(zstats)), pv, 2, cnt, info)
    half = COLS // 2
    active = info[8] == 1

    def each(r):
        ev[row_at(r), :] = grad_row(g[row_at(r), :], uv[row_at(r), :], co, 0, 4).astype(BF)

    def post(i):
        ct = spread(buf, cv[pl.ds(pl.multiple_of(i * half, half), half), :])
        for k in range(2):
            here = row_at(2 * i + k)
            grad = jnp.where(active, gv[here, :] + gsv[here, :], ct)
            ov[here, :] = grad.astype(BF)
            row = zv[here, :]
            grad = grad * silu_slope(affine(row, co, 6, 7))
            add_sums(acc, 0, grad)
            add_sums(acc, 1, grad * affine(row, co, 8, 9))

    for m, read in enumerate(reads):
        read.wait()
        each_row(m, each)
        io.put_tile(ev, e, m)
        if m == 0:
            wait(w_read, cot_read)
        gv[tile_at(m), :] = jnp.dot(ev[tile_at(m), :], wv[...], preferred_element_type=F32)
        wait(*later[m])
        loop(TILE_ROWS // 2, lambda i: post(m * (TILE_ROWS // 2) + i))
        io.put_tile(ov, out, m)
    put_sums(acc, info, payv, 0)
    io.put(payv, pay)
    io.finish()


def trunk_back_kernel(
    rows, which, top, info, cnt, place, params, g, z, recv_g, recv_z, stats, sums, x, xstats, pieces,
    e, out, pay, pv, zv, hv, kv, sv, tv, xv, xsv, ev, payv, wv, taps, mk, co, acc, *rest
):
    io = Copies(rest[-1])
    small = [*fetch_sums(io, stats, sv), *fetch_sums(io, sums, tv), *fetch_sums(io, xstats, xsv),
             io.start(params, pv)]
    gv = rest[:-1] if top else (g,)
    reads = [io.tiles(z, zv, rows)]
    if top:
        reads += [io.tiles(a, b, rows) for a, b in zip(g, gv)]
    reads = list(zip(*reads))
    halo_reads = [io.start(recv_g, hv), io.start(recv_z, kv)]
    w_reads = io.weights(pieces, place, wv)
    x_reads = io.tiles(x, xv, rows)
    acc[...] = jnp.zeros_like(acc)
    make_masks(mk, info)
    wait(*small)
    norm_coefs(co, 0, settle(sv, len(stats)), pv, which, cnt, info)
    grad_coefs(co, 4, 0, settle(tv, len(sums)), cnt, info)
    norm_coefs(co, 6, settle(xsv, len(xstats)), pv, which - 1, cnt, info)

    def grad(g_row, z_row):
        if top:
            g_row = g_row * silu_slope(affine(z_row, co, 0, 1))
        return grad_row(g_row, z_row, co, 0, 4)

    def each(r):
        g_row = gv[0][row_at(r), :]
        if top:
            g_row = g_row.astype(F32) + gv[1][row_at(r), :].astype(F32)
        row = grad(g_row, zv[row_at(r), :])
        ev[row_at(r), :] = row.astype(BF)
        put_row(taps, r + 1, row, mk)

    for m, pair in enumerate(reads):
        wait(*pair)
        each_row(m, each)
        io.put_tile(ev, e, m)
    wait(*halo_reads)
    put_halo(taps, grad(hv[0:COLS, :].astype(F32), kv[0:COLS, :]), mk, info, rows)
    wait(*w_reads)

    def post(r):
        here = row_at(r)
        row = xv[here, :]
        value = out[here, :] * silu_slope(affine(row, co, 6, 7))
        out[here, :] = value
        add_sums(acc, 0, value)
        add_sums(acc, 1, value * affine(row, co, 8, 9))

    for m in range(rows // TILE_ROWS):
        out[tile_at(m), :] = conv_tile(taps, wv, m * TILE_ROWS, TILE_ROWS, True)
        x_reads[m].wait()
        each_row(m, post)
    put_edge(payv, out, info, rows)
    put_sums(acc, info, payv, COLS)
    io.put(payv, pay)
    io.finish()


def wide_quarter(rows, quarter):
    width = rows * COLS
    return jnp.concatenate(
        [quarter[t % 3, (t // 3) * COLS : (t // 3) * COLS + width, :] for t in range(TAPS)], axis=1
    )


def last_grad_kernel(
    rows, info, place, cnt, params, g, z, recv_g, recv_z, stats, sums, quarter,
    e, mine, other, pv, zv, hv, kv, sv, tv, av, ev, wv, co, sems,
):
    io = Copies(sems)
    small = [*fetch_sums(io, stats, sv), *fetch_sums(io, sums, tv), io.start(params, pv)]
    reads = io.tiles(z, zv, rows)
    halo_reads = [io.start(recv_g, hv), io.start(recv_z, kv)]
    a_read = io.start(quarter, av)
    wait(*small)
    norm_coefs(co, 0, settle(sv, len(stats)), pv, 0, cnt, info)
    grad_coefs(co, 4, 0, settle(tv, len(sums)), cnt, info)

    def each(r):
        ev[row_at(r + 1), :] = grad_row(g[row_at(r), :], zv[row_at(r), :], co, 0, 4).astype(BF)

    for m, read in enumerate(reads):
        read.wait()
        each_row(m, each)
    wait(*halo_reads)
    row = grad_row(hv[0:COLS, :], kv[0:COLS, :], co, 0, 4)
    step = COLS // GROUPS
    row = jnp.concatenate(
        [
            row[step * j : step * (j + 1)] * jnp.where(info[4 + j // 2] == 1, 0.0, 1.0)
            for j in range(GROUPS)
        ],
        axis=0,
    ).astype(BF)
    ev[row_at(jnp.where(info[6] == 1, 0, rows + 1)), :] = row
    ev[row_at(jnp.where(info[6] == 1, rows + 1, 0)), :] = jnp.zeros_like(row)
    io.put(ev, e)
    a_read.wait()
    wv[...] = lax.dot_general(
        ev[COLS : (rows + 1) * COLS, :], wide_quarter(rows, av), TN, preferred_element_type=F32
    ).astype(BF)
    if other is None:
        io.put(wv, mine)
    else:
        size = mine.shape[0] // 4
        for k, mask in enumerate((0, 2, 1, 3)):
            for side, dst in ((0, mine), (1, other)):
                block = info[10] ^ (2 * mask + side)
                src = wv.at[pl.ds(pl.multiple_of(block * size, size), size)]
                io.put(src, dst.at[pl.ds(k * size, size)])
    io.finish()


def whole_last_grad_kernel(rows, *refs):
    last_grad_kernel(rows, *refs[:13], None, *refs[13:])


def last_conv_kernel(m, info, place, e, pieces, *refs):
    out, ev, ov, wv, taps, mk, sems = refs[-7:]
    io = Copies(sems)
    high = TILE_ROWS + 2
    read = io.start(e.at[pl.ds(m * TILE_ROWS * COLS, high * COLS)], ev)
    w_reads = io.weights(pieces, place, wv)
    make_masks(mk, info)
    read.wait()
    loop(high, lambda r: put_row(taps, r, ev[row_at(r), :].astype(F32), mk))
    wait(*w_reads)
    ov[...] = conv_tile(taps, wv, 0, TILE_ROWS, True)
    io.put(ov, out.at[pl.ds(m * TILE_ROWS * COLS, TILE_ROWS * COLS)])
    io.finish()


def trunk_wgrad_kernel(rows, quarter, e, part, av, ev, ov, sems):
    io = Copies(sems)
    reads = [io.start(quarter, av), io.start(e, ev)]
    wait(*reads)
    ov[...] = lax.dot_general(ev[...], wide_quarter(rows, av), TN, preferred_element_type=F32).astype(BF)
    io.put(ov, part)
    io.finish()


def branch_wgrad_kernel(rows, taps, ey, p, eq, low, eu, out, tv, yv, pv, qv, lv, uv, ov, sems):
    width = rows * COLS
    channels = ey.shape[1]
    io = Copies(sems)
    y_read = io.start(ey, yv)
    t_reads = [io.start(taps.at[k], tv.at[k]) for k in range(3)]
    reads = [io.start(p, pv), io.start(eq, qv), io.start(low.at[pl.ds(0, width)], lv), io.start(eu, uv)]
    y_read.wait()

    def emit(at, e, a):
        here = pl.ds(at * channels, channels)
        ov[:, here] = lax.dot_general(e, a, TN, preferred_element_type=F32).astype(BF)
        io.put(ov.at[:, here], out.at[:, here])

    for dj in range(3):
        t_reads[dj].wait()
        for di in range(3):
            emit(3 * di + dj, yv[...], tv[dj, di * COLS : di * COLS + width, :])
    wait(*reads)
    emit(TAPS, uv[...], lv[...])
    emit(TAPS + 1, qv[...], pv[...])
    io.finish()


def trunk_result_kernel(tasks, parts, *refs):
    outs = refs[:-1]
    quarter = parts[0].shape[1] // (TAPS * len(outs))
    for k in range(4):
        ref = parts[k]
        there = pl.ds(pl.multiple_of(tasks[k] * quarter, quarter), quarter)
        for layer, out in enumerate(outs):
            for t in range(TAPS):
                start = (layer * TAPS + t) * quarter
                out[t, :, there] = ref[:, start : start + quarter].astype(F32)


def branch_result_kernel(tasks, norm_tasks, parts, norms, out, in_out, mask_out, gains, biases, sems):
    channels = in_out.shape[2]
    for k in range(4):
        ref = parts[k]
        task = tasks[k]

        @pl.when(task < TASKS)
        def _():
            for t in range(TAPS + 2):
                block = ref[:, t * channels : (t + 1) * channels].astype(F32)
                if t < TAPS:
                    out[task, t] = block
                elif t == TAPS:
                    in_out[task] = block
                else:
                    mask_out[task] = block

        @pl.when(norm_tasks[k] < TASKS)
        def _():
            for i in range(3):
                sums = norms[k][i]
                gains[norm_tasks[k], i : i + 1, :] = sums[2:3] + sums[3:4]
                biases[norm_tasks[k], i : i + 1, :] = sums[0:1] + sums[1:2]


VMEM = pl.BlockSpec(memory_space=pltpu.VMEM)
SPARE = 6 * MIB


class Near:
    def __init__(self, value):
        self.value = value


def bytes_of(a):
    return math.prod(a.shape) * jnp.dtype(a.dtype).itemsize


def run(kernel, ins, outs, scratch, flops=0, copies=64, near=False, deps=(), aliases=None):
    flat, specs, groups, resident = [], [], [], 0
    for item in ins:
        parts = list(item) if isinstance(item, (list, tuple)) else [item]
        groups.append(len(parts) if isinstance(item, (list, tuple)) else 0)
        for part in parts:
            kept = near or isinstance(part, Near)
            part = part.value if isinstance(part, Near) else part
            if part.ndim == 1:
                specs.append(SMEM)
            elif kept:
                specs.append(VMEM)
                resident += bytes_of(part)
                if not near:
                    part = pltpu.with_memory_space_constraint(part, pltpu.VMEM)
            else:
                specs.append(HBM)
                part = pltpu.with_memory_space_constraint(part, pltpu.HBM)
            flat.append(part)
    shapes, out_specs = [], []
    for item in outs:
        kept = near or isinstance(item, Near)
        item = item.value if isinstance(item, Near) else item
        if not near:
            item = (pltpu.VMEM if kept else pltpu.HBM)(item.shape, item.dtype)
        shapes.append(item)
        out_specs.append(VMEM if kept else HBM)
        resident += bytes_of(item) if kept else 0
    resident += sum(bytes_of(b) for b in scratch)
    size = sum(bytes_of(a) for a in flat) + sum(bytes_of(o) for o in shapes)
    count = len(flat)

    def body(*refs):
        rest, args = list(refs[:count]), []
        for group in groups:
            if group:
                args.append(tuple(rest[:group]))
                rest = rest[group:]
            else:
                args.append(rest.pop(0))
        kernel(*args, *refs[count + len(deps) :])

    return pl.pallas_call(
        body,
        out_shape=shapes,
        in_specs=specs + [ANY] * len(deps),
        out_specs=out_specs,
        scratch_shapes=list(scratch) + [pltpu.SemaphoreType.DMA((copies,))],
        input_output_aliases=aliases or {},
        compiler_params=pltpu.CompilerParams(vmem_limit_bytes=resident + SPARE),
        cost_estimate=pl.CostEstimate(flops=flops, bytes_accessed=size, transcendentals=0),
    )(*flat, *deps)


def after(value, *others):
    return pl.pallas_call(
        lambda *refs: None,
        out_shape=jax.ShapeDtypeStruct(value.shape, value.dtype),
        in_specs=[HBM] + [ANY] * len(others),
        out_specs=HBM,
        input_output_aliases={0: 0},
    )(value, *others)


def swap(value, axis, mask):
    pairs = [(i, i ^ mask) for i in range(lax.axis_size(axis))]
    return lax.ppermute(value, axis, pairs)


def cross(value, second):
    tasks, width = lax.axis_size("task"), lax.axis_size("dp")
    pairs = []
    for t in range(tasks):
        for d in range(width):
            mask = 1 if (d + second) % 2 == 0 else 2
            pairs.append((t * width + d, (t ^ mask) * width + d))
    return lax.ppermute(value, ("task", "dp"), pairs)


def all_of(value, axis, unit):
    if lax.axis_size(axis) == 4 * unit:
        return [value] + [swap(value, axis, unit * k) for k in (1, 2, 3)]
    mask = unit
    while mask < lax.axis_size(axis):
        value = value + swap(value, axis, mask)
        mask *= 2
    return [value]


def total(parts):
    return (parts[0] + parts[1]) + (parts[2] + parts[3]) if len(parts) == 4 else parts[0]


def sum_parts(pay):
    return all_of(pay + swap(pay, "dp", 1), "dp", 2)


def exchange(pay):
    recv = swap(pay, "dp", 1)
    return recv, all_of(pay[COLS:] + recv[COLS:], "dp", 2)


def join(*parts):
    return jnp.concatenate(parts, axis=0)


def gather_column(part):
    return join(part, swap(part, "dp", 2), swap(part, "dp", 4), swap(part, "dp", 6))


def gather_plane(column):
    first = cross(column, 0)
    return [column, first, cross(column, 1), cross(first, 1)]


def gather_core(parts):
    return parts + [swap(part, "dp", 1) for part in parts]


def domain_counts(size_class, domain_tags):
    big_area = HEIGHT * WIDTH
    small_area = BAND * HALF_WIDTH
    ones_count = jnp.sum(
        jnp.where(
            size_class == 0, big_area * domain_tags[:, 0], small_area * jnp.sum(domain_tags, axis=1)
        )
    )
    all_count = size_class.shape[0] * big_area
    return jnp.maximum(jnp.stack([all_count - ones_count, ones_count]).astype(F32), 1.0)


def on_device(
    images,
    conv_first,
    conv_second,
    conv_third,
    trunk_gains,
    trunk_biases,
    attend_in,
    attend_mask,
    attend_out,
    branch_gains,
    branch_biases,
    size_class,
    domain_tags,
    trunk_cotangent,
    task_cotangent,
):
    rows, cols, ch = images.shape
    pixels = rows * cols
    position = lax.axis_index("dp")
    task_index = lax.axis_index("task")
    width = lax.axis_size("dp")
    task_count = lax.axis_size("task")
    quarter = ch // task_count
    own_out = ch // width
    by_permute = width == 8 and task_count == 4 and own_out == task_count * PIECE
    pair_index = position // 2
    bottom = position % 2
    local_class = lax.dynamic_slice_in_dim(size_class, pair_index * CANVAS, CANVAS, 0)
    local_tags = lax.dynamic_slice_in_dim(domain_tags, pair_index * CANVAS, CANVAS, 0)
    side = jnp.arange(GROUPS) % 2
    slot_class = jnp.repeat(local_class, 2)
    slot_tags = jnp.repeat(local_tags, 2, axis=0)
    which = jnp.where(slot_class == 1, bottom * 2 + side, 0)
    groups = jnp.sum(slot_tags * (jnp.arange(4)[None, :] == which[:, None]), axis=1)
    active = (task_index < TASKS).astype(jnp.int32)
    branch = jnp.minimum(task_index, TASKS - 1)
    info = jnp.concatenate(
        [groups, local_class, jnp.stack([bottom, task_index, active, branch, position])]
    ).astype(jnp.int32)
    cnt = domain_counts(size_class, domain_tags)

    def shape(dims, dtype=F32):
        return jax.ShapeDtypeStruct(dims, dtype)

    z_index, core = position // 2, position % 2
    masks_of = (jnp.where(core == 0, 1, 2), jnp.where(core == 0, 2, 1))
    places = []
    for side_core, (m1, m2) in ((core, masks_of), (1 - core, masks_of[::-1])):
        for t in (task_index, task_index ^ m1, task_index ^ m2, task_index ^ m1 ^ m2):
            for zz in (z_index, z_index ^ 1, z_index ^ 2, z_index ^ 3):
                places.append((2 * zz + side_core) * own_out + t * (own_out // task_count))
    place = jnp.stack(places).astype(jnp.int32)
    pieces_of_task = [task_index, task_index ^ masks_of[0], task_index ^ masks_of[1], task_index ^ 3]
    task_order = jnp.stack(pieces_of_task).astype(jnp.int32)
    norm_order = jnp.stack([task_index ^ k for k in range(4)]).astype(jnp.int32)
    spot = jnp.stack([task_index, branch]).astype(jnp.int32)

    def by_tap(kernel):
        kernel = jnp.swapaxes(kernel, -1, -2)
        tasks = kernel.shape[:1] if kernel.ndim % 2 else ()
        return kernel.reshape(tasks + (-1,) + kernel.shape[-2:])

    def cast(sources, out_rows, pick, deps=()):
        sources = [by_tap(k) for k in sources]
        taps_of = [k.shape[-3] for k in sources]
        (out,) = pl.pallas_call(
            functools.partial(cast_kernel, pick, len(sources)),
            out_shape=[shape((out_rows, sum(taps_of) * ch), BF)],
            in_specs=[SMEM] + [HBM] * len(sources) + [ANY] * len(deps),
            out_specs=[VMEM],
            scratch_shapes=[pltpu.VMEM((n, out_rows, ch), F32) for n in taps_of]
            + [pltpu.SemaphoreType.DMA((len(sources),))],
            compiler_params=pltpu.CompilerParams(vmem_limit_bytes=32 * MIB),
        )(spot, *(pltpu.with_memory_space_constraint(k, pltpu.HBM) for k in sources), *deps)
        return out

    def pick(values):
        return lax.dynamic_index_in_dim(values, branch, 0, keepdims=False)

    params = jnp.concatenate(
        [trunk_gains, pick(branch_gains), trunk_biases, pick(branch_biases), jnp.zeros((4, ch), F32)]
    )
    flat = images.reshape(pixels, ch)
    edge = jnp.where(bottom == 1, flat[:COLS], flat[pixels - COLS :])
    gather = functools.partial(lax.all_gather, axis_name="dp", axis=0, tiled=True)
    halo = swap(edge, "dp", 1)
    early = [params, halo]
    later = []
    if by_permute:
        column_1 = gather_column(cast([conv_first], PIECE, True))
        plane_1 = gather_plane(column_1)
        weights_1 = gather_core(plane_1)
        weights_2 = [gather(cast([conv_second], own_out, False, [column_1]))]
        later = plane_1[1:3]
        column_3 = gather_column(cast([conv_third], PIECE, True, later))
        first, second = cross(column_3, 0), cross(column_3, 1)
        plane_3 = [column_3, first, second, cross(first, 1)]
        weights_3 = gather_core(plane_3)
        early.append(column_3)
    else:
        weights_1, weights_2, weights_3 = [
            [gather(cast([k], own_out, False))] for k in (conv_first, conv_second, conv_third)
        ]
        plane_3 = []
    weights = [weights_1, weights_2, weights_3]
    cast_pair = cast([attend_in, attend_mask], own_out, False, later)
    cast_out = cast([attend_out], own_out, False, later)
    w_pair = gather(cast_pair)
    w_out = gather(cast_out)
    early += [cast_pair, cast_out]

    wide = shape((pixels, ch))
    low_wide = shape((pixels, ch), BF)
    pay_shape = shape((COLS + 8, ch))
    sums_shape = shape((8, ch))
    taps_dims = (3, pixels + 2 * COLS, ch)
    v_params = pltpu.VMEM((16, ch), F32)
    v_wide = pltpu.VMEM((pixels, ch), F32)
    v_low = pltpu.VMEM((pixels, ch), BF)
    v_pay = pltpu.VMEM((COLS + 8, ch), F32)
    v_sums = pltpu.VMEM((8, ch), F32)
    v_four = pltpu.VMEM((4, 8, ch), F32)
    v_pool = pltpu.VMEM((pixels // 4, ch), BF)
    v_conv = pltpu.VMEM((ch, TAPS * ch), BF)
    v_dot = pltpu.VMEM((ch, ch), BF)
    v_quarter = pltpu.VMEM((3, pixels + 2 * COLS, quarter), BF)
    taps = pltpu.VMEM(taps_dims, BF)
    masks = pltpu.VMEM((2, COLS, 128), F32)
    acc = pltpu.VMEM((2, GROUPS, 8, ch), F32)
    buf = pltpu.VMEM((ch // 128, COLS, 128), F32)

    def coefs(blocks):
        return pltpu.VMEM((4 * blocks, ch), F32)

    conv_flops = 2 * TAPS * pixels * ch * ch
    dot_flops = 2 * pixels * ch * ch

    quarter_shape = shape((3, pixels + 2 * COLS, quarter), BF)
    z, recv, stats, quarters = [], [], [], []
    outs = [wide, Near(wide), pay_shape, quarter_shape]
    near = None
    for layer in range(3):
        if layer == 0:
            values, near, pay, part = run(
                functools.partial(first_conv_kernel, rows),
                [info, place, flat, halo, weights_1],
                outs, [v_low, pltpu.VMEM((COLS, ch), BF), v_pay, v_conv, taps, masks, acc], conv_flops,
                deps=early,
            )
        else:
            values, near, pay, part = run(
                functools.partial(conv_kernel, rows, layer - 1),
                [info, cnt, place, params, Near(near), recv[-1], stats[-1], weights[layer]],
                outs, [v_params, v_pay, v_four, v_pay, v_conv, taps, masks, acc, coefs(4)], conv_flops,
                deps=plane_3 if layer == 1 else (),
            )
        got, found = exchange(pay)
        z.append(values)
        recv.append(got)
        stats.append(found)
        quarters.append(part)

    low, trunk_pool, u, near, pay = run(
        functools.partial(enter_kernel, rows, 2),
        [info, cnt, params, Near(near), recv[2], stats[2], w_pair],
        [shape((pixels + COLS, ch), BF), shape((pixels // 4, ch), BF), wide, Near(wide), sums_shape],
        [v_params, v_pay, v_four, v_dot, pltpu.VMEM((pixels + COLS, ch), BF), v_pool, v_sums, acc,
         coefs(4), buf], dot_flops,
    )
    u_stats = sum_parts(pay)
    p, q, near, pay = run(
        functools.partial(mask_kernel, rows, 3),
        [info, cnt, params, Near(near), u_stats, w_pair],
        [low_wide, wide, Near(wide), pay_shape],
        [v_params, v_four, v_dot, v_low, v_pay, acc, coefs(4)], dot_flops,
    )
    q_recv, q_stats = exchange(pay)
    y, near, pay, masked_taps = run(
        functools.partial(branch_conv_kernel, rows, 4),
        [info, cnt, params, low, Near(near), q_recv, q_stats, w_out],
        [wide, Near(wide), pay_shape, shape(taps_dims, BF)],
        [v_params, pltpu.VMEM((pixels + COLS, ch), BF), v_pay, v_four, v_pay, v_conv, taps, masks, acc,
         coefs(4)], conv_flops,
    )
    y_recv, y_stats = exchange(pay)

    branch_pool, near, pay = run(
        functools.partial(turn_kernel, rows, 5),
        [info, cnt, params, Near(near), y_stats, task_cotangent.reshape(TASKS, pixels // 4, ch)],
        [shape((pixels // 4, ch), BF), Near(wide), pay_shape],
        [v_params, v_four, v_pool, v_pool, v_pay, acc, coefs(4), buf],
    )
    task_features = lax.all_gather(branch_pool, "task")
    gy_recv, y_sums = exchange(pay)
    e_y, near, gs, pay = run(
        functools.partial(branch_back_kernel, rows),
        [info, cnt, params, Near(near), y, gy_recv, y_recv, y_stats, y_sums, w_out, low, q, q_stats],
        [low_wide, Near(wide), wide, sums_shape],
        [v_params, v_wide, v_pay, v_pay, v_four, v_four, v_four, v_low, v_wide, v_low, v_sums, v_conv,
         taps, masks, acc, coefs(10)], conv_flops,
    )
    q_sums = sum_parts(pay)
    e_q, near, pay = run(
        functools.partial(mask_back_kernel, rows),
        [info, cnt, params, Near(near), q, q_stats, q_sums, w_pair, u, u_stats],
        [low_wide, Near(wide), sums_shape],
        [v_params, v_wide, v_wide, v_four, v_four, v_four, v_dot, v_low, v_sums, acc, coefs(10)], dot_flops,
    )
    u_sums = sum_parts(pay)
    e_u, grad_shared, pay = run(
        functools.partial(leave_kernel, rows),
        [info, cnt, params, Near(near), u, u_stats, u_sums, w_pair, gs, z[2], stats[2],
         trunk_cotangent.reshape(pixels // 4, ch)],
        [low_wide, low_wide, sums_shape],
        [v_params, v_wide, v_wide, v_four, v_four, v_four, v_dot, v_wide, v_wide, v_pool, v_low, v_low, v_sums, acc,
         coefs(10), buf], dot_flops, deps=[task_features],
    )
    sums = all_of(total(sum_parts(pay)), "task", 1)
    grad_half = grad_shared + after(cross(grad_shared, 0), *sums)
    grad_rest = cross(grad_half, 1)
    (branch_part,) = run(
        functools.partial(branch_wgrad_kernel, rows),
        [masked_taps, e_y, p, e_q, low, e_u],
        [shape((ch, 11 * ch), BF)],
        [taps, v_low, v_low, v_low, v_low, v_low, pltpu.VMEM((ch, 11 * ch), BF)], conv_flops, deps=[grad_half],
    )
    branch_part = after(branch_part, grad_rest)
    branch_part = lax.psum_scatter(branch_part, "dp", scatter_dimension=0, tiled=True)

    edge = jnp.where(
        bottom == 1, grad_half[:COLS] + grad_rest[:COLS], grad_half[-COLS:] + grad_rest[-COLS:]
    )
    g, g_recv = [grad_half, grad_rest], swap(edge, "dp", 1)
    parts = [None, None, None]
    trunk_sums = [None, None, None]
    for layer in (2, 1):
        trunk_sums[layer] = sums
        top = layer == 2
        e, near, pay = run(
            functools.partial(trunk_back_kernel, rows, layer, top),
            [info, cnt, place, params, g, z[layer], g_recv, recv[layer], stats[layer], sums, z[layer - 1],
             stats[layer - 1], weights[layer]],
            [low_wide, Near(wide), pay_shape],
            [v_params, v_wide, pltpu.VMEM((COLS, ch), BF) if top else v_pay, v_pay, v_four, v_four, v_wide, v_four,
             v_low, v_pay, v_conv, taps, masks, coefs(10), acc] + ([v_low, v_low] if top else []), conv_flops,
            deps=parts[2:] if layer == 1 else (),
        )
        (part,) = run(
            functools.partial(trunk_wgrad_kernel, rows),
            [quarters[layer], e], [shape((ch, TAPS * quarter), BF)],
            [v_quarter, v_low, pltpu.VMEM((ch, TAPS * quarter), BF)], conv_flops // 4,
        )
        parts[layer] = part
        g_recv, sums = exchange(pay)
        g = Near(near)
    later_part = lax.psum_scatter(
        jnp.concatenate(parts[1:], axis=1), "dp", scatter_dimension=0, tiled=True
    )
    branch_first, branch_second = cross(branch_part, 0), cross(branch_part, 1)
    branch_third = cross(branch_first, 1)
    trunk_sums[0] = sums
    half_out = shape((ch // 2, TAPS * quarter), BF)
    last_kernel = functools.partial(last_grad_kernel, rows)
    if not by_permute:
        last_kernel = functools.partial(whole_last_grad_kernel, rows)
    e, *halves = run(
        last_kernel,
        [info, place, cnt, params, g, z[0], g_recv, recv[0], stats[0], sums, quarters[0]],
        [shape((pixels + 2 * COLS, ch), BF)]
        + ([half_out, half_out] if by_permute else [shape((ch, TAPS * quarter), BF)]),
        [v_params, v_wide, v_pay, v_pay, v_four, v_four, v_quarter, pltpu.VMEM((pixels + 2 * COLS, ch), BF),
         pltpu.VMEM((ch, TAPS * quarter), BF), coefs(10)], conv_flops // 4,
        deps=[parts[1], branch_first, branch_second],
    )

    def input_grad(m, before, deps):
        tile = TILE_ROWS * COLS
        ins = [info, place, e, weights[0]] + before
        (out,) = run(
            functools.partial(last_conv_kernel, m), ins, [wide],
            [pltpu.VMEM((tile + 2 * COLS, ch), BF), pltpu.VMEM((tile, ch), F32), v_conv,
             pltpu.VMEM((3, tile + 2 * COLS, ch), BF), masks], conv_flops // 3, deps=deps,
            aliases={2 + len(weights[0]) + 1: 0} if before else None,
        )
        return [out]

    def plane(part, *others):
        first, second = cross(part, 0), cross(part, 1)
        return [part, first, second, cross(after(first, *others) if others else first, 1)]

    tiles = rows // TILE_ROWS
    norm_sums = jnp.stack([total(s)[:4] for s in (u_sums, q_sums, y_sums)])
    if by_permute:
        mine, other = halves
        half = mine.shape[0] // 2
        got = swap(other, "dp", 1)
        images_grad = input_grad(0, [], [got])
        send, keep = mine[half:] + got[half:], mine[:half] + got[:half]
        got = swap(send, "dp", 2)
        images_grad = input_grad(1, images_grad, [got])
        later_parts = plane(after(later_part, got))
        half = half // 2
        send, keep = keep[half:] + got[half:], keep[:half] + got[:half]
        norm_sums = after(norm_sums, got)
        got = after(swap(send, "dp", 4), *images_grad)
        first_part = keep + got
        for m in range(2, tiles):
            images_grad = input_grad(m, images_grad, [first_part])
        first_parts = plane(first_part, *images_grad)
        result_deps = [first_parts[1]]
    else:
        first_part = lax.psum_scatter(halves[0], "dp", scatter_dimension=0, tiled=True)
        images_grad, result_deps = [], []
        for m in range(tiles):
            images_grad = input_grad(m, images_grad, [])
        first_parts, later_parts = plane(first_part), plane(later_part)
    (images_grad,) = images_grad
    out_grad, in_grad, mask_grad, branch_gains_grad, branch_biases_grad = run(
        branch_result_kernel,
        [task_order, norm_order, [branch_part, branch_first, branch_second, branch_third],
         [norm_sums] + [swap(norm_sums, "task", k) for k in (1, 2, 3)]],
        [shape((TASKS, TAPS, own_out, ch)), shape((TASKS, own_out, ch)), shape((TASKS, own_out, ch)),
         shape((TASKS, 3, ch)), shape((TASKS, 3, ch))],
        [], near=True, deps=result_deps,
    )
    grad_shape = shape((TAPS, own_out, ch))
    later_grads = run(
        trunk_result_kernel, [task_order, later_parts], [grad_shape] * 2, [], near=True, deps=result_deps
    )
    (first_grad,) = run(trunk_result_kernel, [task_order, first_parts], [grad_shape], [], near=True)
    kernel_grads = [
        jnp.swapaxes(k.reshape(3, 3, own_out, ch), 2, 3) for k in (first_grad, *later_grads)
    ]
    trunk_sums = jnp.stack([total(s)[:4] for s in trunk_sums])
    return (
        trunk_pool.reshape(rows // 2, cols // 2, ch),
        task_features[:TASKS].reshape(TASKS, rows // 2, cols // 2, ch),
        images_grad.reshape(rows, cols, ch),
        *kernel_grads,
        trunk_sums[:, 2] + trunk_sums[:, 3],
        trunk_sums[:, 0] + trunk_sums[:, 1],
        jnp.swapaxes(in_grad, 1, 2),
        jnp.swapaxes(mask_grad, 1, 2),
        jnp.swapaxes(out_grad.reshape(TASKS, 3, 3, own_out, ch), 3, 4),
        branch_gains_grad,
        branch_biases_grad,
    )


def solution(mesh):
    in_specs = (
        P("dp", None, None),
        P(None, None, None, "dp"),
        P(None, None, None, "dp"),
        P(None, None, None, "dp"),
        P(),
        P(),
        P(None, None, "dp"),
        P(None, None, "dp"),
        P(None, None, None, None, "dp"),
        P(),
        P(),
        P(),
        P(),
        P("dp", None, None),
        P(None, "dp", None, None),
    )
    out_specs = (
        P("dp", None, None),
        P(None, "dp", None, None),
        P("dp", None, None),
        P(None, None, None, "dp"),
        P(None, None, None, "dp"),
        P(None, None, None, "dp"),
        P(),
        P(),
        P(None, None, "dp"),
        P(None, None, "dp"),
        P(None, None, None, None, "dp"),
        P(),
        P(),
    )
    return jax.shard_map(
        on_device, mesh=mesh, in_specs=in_specs, out_specs=out_specs, check_vma=False
    )
```

time: 718 us -> 537 us (0.75)
  waiting for transfers between devices: 281 us -> 132 us
  local copies, waits for them, and re-layouts: 141 us -> 25.9 us
  starting transfers between devices: 24.8 us -> 106 us
  blocking collectives: 74.9 us -> 0 us
  Pallas kernels: 156 us -> 227 us
    all_gather x6 -> x4, waiting for transfers between devices: 103 us -> 0.01 us  [the longest x1 0.01 us: on_device(): weights_2 = [gather(cast([conv_second], own_out, False, [column_1]))]]
    all_gather x6 -> x0, blocking collectives: 74.9 us -> none  [the longest x4 41 us: collect(): return lax.all_gather(values, 'task', axis=0, tiled=False)]
    pallas_call x17 -> x33, Pallas kernels: 156 us -> 227 us  [the longest x22 217 us: run(): pl.pallas_call(body, out_shape=shapes, in_specs=specs + [ANY] * len(deps)...]
    unnamed x272 -> x215, local copies, waits for them, and re-layouts: 94.4 us -> 23.5 us
    ppermute x40 -> x73, starting transfers between devices: 23.7 us -> 87 us  [swap(): return lax.ppermute(value, axis, pairs)]
    reduce_scatter x4 -> x2, waiting for transfers between devices: 40.5 us -> 0.02 us  [the longest x1 0.02 us: on_device(): lax.psum_scatter(branch_part, 'dp', scatter_dimension=0, tiled=True)]
    psum x1 -> x0, waiting for transfers between devices: 39.5 us -> none  [on_device(): grad_shared = lax.psum(grad_shared, 'task')]
    ppermute x0 -> x17, waiting for transfers between devices: none -> 35.5 us  [cross(): return lax.ppermute(value, ('task', 'dp'), pairs)]
  transfers between devices with their start and end apart: 51 -> 96, of which waited for: 42 -> 48; matrix products, arithmetic and copies ran while one was open for 6% -> 4% of each run, Pallas kernels for 16% -> 36%
where the time goes in v2:
time: 537 us; the launch traced here: 529 us
  Pallas kernels  227 us (42%)
  waiting for transfers between devices  132 us (25%)
  starting transfers between devices  106 us (20%)
  local copies, waits for them, and re-layouts  25.9 us (5%)
  other arithmetic  21.6 us (4%)
  between operations  16.3 us (3%)
    pallas_call x22, Pallas kernels, run(): pl.pallas_call(body, out_shape=shapes, in_specs=specs + [ANY] * len(deps)...  217 us
    ppermute x73, waiting for transfers between devices, swap(): return lax.ppermute(value, axis, pairs)  96.1 us
    ppermute x73, starting transfers between devices, swap(): return lax.ppermute(value, axis, pairs)  87 us
    ppermute x17, waiting for transfers between devices, cross(): return lax.ppermute(value, ('task', 'dp'), pairs)  35.5 us
    unnamed x215, local copies, waits for them, and re-layouts  23.5 us
    ppermute x17, starting transfers between devices, cross(): return lax.ppermute(value, ('task', 'dp'), pairs)  18.3 us
  transfers between devices with their start and end apart: 96, of which 48 were waited for; matrix products, arithmetic and copies ran while one was open for 4% of the time, Pallas kernels for 36%

profile of v2, /device:TPU:0, one launch (start us, length us, event | category | flops | bytes accessed | tf_op | source)
XLA Modules:
  0.0 528.5 jit_solution(4458802678677071576)
XLA Ops:
  8.8 3.1 collective-permute-start.1
  11.9 2.6 collective-permute-start.2
  14.5 3.3 collective-permute-done.1
  17.8 8.1 %collective-permute-done.2 = bf16[16,4608]{1,0:T(8,128)(2,1)S(1)} collective-permute-done((bf16[16,4608]{1,0:T(8,128)(2,1)S(1)}, bf16[16,4608]{1,0:T(8,128)(2,1)S(1)}, u32[]{:S(2)}, u32[]{:S(2)}) %collective-permute-start.2) | collective-permute-done | bytes 147488 | tf_op jit(solution)/shard_map/ppermute | solution.py:914
  26.0 2.7 shard_map.251
  31.8 10.8 %collective-permute-done.4.refs_1_.refs_2_.refs_5_.refs_4_ = bf16[64,4608]{1,0:T(8,128)(2,1)S(1)} collective-permute-done((bf16[64,4608]{1,0:T(8,128)(2,1)S(1)}, bf16[64,4608]{1,0:T(8,128)(2,1)S(1)}, u32[]{:S(2)}, u32[]{:S(2)}) %collective-permute-start.4) | collective-permute-done | bytes 589856 | tf_op jit(solution)/shard_map/ppermute | solution.py:924
  42.7 2.2 shard_map.248.refs_15_
  45.0 2.7 shard_map.249.refs_16_
  49.4 3.6 collective-permute-start.11
  57.3 10.1 %collective-permute-done.11 = bf16[16,4608]{1,0:T(8,128)(2,1)S(1)} collective-permute-done((bf16[16,4608]{1,0:T(8,128)(2,1)S(1)}, bf16[16,4608]{1,0:T(8,128)(2,1)S(1)}, u32[]{:S(2)}, u32[]{:S(2)}) %collective-permute-start.11) | collective-permute-done | bytes 147488 | tf_op jit(solution)/shard_map/ppermute | solution.py:914
  67.4 4.0 collective-permute-done.12
  71.4 4.2 collective-permute-done.13
  79.8 9.3 %collective-permute-done.18.refs_12_.refs_11_.refs_23_ = bf16[64,4608]{1,0:T(8,128)(2,1)S(1)} collective-permute-done((bf16[64,4608]{1,0:T(8,128)(2,1)S(1)}, bf16[64,4608]{1,0:T(8,128)(2,1)S(1)}, u32[]{:S(2)}, u32[]{:S(2)}) %collective-permute-start.18) | collective-permute-done | bytes 589856 | tf_op jit(solution)/shard_map/ppermute | solution.py:924
  89.2 13.6 %shard_map.250 = (f32[1728,512]{1,0:T(8,128)}, f32[1728,512]{1,0:T(8,128)S(1)}, f32[104,512]{1,0:T(8,128)}, bf16[3,1920,128]{2,1,0:T(8,128)(2,1)}) custom-call(s32[11]{0:T(128)S(1)} %concatenate.15.refs_0_, s32[32]{0:T(128)S(1)} %stack.220.refs_1_.refs_2_, bf16[1728,512]{1,0:T(8,128)(2,1)} %bitcast.121, bf16[96,512]{1,0:T(8,128)(2,1)} %copy-done.101, ...), custom_call_target="tpu_custom_call" | custom-call | flops 8153726976 | bytes 15351980 | tf_op jit(solution)/shard_map/pallas_call | solution.py:890
  107.5 10.8 %collective-permute-start.15 = (f32[8,512]{1,0:T(8,128)S(1)}, f32[8,512]{1,0:T(8,128)S(1)}, u32[]{:S(2)}, u32[]{:S(2)}) collective-permute-start(f32[8,512]{1,0:T(8,128)S(1)} %slice_add_fusion.13.refs_6_.refs_17_.refs_8_), channel_id=1, source_target_pairs={{0,2},{1,3},{2,0},{3,1},{4,6},{5,7},{6,4},{7,5},{8,10},{9,11},{10,... | collective-permute-start | bytes 49160 | tf_op jit(solution)/shard_map/ppermute | solution.py:914
  123.7 2.3 collective-permute-done.17.refs_9_.refs_20_.refs_11_
  126.6 2.4 copy-done.21
  129.0 13.7 %shard_map.252 = (f32[1728,512]{1,0:T(8,128)}, f32[1728,512]{1,0:T(8,128)S(1)}, f32[104,512]{1,0:T(8,128)}, bf16[3,1920,128]{2,1,0:T(8,128)(2,1)}) custom-call(s32[11]{0:T(128)S(1)} %concatenate.15.refs_0_, f32[2]{0:T(128)S(1)} %fusion.18.refs_1_.refs_2_, s32[32]{0:T(128)S(1)} %stack.220.refs_1_.refs_2_, f32[16,512]{1,0:T(8,128)} %copy-done.12, ...), custom_call_target="tpu_custom_call" | custom-call | flops 8153726976 | bytes 17334452 | tf_op jit(solution)/shard_map/pallas_call | solution.py:890
  147.1 2.5 collective-permute-start.24
  150.5 2.4 collective-permute-done.24.refs_9_.refs_21_.refs_11_
  153.5 13.5 %shard_map.253 = (f32[1728,512]{1,0:T(8,128)}, f32[1728,512]{1,0:T(8,128)S(1)}, f32[104,512]{1,0:T(8,128)}, bf16[3,1920,128]{2,1,0:T(8,128)(2,1)}) custom-call(s32[11]{0:T(128)S(1)} %concatenate.15.refs_0_, f32[2]{0:T(128)S(1)} %fusion.18.refs_1_.refs_2_, s32[32]{0:T(128)S(1)} %stack.220.refs_1_.refs_2_, f32[16,512]{1,0:T(8,128)} %copy-done.12, ...), custom_call_target="tpu_custom_call" | custom-call | flops 8153726976 | bytes 17334452 | tf_op jit(solution)/shard_map/pallas_call | solution.py:890
  171.6 2.4 collective-permute-start.31
  176.5 3.3 collective-permute-done.32.refs_8_.refs_19_.refs_12_
  179.8 7.2 %shard_map.254 = (bf16[1824,512]{1,0:T(8,128)(2,1)}, bf16[432,512]{1,0:T(8,128)(2,1)}, f32[1728,512]{1,0:T(8,128)}, f32[1728,512]{1,0:T(8,128)S(1)}, f32[8,512]{1,0:T(8,128)}) custom-call(s32[11]{0:T(128)S(1)} %concatenate.15.refs_0_, f32[2]{0:T(128)S(1)} %fusion.18.refs_1_.refs_2_, f32[16,512]{1,0:T(8,128)} %copy-done.12, ...), custom_call_target="tpu_custom_call" | custom-call | flops 905969664 | bytes 14303284 | tf_op jit(solution)/shard_map/pallas_call | solution.py:890
  191.0 2.6 collective-permute-start.36
  193.9 2.6 collective-permute-done.36.refs_7_.refs_18_.refs_8_
  197.1 5.7 %shard_map.255 = (bf16[1728,512]{1,0:T(8,128)(2,1)}, f32[1728,512]{1,0:T(8,128)}, f32[1728,512]{1,0:T(8,128)S(1)}, f32[104,512]{1,0:T(8,128)}) custom-call(s32[11]{0:T(128)S(1)} %concatenate.15.refs_0_, f32[2]{0:T(128)S(1)} %fusion.18.refs_1_.refs_2_, f32[16,512]{1,0:T(8,128)} %copy-done.12, f32[1728,512]{1,0:T(8,128)S(1)} %get-tuple-element.75.refs_3_, ...), custom_call_target="tpu_custom_call" | custom-call | flops 905969664 | bytes 13746228 | tf_op jit(solution)/shard_map/pallas_call | solution.py:890
  206.5 3.2 collective-permute-start.39
  212.0 3.6 collective-permute-done.40.refs_9_.refs_21_.refs_8_
  215.6 14.3 %shard_map.256 = (f32[1728,512]{1,0:T(8,128)}, f32[1728,512]{1,0:T(8,128)S(1)}, f32[104,512]{1,0:T(8,128)}, bf16[3,1920,512]{2,1,0:T(8,128)(2,1)}) custom-call(s32[11]{0:T(128)S(1)} %concatenate.15.refs_0_, f32[2]{0:T(128)S(1)} %fusion.18.refs_1_.refs_2_, f32[16,512]{1,0:T(8,128)} %copy-done.12, ...), custom_call_target="tpu_custom_call" | custom-call | flops 8153726976 | bytes 23625780 | tf_op jit(solution)/shard_map/pallas_call | solution.py:890
  234.1 2.6 collective-permute-start.44
  237.0 2.6 collective-permute-done.44.refs_7_.refs_10_
  240.3 5.9 %shard_map.257 = (bf16[432,512]{1,0:T(8,128)(2,1)}, f32[1728,512]{1,0:T(8,128)S(1)}, f32[104,512]{1,0:T(8,128)}) custom-call(s32[11]{0:T(128)S(1)} %concatenate.15.refs_0_, f32[2]{0:T(128)S(1)} %fusion.18.refs_1_.refs_2_, f32[16,512]{1,0:T(8,128)} %copy-done.12, f32[1728,512]{1,0:T(8,128)S(1)} %get-tuple-element.79.refs_3_, f32[8,512]{1,0:T(8,128)} %copy-done.43, ...), custom_call_target="tpu_custom_call" | custom-call | bytes 9158708 | tf_op jit(solution)/shard_map/pallas_call | solution.py:890
  248.7 3.2 collective-permute-start.47
  253.6 3.8 collective-permute-done.48.refs_14_
  258.0 18.8 %shard_map.258 = (bf16[1728,512]{1,0:T(8,128)(2,1)}, f32[1728,512]{1,0:T(8,128)S(1)}, f32[1728,512]{1,0:T(8,128)}, f32[8,512]{1,0:T(8,128)}) custom-call(s32[11]{0:T(128)S(1)} %concatenate.15.refs_0_, f32[2]{0:T(128)S(1)} %fusion.18.refs_1_.refs_2_, f32[16,512]{1,0:T(8,128)} %copy-done.12, f32[1728,512]{1,0:T(8,128)S(1)} %get-tuple-element.82.refs_3_, ...), custom_call_target="tpu_custom_call" | custom-call | flops 8153726976 | bytes 26722356 | tf_op jit(solution)/shard_map/pallas_call | solution.py:890
  280.7 2.6 collective-permute-start.52
  283.7 2.6 collective-permute-done.52.refs_12_
  286.9 7.9 %shard_map.259 = (bf16[1728,512]{1,0:T(8,128)(2,1)}, f32[1728,512]{1,0:T(8,128)S(1)}, f32[8,512]{1,0:T(8,128)}) custom-call(s32[11]{0:T(128)S(1)} %concatenate.15.refs_0_, f32[2]{0:T(128)S(1)} %fusion.18.refs_1_.refs_2_, f32[16,512]{1,0:T(8,128)} %copy-done.12, f32[1728,512]{1,0:T(8,128)S(1)} %get-tuple-element.86.refs_3_, ...), custom_call_target="tpu_custom_call" | custom-call | flops 905969664 | bytes 17219636 | tf_op jit(solution)/shard_map/pallas_call | solution.py:890
  297.0 3.2 collective-permute-start.55
  302.6 3.2 collective-permute-done.56.refs_12_
  307.3 11.3 %shard_map.260 = (bf16[1728,512]{1,0:T(8,128)(2,1)}, bf16[1728,512]{1,0:T(8,128)(2,1)}, f32[8,512]{1,0:T(8,128)}) custom-call(s32[11]{0:T(128)S(1)} %concatenate.15.refs_0_, f32[2]{0:T(128)S(1)} %fusion.18.refs_1_.refs_2_, f32[16,512]{1,0:T(8,128)} %copy-done.12, f32[1728,512]{1,0:T(8,128)S(1)} %get-tuple-element.89.refs_3_, ...), custom_call_target="tpu_custom_call" | custom-call | flops 905969664 | bytes 19431476 | tf_op jit(solution)/shard_map/pallas_call | solution.py:890
  324.7 2.4 collective-permute-start.61
  327.3 2.9 collective-permute-done.61
  333.8 8.2 %collective-permute-done.62.refs_2_.refs_14_ = f32[8,512]{1,0:T(8,128)S(1)} collective-permute-done((f32[8,512]{1,0:T(8,128)S(1)}, f32[8,512]{1,0:T(8,128)S(1)}, u32[]{:S(2)}, u32[]{:S(2)}) %collective-permute-start.62) | collective-permute-done | bytes 16416 | tf_op jit(solution)/shard_map/ppermute | solution.py:914
  345.1 2.5 add.378.refs_4_.refs_6_
  348.1 14.9 %shard_map.266.refs_0_ = bf16[512,5632]{1,0:T(8,128)(2,1)} custom-call(bf16[3,1920,512]{2,1,0:T(8,128)(2,1)} %get-tuple-element.106.refs_0_, bf16[1728,512]{1,0:T(8,128)(2,1)} %get-tuple-element.107.refs_1_, bf16[1728,512]{1,0:T(8,128)(2,1)} %get-tuple-element.108.refs_2_, bf16[1728,512]{1,0:T(8,128)(2,1)} %get-tuple-element.109.refs_3_, ...), custom_call_target="tpu_custom_call" | custom-call | flops 8153726976 | bytes 20611072 | tf_op jit(solution)/shard_map/pallas_call | solution.py:890
  363.0 7.2 %collective-permute-done.65.refs_5_.refs_1_ = bf16[1728,512]{1,0:T(8,128)(2,1)S(1)} collective-permute-done((bf16[1728,512]{1,0:T(8,128)(2,1)S(1)}, bf16[1728,512]{1,0:T(8,128)(2,1)S(1)}, u32[]{:S(2)}, u32[]{:S(2)}) %collective-permute-start.65) | collective-permute-done | bytes 1769504 | tf_op jit(solution)/shard_map/ppermute | solution.py:924
  374.5 19.7 %shard_map.262 = (bf16[1728,512]{1,0:T(8,128)(2,1)}, f32[1728,512]{1,0:T(8,128)S(1)}, f32[104,512]{1,0:T(8,128)}) custom-call(s32[11]{0:T(128)S(1)} %concatenate.15.refs_0_, f32[2]{0:T(128)S(1)} %fusion.18.refs_1_.refs_2_, s32[32]{0:T(128)S(1)} %stack.220.refs_1_.refs_2_, f32[16,512]{1,0:T(8,128)} %copy-done.12, bf16[1728,512]{1,0:T(8,128)(2,1)} %copy-done.11, ...), custom_call_target="tpu_custom_call" | custom-call | flops 8153726976 | bytes 21397684 | tf_op jit(solution)/shard_map/pallas_call | solution.py:890
  398.2 2.8 collective-permute-start.70
  401.1 6.1 %shard_map.263.refs_22_ = bf16[512,1152]{1,0:T(8,128)(2,1)} custom-call(bf16[3,1920,128]{2,1,0:T(8,128)(2,1)} %get-tuple-element.99.refs_0_, bf16[1728,512]{1,0:T(8,128)(2,1)} %get-tuple-element.100.refs_1_), custom_call_target="tpu_custom_call" | custom-call | flops 2038431744 | bytes 4423680 | tf_op jit(solution)/shard_map/pallas_call | solution.py:890
  409.1 17.2 %shard_map.264 = (bf16[1728,512]{1,0:T(8,128)(2,1)}, f32[1728,512]{1,0:T(8,128)S(1)}, f32[104,512]{1,0:T(8,128)}) custom-call(s32[11]{0:T(128)S(1)} %concatenate.15.refs_0_, f32[2]{0:T(128)S(1)} %fusion.18.refs_1_.refs_2_, s32[32]{0:T(128)S(1)} %stack.220.refs_1_.refs_2_, f32[16,512]{1,0:T(8,128)} %copy-done.12, f32[1728,512]{1,0:T(8,128)S(1)} %get-tuple-element.96.refs_4_, ...), custom_call_target="tpu_custom_call" | custom-call | flops 8153726976 | bytes 21512372 | tf_op jit(solution)/shard_map/pallas_call | solution.py:890
  426.3 7.4 %shard_map.265.refs_17_ = bf16[512,1152]{1,0:T(8,128)(2,1)} custom-call(bf16[3,1920,128]{2,1,0:T(8,128)(2,1)} %get-tuple-element.104.refs_0_, bf16[1728,512]{1,0:T(8,128)(2,1)} %get-tuple-element.105.refs_1_), custom_call_target="tpu_custom_call" | custom-call | flops 2038431744 | bytes 4423680 | tf_op jit(solution)/shard_map/pallas_call | solution.py:890
  433.7 2.9 pad_maximum_fusion
  442.3 2.9 collective-permute-start.74
  445.6 2.3 collective-permute-done.74.refs_15_
  447.9 6.8 %collective-permute-done.75.refs_18_.refs_3_ = bf16[64,5632]{1,0:T(8,128)(2,1)S(1)} collective-permute-done((bf16[64,5632]{1,0:T(8,128)(2,1)}, bf16[64,5632]{1,0:T(8,128)(2,1)S(1)}, u32[]{:S(2)}, u32[]{:S(2)}) %collective-permute-start.75) | collective-permute-done | bytes 720928 | tf_op jit(solution)/shard_map/ppermute | solution.py:924
  456.8 7.5 %shard_map.268 = (bf16[1920,512]{1,0:T(8,128)(2,1)}, bf16[256,1152]{1,0:T(8,128)(2,1)}, bf16[256,1152]{1,0:T(8,128)(2,1)}) custom-call(s32[11]{0:T(128)S(1)} %concatenate.15.refs_0_, s32[32]{0:T(128)S(1)} %stack.220.refs_1_.refs_2_, f32[2]{0:T(128)S(1)} %fusion.18.refs_1_.refs_2_, f32[16,512]{1,0:T(8,128)} %copy-done.12, f32[1728,512]{1,0:T(8,128)S(1)} %copy-done.10, ...), custom_call_target="tpu_custom_call" | custom-call | flops 2038431744 | bytes 12288180 | tf_op jit(solution)/shard_map/pallas_call | solution.py:890
  469.2 7.6 %shard_map.269.refs_11_ = f32[1728,512]{1,0:T(8,128)} custom-call(s32[11]{0:T(128)S(1)} %concatenate.15.refs_0_, s32[32]{0:T(128)S(1)} %stack.220.refs_1_.refs_2_, bf16[1920,512]{1,0:T(8,128)(2,1)} %get-tuple-element.111.refs_2_, bf16[64,4608]{1,0:T(8,128)(2,1)} %copy-done.2, bf16[64,4608]{1,0:T(8,128)(2,1)} %copy-done, bf16[64,4608]{1,0:T(8,128)(2,1)} %copy-done.1, ...), custom_call_target="tpu_custom_call" | custom-call | flops 2717908992 | bytes 10223788 | tf_op jit(solution)/shard_map/pallas_call | solution.py:890
  481.2 7.5 %shard_map.270.refs_1_.refs_11_ = f32[1728,512]{1,0:T(8,128)} custom-call(s32[11]{0:T(128)S(1)} %concatenate.15.refs_0_, s32[32]{0:T(128)S(1)} %stack.220.refs_1_.refs_2_, bf16[1920,512]{1,0:T(8,128)(2,1)} %get-tuple-element.111.refs_2_, bf16[64,4608]{1,0:T(8,128)(2,1)} %copy-done.2, bf16[64,4608]{1,0:T(8,128)(2,1)} %copy-done, ...), custom_call_target="tpu_custom_call", output_to_operand_aliasing={{}: (11, {})} | custom-call | flops 2717908992 | bytes 13762732 | tf_op jit(solution)/shard_map/pallas_call | solution.py:890
  497.9 7.5 %shard_map.272.refs_1_ = f32[1728,512]{1,0:T(8,128)} custom-call(s32[11]{0:T(128)S(1)} %concatenate.15.refs_0_, s32[32]{0:T(128)S(1)} %stack.220.refs_1_.refs_2_, bf16[1920,512]{1,0:T(8,128)(2,1)} %get-tuple-element.111.refs_2_, bf16[64,4608]{1,0:T(8,128)(2,1)} %copy-done.2, bf16[64,4608]{1,0:T(8,128)(2,1)} %copy-done, ...), custom_call_target="tpu_custom_call", output_to_operand_aliasing={{}: (11, {})} | custom-call | flops 2717908992 | bytes 13762732 | tf_op jit(solution)/shard_map/pallas_call | solution.py:890
  511.9 3.7 shard_map.278
  515.7 2.3 shard_map.274
  518.0 3.4 shard_map.276
  (431 shorter events, 125.9 us)
Async XLA Ops:
  7.2 118.9 %all-gather.6.cloned.1.call-start = ((), (), s32[]{:S(2)}) async-start(), calls=%async_computation.2 | async-start | bytes 5308416 | tf_op jit(solution)/shard_map/all_gather | solution.py:1072
  8.8 8.9 %collective-permute-start.1 = (bf16[16,4608]{1,0:T(8,128)(2,1)S(1)}, bf16[16,4608]{1,0:T(8,128)(2,1)S(1)}, u32[]{:S(2)}, u32[]{:S(2)}) collective-permute-start(bf16[16,4608]{1,0:T(8,128)(2,1)S(1)} %shard_map.246), channel_id=1, source_target_pairs={{0,2},{1,3},{2,0},{3,1},{4,6},{5,7},{6,4},{7,5},{8,10},{9,11},{10,... | collective-permute-start | bytes 442376 | tf_op jit(solution)/shard_map/ppermute | solution.py:914
  11.9 14.0 %collective-permute-start.2 = (bf16[16,4608]{1,0:T(8,128)(2,1)S(1)}, bf16[16,4608]{1,0:T(8,128)(2,1)S(1)}, u32[]{:S(2)}, u32[]{:S(2)}) collective-permute-start(bf16[16,4608]{1,0:T(8,128)(2,1)S(1)} %shard_map.246), channel_id=1, source_target_pairs={{0,4},{1,5},{2,6},{3,7},{4,0},{5,1},{6,2},{7,3},{8,12},{9,13},{10,... | collective-permute-start | bytes 442376 | tf_op jit(solution)/shard_map/ppermute | solution.py:914
  14.5 11.4 %collective-permute-start.3 = (bf16[16,4608]{1,0:T(8,128)(2,1)S(1)}, bf16[16,4608]{1,0:T(8,128)(2,1)S(1)}, u32[]{:S(2)}, u32[]{:S(2)}) collective-permute-start(bf16[16,4608]{1,0:T(8,128)(2,1)S(1)} %shard_map.246), channel_id=1, source_target_pairs={{0,6},{1,7},{2,4},{3,5},{4,2},{5,3},{6,0},{7,1},{8,14},{9,15},{10,... | collective-permute-start | bytes 442376 | tf_op jit(solution)/shard_map/ppermute | solution.py:914
  28.7 146.4 %all-gather.8.cloned.1.call-start = ((), (), s32[]{:S(2)}) async-start(), calls=%async_computation.3 | async-start | bytes 1179648 | tf_op jit(solution)/shard_map/all_gather | solution.py:1087
  28.8 13.9 %collective-permute-start.4 = (bf16[64,4608]{1,0:T(8,128)(2,1)S(1)}, bf16[64,4608]{1,0:T(8,128)(2,1)S(1)}, u32[]{:S(2)}, u32[]{:S(2)}) collective-permute-start(bf16[64,4608]{1,0:T(8,128)(2,1)S(1)} %pad_maximum_fusion.1.refs_4_.refs_1_.refs_3_), channel_id=1, source_target_pairs={{0,8},{1,17},{2,10},{3,19},{4,12},{5,21},{6,14},{7,23},{8,0},{9,25... | collective-permute-start | bytes 1769480 | tf_op jit(solution)/shard_map/ppermute | solution.py:924
  30.3 12.4 %collective-permute-start.5 = (bf16[64,4608]{1,0:T(8,128)(2,1)S(1)}, bf16[64,4608]{1,0:T(8,128)(2,1)S(1)}, u32[]{:S(2)}, u32[]{:S(2)}) collective-permute-start(bf16[64,4608]{1,0:T(8,128)(2,1)S(1)} %pad_maximum_fusion.1.refs_4_.refs_1_.refs_3_), channel_id=1, source_target_pairs={{0,16},{1,9},{2,18},{3,11},{4,20},{5,13},{6,22},{7,15},{8,24},{9,1... | collective-permute-start | bytes 1769480 | tf_op jit(solution)/shard_map/ppermute | solution.py:924
  44.9 166.0 %all-gather.10.cloned.1.call-start = ((), (), s32[]{:S(2)}) async-start(), calls=%async_computation.4 | async-start | bytes 5308416 | tf_op jit(solution)/shard_map/all_gather | solution.py:1088
  47.7 258.1 %all-gather.12.cloned.1.call-start = ((), (), s32[]{:S(2)}) async-start(), calls=%async_computation.7 | async-start | bytes 2211840 | tf_op jit(solution)/shard_map/all_gather | solution.py:1172
  49.4 18.0 %collective-permute-start.11 = (bf16[16,4608]{1,0:T(8,128)(2,1)S(1)}, bf16[16,4608]{1,0:T(8,128)(2,1)S(1)}, u32[]{:S(2)}, u32[]{:S(2)}) collective-permute-start(bf16[16,4608]{1,0:T(8,128)(2,1)S(1)} %shard_map.247), channel_id=1, source_target_pairs={{0,2},{1,3},{2,0},{3,1},{4,6},{5,7},{6,4},{7,5},{8,10},{9,11},{10,... | collective-permute-start | bytes 442376 | tf_op jit(solution)/shard_map/ppermute | solution.py:914
  53.0 18.4 %collective-permute-start.12 = (bf16[16,4608]{1,0:T(8,128)(2,1)S(1)}, bf16[16,4608]{1,0:T(8,128)(2,1)S(1)}, u32[]{:S(2)}, u32[]{:S(2)}) collective-permute-start(bf16[16,4608]{1,0:T(8,128)(2,1)S(1)} %shard_map.247), channel_id=1, source_target_pairs={{0,4},{1,5},{2,6},{3,7},{4,0},{5,1},{6,2},{7,3},{8,12},{9,13},{10,... | collective-permute-start | bytes 442376 | tf_op jit(solution)/shard_map/ppermute | solution.py:914
  54.3 21.3 %collective-permute-start.13 = (bf16[16,4608]{1,0:T(8,128)(2,1)S(1)}, bf16[16,4608]{1,0:T(8,128)(2,1)S(1)}, u32[]{:S(2)}, u32[]{:S(2)}) collective-permute-start(bf16[16,4608]{1,0:T(8,128)(2,1)S(1)} %shard_map.247), channel_id=1, source_target_pairs={{0,6},{1,7},{2,4},{3,5},{4,2},{5,3},{6,0},{7,1},{8,14},{9,15},{10,... | collective-permute-start | bytes 442376 | tf_op jit(solution)/shard_map/ppermute | solution.py:914
  55.7 21.6 %collective-permute-start.6 = (bf16[64,4608]{1,0:T(8,128)(2,1)S(1)}, bf16[64,4608]{1,0:T(8,128)(2,1)}, u32[]{:S(2)}, u32[]{:S(2)}) collective-permute-start(bf16[64,4608]{1,0:T(8,128)(2,1)S(1)} %collective-permute-done.4.refs_1_.refs_2_.refs_5_.refs_4_), channel_id=1, source_target_pairs={{0,16},{1,9},{2,18},{3,11},{4,20},{5,13},{6,22},{7,15},{8,24},{9,1... | collective-permute-start | bytes 1769480 | tf_op jit(solution)/shard_map/ppermute | solution.py:924
  57.2 18.5 %collective-permute-start = (bf16[96,512]{1,0:T(8,128)(2,1)S(1)}, bf16[96,512]{1,0:T(8,128)(2,1)S(1)}, u32[]{:S(2)}, u32[]{:S(2)}) collective-permute-start(bf16[96,512]{1,0:T(8,128)(2,1)S(1)} %select_bitcast_fusion), channel_id=1, source_target_pairs={{0,1},{1,0},{2,3},{3,2},{4,5},{5,4},{6,7},{7,6},{8,9},{9,8},{10,11... | collective-permute-start | bytes 294920 | tf_op jit(solution)/shard_map/ppermute | solution.py:914
  67.4 11.6 %collective-permute-start.7 = (bf16[64,4608]{1,0:T(8,128)(2,1)S(1)}, bf16[64,4608]{1,0:T(8,128)(2,1)}, u32[]{:S(2)}, u32[]{:S(2)}) collective-permute-start(bf16[64,4608]{1,0:T(8,128)(2,1)S(1)} %pad_maximum_fusion.1.refs_4_.refs_1_.refs_3_), channel_id=1, source_target_pairs={{0,1},{1,0},{2,3},{3,2},{4,5},{5,4},{6,7},{7,6},{8,9},{9,8},{10,11... | collective-permute-start | bytes 1769480 | tf_op jit(solution)/shard_map/ppermute | solution.py:914
  71.4 17.7 %collective-permute-start.8 = (bf16[64,4608]{1,0:T(8,128)(2,1)S(1)}, bf16[64,4608]{1,0:T(8,128)(2,1)}, u32[]{:S(2)}, u32[]{:S(2)}) collective-permute-start(bf16[64,4608]{1,0:T(8,128)(2,1)S(1)} %collective-permute-done.4.refs_1_.refs_2_.refs_5_.refs_4_), channel_id=1, source_target_pairs={{0,1},{1,0},{2,3},{3,2},{4,5},{5,4},{6,7},{7,6},{8,9},{9,8},{10,11... | collective-permute-start | bytes 1769480 | tf_op jit(solution)/shard_map/ppermute | solution.py:914
  75.6 13.5 %collective-permute-start.9 = (bf16[64,4608]{1,0:T(8,128)(2,1)S(1)}, bf16[64,4608]{1,0:T(8,128)(2,1)}, u32[]{:S(2)}, u32[]{:S(2)}) collective-permute-start(bf16[64,4608]{1,0:T(8,128)(2,1)S(1)} %collective-permute-done.5.refs_2_.refs_3_.refs_6_.refs_5_), channel_id=1, source_target_pairs={{0,1},{1,0},{2,3},{3,2},{4,5},{5,4},{6,7},{7,6},{8,9},{9,8},{10,11... | collective-permute-start | bytes 1769480 | tf_op jit(solution)/shard_map/ppermute | solution.py:914
  75.7 13.4 %collective-permute-start.18 = (bf16[64,4608]{1,0:T(8,128)(2,1)S(1)}, bf16[64,4608]{1,0:T(8,128)(2,1)S(1)}, u32[]{:S(2)}, u32[]{:S(2)}) collective-permute-start(bf16[64,4608]{1,0:T(8,128)(2,1)S(1)} %pad_maximum_fusion.2.refs_14_.refs_11_.refs_10_.refs_22_), channel_id=1, source_target_pairs={{0,8},{1,17},{2,10},{3,19},{4,12},{5,21},{6,14},{7,23},{8,0},{9,25... | collective-permute-start | bytes 1769480 | tf_op jit(solution)/shard_map/ppermute | solution.py:924
  77.3 11.8 %collective-permute-start.10 = (bf16[64,4608]{1,0:T(8,128)(2,1)}, bf16[64,4608]{1,0:T(8,128)(2,1)}, u32[]{:S(2)}, u32[]{:S(2)}) collective-permute-start(bf16[64,4608]{1,0:T(8,128)(2,1)} %collective-permute-done.6.refs_7_.refs_6_), channel_id=1, source_target_pairs={{0,1},{1,0},{2,3},{3,2},{4,5},{5,4},{6,7},{7,6},{8,9},{9,8},{10,11... | collective-permute-start | bytes 1769480 | tf_op jit(solution)/shard_map/ppermute | solution.py:914
  79.1 43.6 %collective-permute-start.19 = (bf16[64,4608]{1,0:T(8,128)(2,1)S(1)}, bf16[64,4608]{1,0:T(8,128)(2,1)S(1)}, u32[]{:S(2)}, u32[]{:S(2)}) collective-permute-start(bf16[64,4608]{1,0:T(8,128)(2,1)S(1)} %pad_maximum_fusion.2.refs_14_.refs_11_.refs_10_.refs_22_), channel_id=1, source_target_pairs={{0,16},{1,9},{2,18},{3,11},{4,20},{5,13},{6,22},{7,15},{8,24},{9,1... | collective-permute-start | bytes 1769480 | tf_op jit(solution)/shard_map/ppermute | solution.py:924
  89.1 33.5 %collective-permute-start.20 = (bf16[64,4608]{1,0:T(8,128)(2,1)S(1)}, bf16[64,4608]{1,0:T(8,128)(2,1)}, u32[]{:S(2)}, u32[]{:S(2)}) collective-permute-start(bf16[64,4608]{1,0:T(8,128)(2,1)S(1)} %collective-permute-done.18.refs_12_.refs_11_.refs_23_), channel_id=1, source_target_pairs={{0,16},{1,9},{2,18},{3,11},{4,20},{5,13},{6,22},{7,15},{8,24},{9,1... | collective-permute-start | bytes 1769480 | tf_op jit(solution)/shard_map/ppermute | solution.py:924
  107.5 15.6 %collective-permute-start.15 = (f32[8,512]{1,0:T(8,128)S(1)}, f32[8,512]{1,0:T(8,128)S(1)}, u32[]{:S(2)}, u32[]{:S(2)}) collective-permute-start(f32[8,512]{1,0:T(8,128)S(1)} %slice_add_fusion.13.refs_6_.refs_17_.refs_8_), channel_id=1, source_target_pairs={{0,2},{1,3},{2,0},{3,1},{4,6},{5,7},{6,4},{7,5},{8,10},{9,11},{10,... | collective-permute-start | bytes 49160 | tf_op jit(solution)/shard_map/ppermute | solution.py:914
  120.5 5.5 %collective-permute-start.17 = (f32[8,512]{1,0:T(8,128)S(1)}, f32[8,512]{1,0:T(8,128)S(1)}, u32[]{:S(2)}, u32[]{:S(2)}) collective-permute-start(f32[8,512]{1,0:T(8,128)S(1)} %slice_add_fusion.13.refs_6_.refs_17_.refs_8_), channel_id=1, source_target_pairs={{0,6},{1,7},{2,4},{3,5},{4,2},{5,3},{6,0},{7,1},{8,14},{9,15},{10,... | collective-permute-start | bytes 49160 | tf_op jit(solution)/shard_map/ppermute | solution.py:914
  122.6 22.6 %collective-permute-start.25 = (bf16[64,4608]{1,0:T(8,128)(2,1)S(1)}, bf16[64,4608]{1,0:T(8,128)(2,1)S(1)}, u32[]{:S(2)}, u32[]{:S(2)}) collective-permute-start(bf16[64,4608]{1,0:T(8,128)(2,1)S(1)} %pad_maximum_fusion.2.refs_14_.refs_11_.refs_10_.refs_22_), channel_id=1, source_target_pairs={{0,1},{1,0},{2,3},{3,2},{4,5},{5,4},{6,7},{7,6},{8,9},{9,8},{10,11... | collective-permute-start | bytes 1769480 | tf_op jit(solution)/shard_map/ppermute | solution.py:914
  122.7 24.4 %collective-permute-start.26 = (bf16[64,4608]{1,0:T(8,128)(2,1)S(1)}, bf16[64,4608]{1,0:T(8,128)(2,1)S(1)}, u32[]{:S(2)}, u32[]{:S(2)}) collective-permute-start(bf16[64,4608]{1,0:T(8,128)(2,1)S(1)} %collective-permute-done.18.refs_12_.refs_11_.refs_23_), channel_id=1, source_target_pairs={{0,1},{1,0},{2,3},{3,2},{4,5},{5,4},{6,7},{7,6},{8,9},{9,8},{10,11... | collective-permute-start | bytes 1769480 | tf_op jit(solution)/shard_map/ppermute | solution.py:914
  123.2 26.4 %collective-permute-start.27 = (bf16[64,4608]{1,0:T(8,128)(2,1)S(1)}, bf16[64,4608]{1,0:T(8,128)(2,1)}, u32[]{:S(2)}, u32[]{:S(2)}) collective-permute-start(bf16[64,4608]{1,0:T(8,128)(2,1)S(1)} %collective-permute-done.19.refs_13_.refs_12_.refs_24_), channel_id=1, source_target_pairs={{0,1},{1,0},{2,3},{3,2},{4,5},{5,4},{6,7},{7,6},{8,9},{9,8},{10,11... | collective-permute-start | bytes 1769480 | tf_op jit(solution)/shard_map/ppermute | solution.py:914
  123.3 26.3 %collective-permute-start.28 = (bf16[64,4608]{1,0:T(8,128)(2,1)}, bf16[64,4608]{1,0:T(8,128)(2,1)}, u32[]{:S(2)}, u32[]{:S(2)}) collective-permute-start(bf16[64,4608]{1,0:T(8,128)(2,1)} %collective-permute-done.20.refs_14_.refs_13_.refs_25_), channel_id=1, source_target_pairs={{0,1},{1,0},{2,3},{3,2},{4,5},{5,4},{6,7},{7,6},{8,9},{9,8},{10,11... | collective-permute-start | bytes 1769480 | tf_op jit(solution)/shard_map/ppermute | solution.py:914
  145.2 5.0 collective-permute-start.22
  145.3 5.3 %collective-permute-start.23 = (f32[8,512]{1,0:T(8,128)S(1)}, f32[8,512]{1,0:T(8,128)S(1)}, u32[]{:S(2)}, u32[]{:S(2)}) collective-permute-start(f32[8,512]{1,0:T(8,128)S(1)} %slice_add_fusion.12.refs_6_.refs_18_.refs_8_), channel_id=1, source_target_pairs={{0,4},{1,5},{2,6},{3,7},{4,0},{5,1},{6,2},{7,3},{8,12},{9,13},{10,... | collective-permute-start | bytes 49160 | tf_op jit(solution)/shard_map/ppermute | solution.py:914
  147.1 5.9 %collective-permute-start.24 = (f32[8,512]{1,0:T(8,128)S(1)}, f32[8,512]{1,0:T(8,128)S(1)}, u32[]{:S(2)}, u32[]{:S(2)}) collective-permute-start(f32[8,512]{1,0:T(8,128)S(1)} %slice_add_fusion.12.refs_6_.refs_18_.refs_8_), channel_id=1, source_target_pairs={{0,6},{1,7},{2,4},{3,5},{4,2},{5,3},{6,0},{7,1},{8,14},{9,15},{10,... | collective-permute-start | bytes 49160 | tf_op jit(solution)/shard_map/ppermute | solution.py:914
  173.9 5.9 %collective-permute-start.32 = (f32[8,512]{1,0:T(8,128)}, f32[8,512]{1,0:T(8,128)}, u32[]{:S(2)}, u32[]{:S(2)}) collective-permute-start(f32[8,512]{1,0:T(8,128)} %slice_add_fusion.11.refs_5_.refs_16_.refs_9_), channel_id=1, source_target_pairs={{0,6},{1,7},{2,4},{3,5},{4,2},{5,3},{6,0},{7,1},{8,14},{9,15},{10,... | collective-permute-start | bytes 49160 | tf_op jit(solution)/shard_map/ppermute | solution.py:914
  191.0 5.5 %collective-permute-start.36 = (f32[8,512]{1,0:T(8,128)S(1)}, f32[8,512]{1,0:T(8,128)S(1)}, u32[]{:S(2)}, u32[]{:S(2)}) collective-permute-start(f32[8,512]{1,0:T(8,128)S(1)} %add.368.refs_4_.refs_15_.refs_5_), channel_id=1, source_target_pairs={{0,6},{1,7},{2,4},{3,5},{4,2},{5,3},{6,0},{7,1},{8,14},{9,15},{10,... | collective-permute-start | bytes 49160 | tf_op jit(solution)/shard_map/ppermute | solution.py:914
  206.5 5.4 %collective-permute-start.39 = (f32[8,512]{1,0:T(8,128)}, f32[8,512]{1,0:T(8,128)}, u32[]{:S(2)}, u32[]{:S(2)}) collective-permute-start(f32[8,512]{1,0:T(8,128)} %slice_add_fusion.10.refs_6_.refs_18_.refs_5_), channel_id=1, source_target_pairs={{0,4},{1,5},{2,6},{3,7},{4,0},{5,1},{6,2},{7,3},{8,12},{9,13},{10,... | collective-permute-start | bytes 49160 | tf_op jit(solution)/shard_map/ppermute | solution.py:914
  209.7 5.9 %collective-permute-start.40 = (f32[8,512]{1,0:T(8,128)}, f32[8,512]{1,0:T(8,128)}, u32[]{:S(2)}, u32[]{:S(2)}) collective-permute-start(f32[8,512]{1,0:T(8,128)} %slice_add_fusion.10.refs_6_.refs_18_.refs_5_), channel_id=1, source_target_pairs={{0,6},{1,7},{2,4},{3,5},{4,2},{5,3},{6,0},{7,1},{8,14},{9,15},{10,... | collective-permute-start | bytes 49160 | tf_op jit(solution)/shard_map/ppermute | solution.py:914
  234.1 5.5 %collective-permute-start.44 = (f32[8,512]{1,0:T(8,128)S(1)}, f32[8,512]{1,0:T(8,128)S(1)}, u32[]{:S(2)}, u32[]{:S(2)}) collective-permute-start(f32[8,512]{1,0:T(8,128)S(1)} %slice_add_fusion.9.refs_4_.refs_7_), channel_id=1, source_target_pairs={{0,6},{1,7},{2,4},{3,5},{4,2},{5,3},{6,0},{7,1},{8,14},{9,15},{10,... | collective-permute-start | bytes 49160 | tf_op jit(solution)/shard_map/ppermute | solution.py:914
  246.2 190.5 %reduce-scatter.3.cloned.1.call-start = ((), (), s32[]{:S(2)}) async-start(), calls=%async_computation.5 | async-start | bytes 6488064 | tf_op jit(solution)/shard_map/reduce_scatter | solution.py:1207
  251.9 5.5 %collective-permute-start.48 = (f32[8,512]{1,0:T(8,128)S(1)}, f32[8,512]{1,0:T(8,128)S(1)}, u32[]{:S(2)}, u32[]{:S(2)}) collective-permute-start(f32[8,512]{1,0:T(8,128)S(1)} %slice_add_fusion.8.refs_11_), channel_id=1, source_target_pairs={{0,6},{1,7},{2,4},{3,5},{4,2},{5,3},{6,0},{7,1},{8,14},{9,15},{10,... | collective-permute-start | bytes 49160 | tf_op jit(solution)/shard_map/ppermute | solution.py:914
  280.7 5.5 %collective-permute-start.52 = (f32[8,512]{1,0:T(8,128)S(1)}, f32[8,512]{1,0:T(8,128)S(1)}, u32[]{:S(2)}, u32[]{:S(2)}) collective-permute-start(f32[8,512]{1,0:T(8,128)S(1)} %add.372.refs_9_), channel_id=1, source_target_pairs={{0,6},{1,7},{2,4},{3,5},{4,2},{5,3},{6,0},{7,1},{8,14},{9,15},{10,... | collective-permute-start | bytes 49160 | tf_op jit(solution)/shard_map/ppermute | solution.py:914
  300.2 5.6 %collective-permute-start.56 = (f32[8,512]{1,0:T(8,128)S(1)}, f32[8,512]{1,0:T(8,128)}, u32[]{:S(2)}, u32[]{:S(2)}) collective-permute-start(f32[8,512]{1,0:T(8,128)S(1)} %add.373.refs_9_), channel_id=1, source_target_pairs={{0,6},{1,7},{2,4},{3,5},{4,2},{5,3},{6,0},{7,1},{8,14},{9,15},{10,... | collective-permute-start | bytes 49160 | tf_op jit(solution)/shard_map/ppermute | solution.py:914
  318.6 24.7 %collective-permute-start.57 = (bf16[1728,512]{1,0:T(8,128)(2,1)}, bf16[1728,512]{1,0:T(8,128)(2,1)S(1)}, u32[]{:S(2)}, u32[]{:S(2)}) collective-permute-start(bf16[1728,512]{1,0:T(8,128)(2,1)} %get-tuple-element.93), channel_id=1, source_target_pairs={{0,8},{1,17},{2,10},{3,19},{4,12},{5,21},{6,14},{7,23},{8,0},{9,25... | collective-permute-start | bytes 5308424 | tf_op jit(solution)/shard_map/ppermute | solution.py:924
  324.7 5.5 %collective-permute-start.61 = (f32[8,512]{1,0:T(8,128)S(1)}, f32[8,512]{1,0:T(8,128)S(1)}, u32[]{:S(2)}, u32[]{:S(2)}) collective-permute-start(f32[8,512]{1,0:T(8,128)S(1)} %add.374), channel_id=1, source_target_pairs={{0,6},{1,7},{2,4},{3,5},{4,2},{5,3},{6,0},{7,1},{8,14},{9,15},{10,... | collective-permute-start | bytes 49160 | tf_op jit(solution)/shard_map/ppermute | solution.py:914
  330.2 11.7 %collective-permute-start.62 = (f32[8,512]{1,0:T(8,128)S(1)}, f32[8,512]{1,0:T(8,128)S(1)}, u32[]{:S(2)}, u32[]{:S(2)}) collective-permute-start(f32[8,512]{1,0:T(8,128)S(1)} %add_add_fusion.refs_1_.refs_13_), channel_id=1, source_target_pairs={{0,8},{8,0},{16,24},{24,16},{1,9},{9,1},{17,25},{25,17},{2,10},{10... | collective-permute-start | bytes 49160 | tf_op jit(solution)/shard_map/ppermute | solution.py:914
  330.4 11.6 %collective-permute-start.63 = (f32[8,512]{1,0:T(8,128)S(1)}, f32[8,512]{1,0:T(8,128)S(1)}, u32[]{:S(2)}, u32[]{:S(2)}) collective-permute-start(f32[8,512]{1,0:T(8,128)S(1)} %add_add_fusion.refs_1_.refs_13_), channel_id=1, source_target_pairs={{0,16},{8,24},{16,0},{24,8},{1,17},{9,25},{17,1},{25,9},{2,18},{10... | collective-permute-start | bytes 49160 | tf_op jit(solution)/shard_map/ppermute | solution.py:914
  332.3 11.0 %collective-permute-start.64 = (f32[8,512]{1,0:T(8,128)S(1)}, f32[8,512]{1,0:T(8,128)S(1)}, u32[]{:S(2)}, u32[]{:S(2)}) collective-permute-start(f32[8,512]{1,0:T(8,128)S(1)} %add_add_fusion.refs_1_.refs_13_), channel_id=1, source_target_pairs={{0,24},{8,16},{16,8},{24,0},{1,25},{9,17},{17,9},{25,1},{2,26},{10... | collective-permute-start | bytes 49160 | tf_op jit(solution)/shard_map/ppermute | solution.py:914
  347.7 22.6 %collective-permute-start.65 = (bf16[1728,512]{1,0:T(8,128)(2,1)S(1)}, bf16[1728,512]{1,0:T(8,128)(2,1)S(1)}, u32[]{:S(2)}, u32[]{:S(2)}) collective-permute-start(bf16[1728,512]{1,0:T(8,128)(2,1)S(1)} %add.378.refs_4_.refs_6_), channel_id=1, source_target_pairs={{0,16},{1,9},{2,18},{3,11},{4,20},{5,13},{6,22},{7,15},{8,24},{9,1... | collective-permute-start | bytes 5308424 | tf_op jit(solution)/shard_map/ppermute | solution.py:924
  371.5 107.6 %reduce-scatter.5.cloned.1.call-start = ((), (), s32[]{:S(2)}) async-start(), calls=%async_computation.6 | async-start | bytes 2654208 | tf_op jit(solution)/shard_map/reduce_scatter | solution.py:1235
  396.7 10.5 %collective-permute-start.68 = (f32[8,512]{1,0:T(8,128)S(1)}, f32[8,512]{1,0:T(8,128)S(1)}, u32[]{:S(2)}, u32[]{:S(2)}) collective-permute-start(f32[8,512]{1,0:T(8,128)S(1)} %slice_add_fusion.7.refs_12_), channel_id=1, source_target_pairs={{0,2},{1,3},{2,0},{3,1},{4,6},{5,7},{6,4},{7,5},{8,10},{9,11},{10,... | collective-permute-start | bytes 49160 | tf_op jit(solution)/shard_map/ppermute | solution.py:914
  396.7 10.5 %collective-permute-start.69 = (f32[8,512]{1,0:T(8,128)S(1)}, f32[8,512]{1,0:T(8,128)S(1)}, u32[]{:S(2)}, u32[]{:S(2)}) collective-permute-start(f32[8,512]{1,0:T(8,128)S(1)} %slice_add_fusion.7.refs_12_), channel_id=1, source_target_pairs={{0,4},{1,5},{2,6},{3,7},{4,0},{5,1},{6,2},{7,3},{8,12},{9,13},{10,... | collective-permute-start | bytes 49160 | tf_op jit(solution)/shard_map/ppermute | solution.py:914
  398.2 9.0 %collective-permute-start.70 = (f32[8,512]{1,0:T(8,128)S(1)}, f32[8,512]{1,0:T(8,128)S(1)}, u32[]{:S(2)}, u32[]{:S(2)}) collective-permute-start(f32[8,512]{1,0:T(8,128)S(1)} %slice_add_fusion.7.refs_12_), channel_id=1, source_target_pairs={{0,6},{1,7},{2,4},{3,5},{4,2},{5,3},{6,0},{7,1},{8,14},{9,15},{10,... | collective-permute-start | bytes 49160 | tf_op jit(solution)/shard_map/ppermute | solution.py:914
  436.7 18.0 %collective-permute-start.75 = (bf16[64,5632]{1,0:T(8,128)(2,1)}, bf16[64,5632]{1,0:T(8,128)(2,1)S(1)}, u32[]{:S(2)}, u32[]{:S(2)}) collective-permute-start(bf16[64,5632]{1,0:T(8,128)(2,1)} %reduce-scatter.3.cloned.1.call-done.refs_2_), channel_id=1, source_target_pairs={{0,8},{1,17},{2,10},{3,19},{4,12},{5,21},{6,14},{7,23},{8,0},{9,25... | collective-permute-start | bytes 2162696 | tf_op jit(solution)/shard_map/ppermute | solution.py:924
  438.7 16.0 %collective-permute-start.76 = (bf16[64,5632]{1,0:T(8,128)(2,1)}, bf16[64,5632]{1,0:T(8,128)(2,1)S(1)}, u32[]{:S(2)}, u32[]{:S(2)}) collective-permute-start(bf16[64,5632]{1,0:T(8,128)(2,1)} %reduce-scatter.3.cloned.1.call-done.refs_2_), channel_id=1, source_target_pairs={{0,16},{1,9},{2,18},{3,11},{4,20},{5,13},{6,22},{7,15},{8,24},{9,1... | collective-permute-start | bytes 2162696 | tf_op jit(solution)/shard_map/ppermute | solution.py:924
  442.3 5.6 %collective-permute-start.74 = (f32[8,512]{1,0:T(8,128)S(1)}, f32[8,512]{1,0:T(8,128)S(1)}, u32[]{:S(2)}, u32[]{:S(2)}) collective-permute-start(f32[8,512]{1,0:T(8,128)S(1)} %slice_add_fusion.6.refs_12_), channel_id=1, source_target_pairs={{0,6},{1,7},{2,4},{3,5},{4,2},{5,3},{6,0},{7,1},{8,14},{9,15},{10,... | collective-permute-start | bytes 49160 | tf_op jit(solution)/shard_map/ppermute | solution.py:914
  467.2 10.7 %collective-permute-start.78 = (bf16[128,1152]{1,0:T(8,128)(2,1)S(1)}, bf16[128,1152]{1,0:T(8,128)(2,1)S(1)}, u32[]{:S(2)}, u32[]{:S(2)}) collective-permute-start(bf16[128,1152]{1,0:T(8,128)(2,1)S(1)} %get-tuple-element.124), channel_id=1, source_target_pairs={{0,2},{1,3},{2,0},{3,1},{4,6},{5,7},{6,4},{7,5},{8,10},{9,11},{10,... | collective-permute-start | bytes 884744 | tf_op jit(solution)/shard_map/ppermute | solution.py:914
  468.0 38.2 %collective-permute-start.86 = (bf16[64,5632]{1,0:T(8,128)(2,1)S(1)}, bf16[64,5632]{1,0:T(8,128)(2,1)S(1)}, u32[]{:S(2)}, u32[]{:S(2)}) collective-permute-start(bf16[64,5632]{1,0:T(8,128)(2,1)S(1)} %collective-permute-done.75.refs_18_.refs_3_), channel_id=1, source_target_pairs={{0,16},{1,9},{2,18},{3,11},{4,20},{5,13},{6,22},{7,15},{8,24},{9,1... | collective-permute-start | bytes 2162696 | tf_op jit(solution)/shard_map/ppermute | solution.py:924
  477.9 10.9 %collective-permute-start.79 = (bf16[64,1152]{1,0:T(8,128)(2,1)S(1)}, bf16[64,1152]{1,0:T(8,128)(2,1)S(1)}, u32[]{:S(2)}, u32[]{:S(2)}) collective-permute-start(bf16[64,1152]{1,0:T(8,128)(2,1)S(1)} %slice_add_fusion.2), channel_id=1, source_target_pairs={{0,4},{1,5},{2,6},{3,7},{4,0},{5,1},{6,2},{7,3},{8,12},{9,13},{10,... | collective-permute-start | bytes 442376 | tf_op jit(solution)/shard_map/ppermute | solution.py:914
  479.0 18.2 %collective-permute-start.83 = (bf16[64,2304]{1,0:T(8,128)(2,1)}, bf16[64,2304]{1,0:T(8,128)(2,1)}, u32[]{:S(2)}, u32[]{:S(2)}) collective-permute-start(bf16[64,2304]{1,0:T(8,128)(2,1)} %shard_map.275.refs_1_), channel_id=1, source_target_pairs={{0,8},{1,17},{2,10},{3,19},{4,12},{5,21},{6,14},{7,23},{8,0},{9,25... | collective-permute-start | bytes 884744 | tf_op jit(solution)/shard_map/ppermute | solution.py:924
  490.7 5.2 collective-permute-start.80
  492.2 16.4 %collective-permute-start.87 = (f32[3,4,512]{2,1,0:T(4,128)}, f32[3,4,512]{2,1,0:T(4,128)S(1)}, u32[]{:S(2)}, u32[]{:S(2)}) collective-permute-start(f32[3,4,512]{2,1,0:T(4,128)} %shard_map.277.refs_6_), channel_id=1, source_target_pairs={{0,8},{8,0},{16,24},{24,16},{1,9},{9,1},{17,25},{25,17},{2,10},{10... | collective-permute-start | bytes 73736 | tf_op jit(solution)/shard_map/ppermute | solution.py:914
  493.4 16.0 %collective-permute-start.88 = (f32[3,4,512]{2,1,0:T(4,128)}, f32[3,4,512]{2,1,0:T(4,128)}, u32[]{:S(2)}, u32[]{:S(2)}) collective-permute-start(f32[3,4,512]{2,1,0:T(4,128)} %shard_map.277.refs_6_), channel_id=1, source_target_pairs={{0,16},{8,24},{16,0},{24,8},{1,17},{9,25},{17,1},{25,9},{2,18},{10... | collective-permute-start | bytes 73736 | tf_op jit(solution)/shard_map/ppermute | solution.py:914
  495.9 22.1 %collective-permute-start.84 = (bf16[64,2304]{1,0:T(8,128)(2,1)S(1)}, bf16[64,2304]{1,0:T(8,128)(2,1)}, u32[]{:S(2)}, u32[]{:S(2)}) collective-permute-start(bf16[64,2304]{1,0:T(8,128)(2,1)S(1)} %copy-done.13), channel_id=1, source_target_pairs={{0,16},{1,9},{2,18},{3,11},{4,20},{5,13},{6,22},{7,15},{8,24},{9,1... | collective-permute-start | bytes 884744 | tf_op jit(solution)/shard_map/ppermute | solution.py:924
  497.2 20.8 %collective-permute-start.85 = (bf16[64,2304]{1,0:T(8,128)(2,1)}, bf16[64,2304]{1,0:T(8,128)(2,1)}, u32[]{:S(2)}, u32[]{:S(2)}) collective-permute-start(bf16[64,2304]{1,0:T(8,128)(2,1)} %collective-permute-done.83.refs_2_), channel_id=1, source_target_pairs={{0,16},{1,9},{2,18},{3,11},{4,20},{5,13},{6,22},{7,15},{8,24},{9,1... | collective-permute-start | bytes 884744 | tf_op jit(solution)/shard_map/ppermute | solution.py:924
  506.9 5.1 collective-permute-start.89
  508.6 7.1 %collective-permute-start.81 = (bf16[64,1152]{1,0:T(8,128)(2,1)S(1)}, bf16[64,1152]{1,0:T(8,128)(2,1)S(1)}, u32[]{:S(2)}, u32[]{:S(2)}) collective-permute-start(bf16[64,1152]{1,0:T(8,128)(2,1)S(1)} %fusion.refs_12_.refs_1_), channel_id=1, source_target_pairs={{0,16},{1,9},{2,18},{3,11},{4,20},{5,13},{6,22},{7,15},{8,24},{9,1... | collective-permute-start | bytes 442376 | tf_op jit(solution)/shard_map/ppermute | solution.py:924
  509.4 6.3 %collective-permute-start.82 = (bf16[64,1152]{1,0:T(8,128)(2,1)}, bf16[64,1152]{1,0:T(8,128)(2,1)S(1)}, u32[]{:S(2)}, u32[]{:S(2)}) collective-permute-start(bf16[64,1152]{1,0:T(8,128)(2,1)} %shard_map.273), channel_id=1, source_target_pairs={{0,16},{1,9},{2,18},{3,11},{4,20},{5,13},{6,22},{7,15},{8,24},{9,1... | collective-permute-start | bytes 442376 | tf_op jit(solution)/shard_map/ppermute | solution.py:924
  (138 other events, 946.0 us)
Sparse Core Ops, SparseCore 0:
  28.8 65.0 all-gather.5
  96.1 20.7 all-gather.7
  119.1 52.6 all-gather.9
  246.3 33.4 all-gather.11
  371.6 64.6 reduce-scatter.2
  438.5 36.6 reduce-scatter.4

commit v3 on v2

v3 whole, which is shorter than its diff:
```python
import functools
import math

import jax
import jax.numpy as jnp
from jax import lax
from jax.experimental import pallas as pl
from jax.experimental.pallas import tpu as pltpu
from jax.sharding import PartitionSpec as P

HEIGHT = 36
WIDTH = 48
BAND = 18
HALF_WIDTH = 24
CANVAS = 2
TASKS = 3
COLS = CANVAS * WIDTH
GROUPS = COLS // HALF_WIDTH
EPSILON = 1e-05
TAPS = 9
TILE_ROWS = 6
LANES = 128
PIECE = 16
MIB = 2**20
BF = jnp.bfloat16
F32 = jnp.float32
NT = (((1,), (1,)), ((), ()))
TN = (((0,), (0,)), ((), ()))

ANY = pl.BlockSpec(memory_space=pl.ANY)
HBM = pl.BlockSpec(memory_space=pltpu.HBM)
SMEM = pl.BlockSpec(memory_space=pltpu.SMEM)


def affine(row, co, scale, shift):
    step = row.shape[0] // GROUPS
    return jnp.concatenate(
        [
            row[step * j : step * (j + 1)] * co[4 * scale + j : 4 * scale + j + 1, :]
            + co[4 * shift + j : 4 * shift + j + 1, :]
            for j in range(GROUPS)
        ],
        axis=0,
    )


def scaled(row, co, scale):
    step = row.shape[0] // GROUPS
    return jnp.concatenate(
        [
            row[step * j : step * (j + 1)] * co[4 * scale + j : 4 * scale + j + 1, :]
            for j in range(GROUPS)
        ],
        axis=0,
    )


def sigmoid(v):
    return 0.5 * jnp.tanh(0.5 * v) + 0.5


def silu(v):
    return v * sigmoid(v)


def silu_slope(v):
    s = sigmoid(v)
    return s * (1.0 + v * (1.0 - s))


def norm_coefs(co, base, stats, params, which, cnt, info):
    gain = params[which : which + 1, :]
    bias = params[which + 6 : which + 7, :]
    means, scales = [], []
    for d in range(2):
        mean = stats[d : d + 1, :] / cnt[d]
        var = stats[2 + d : 3 + d, :] / cnt[d] - mean * mean
        means.append(mean)
        scales.append(lax.rsqrt(var + EPSILON))
    for j in range(GROUPS):
        one = info[j] == 1
        mean = jnp.where(one, means[1], means[0])
        scale = jnp.where(one, scales[1], scales[0])
        full = scale * gain
        co[4 * base + j : 4 * base + j + 1, :] = full
        co[4 * base + 4 + j : 4 * base + 5 + j, :] = bias - mean * full
        co[4 * base + 8 + j : 4 * base + 9 + j, :] = scale
        co[4 * base + 12 + j : 4 * base + 13 + j, :] = -mean * scale


def grad_coefs(co, base, norm, sums, cnt, info):
    for j in range(GROUPS):
        one = info[j] == 1
        count = jnp.where(one, cnt[1], cnt[0])
        plain = jnp.where(one, sums[1:2, :], sums[0:1, :]) / count
        cross = jnp.where(one, sums[3:4, :], sums[2:3, :]) / count
        full = co[4 * norm + j : 4 * norm + j + 1, :]
        scale = co[4 * norm + 8 + j : 4 * norm + 9 + j, :]
        shift = co[4 * norm + 12 + j : 4 * norm + 13 + j, :]
        co[4 * base + j : 4 * base + j + 1, :] = -full * cross * scale
        co[4 * base + 4 + j : 4 * base + 5 + j, :] = -full * (plain + cross * shift)


def grad_row(g, z, co, norm, base):
    return scaled(g, co, norm) + affine(z, co, base, base + 1)


def add_sums(acc, slot, values):
    step = HALF_WIDTH // 8
    count = values.shape[0] // COLS
    channels = values.shape[1]
    acc[slot] += jnp.sum(
        values.reshape(count, GROUPS, step, 8, channels), axis=(0, 2)
    )


def put_sums(acc, info, out, start):
    for slot in range(2):
        groups = [jnp.sum(acc[slot, j], axis=0, keepdims=True) for j in range(GROUPS)]
        for d in range(2):
            total = jnp.zeros_like(groups[0])
            for j in range(GROUPS):
                total = total + jnp.where(info[j] == d, groups[j], 0.0)
            row = start + 2 * slot + d
            out[row : row + 1, :] = total
    out[start + 4 : start + 8, :] = jnp.zeros((4, out.shape[1]), F32)


def put_edge(out, ref, info, rows):
    start = jnp.where(info[6] == 1, 0, (rows - 1) * COLS)
    out[0:COLS, :] = ref[pl.ds(pl.multiple_of(start, COLS), COLS), :].astype(out.dtype)


def make_masks(mk, info):
    col = lax.broadcasted_iota(jnp.int32, mk.shape[1:], 0)
    small = (info[4] == 1, info[5] == 1)
    left = (col == 0) | (col == WIDTH)
    right = (col == WIDTH - 1) | (col == COLS - 1)
    for s in range(2):
        left = left | ((col == s * WIDTH + HALF_WIDTH) & small[s])
        right = right | ((col == s * WIDTH + HALF_WIDTH - 1) & small[s])
    mk[0] = jnp.where(left, 0.0, 1.0)
    mk[1] = jnp.where(right, 0.0, 1.0)


def part(ref, c):
    return ref.at[(slice(None),) * (len(ref.shape) - 1) + (pl.ds(c * LANES, LANES),)]


def put_row(taps, at, row, mk):
    here = pl.ds(pl.multiple_of(at * COLS, COLS), COLS)
    taps[0, here, :] = (pltpu.roll(row, 1, 0) * mk[0]).astype(BF)
    taps[1, here, :] = row.astype(BF)
    taps[2, here, :] = (pltpu.roll(row, COLS - 1, 0) * mk[1]).astype(BF)


def keep_large(row, info):
    step = COLS // GROUPS
    keep = [jnp.where(info[4 + j // 2] == 1, 0.0, 1.0) for j in range(GROUPS)]
    return jnp.concatenate(
        [row[step * j : step * (j + 1)] * keep[j] for j in range(GROUPS)], axis=0
    )


def put_halo(taps, make, mk, info, rows):
    for c in range(taps.shape[2] // LANES):
        row = keep_large(make(c), info)
        put_row(part(taps, c), jnp.where(info[6] == 1, 0, rows + 1), row, mk)
        put_row(part(taps, c), jnp.where(info[6] == 1, rows + 1, 0), jnp.zeros_like(row), mk)


def conv_tile(taps, w, at, rows, transpose):
    acc = None
    channels = taps.shape[2]
    for t in range(TAPS):
        di, dj = divmod(t, 3)
        a = taps[dj, (at + di) * COLS : (at + di + rows) * COLS, :]
        if transpose:
            k = w[:, (8 - t) * channels : (9 - t) * channels]
            r = jnp.dot(a, k, preferred_element_type=F32)
        else:
            k = w[:, t * channels : (t + 1) * channels]
            r = lax.dot_general(a, k, NT, preferred_element_type=F32)
        acc = r if acc is None else acc + r
    return acc


def row_at(r):
    return pl.ds(pl.multiple_of(r * COLS, COLS), COLS)


def tile_at(m):
    return slice(m * TILE_ROWS * COLS, (m + 1) * TILE_ROWS * COLS)


def loop(count, body):
    def step(i, carry):
        body(i)
        return carry

    lax.fori_loop(0, count, step, 0)


def pooled(buf, values):
    half = COLS // 2
    buf[...] = values
    return (buf[pl.ds(0, half, stride=2), :] + buf[pl.ds(1, half, stride=2), :]) * 0.25


def spread(buf, values):
    half = COLS // 2
    quarter = values.astype(F32) * 0.25
    buf[pl.ds(0, half, stride=2), :] = quarter
    buf[pl.ds(1, half, stride=2), :] = quarter
    return buf[...]


class Copies:
    def __init__(self, sems):
        self.sems = sems
        self.used = 0
        self.open = []

    def start(self, src, dst):
        copy = pltpu.make_async_copy(src, dst, self.sems.at[self.used])
        self.used += 1
        copy.start()
        return copy

    def put(self, src, dst):
        self.open.append(self.start(src, dst))

    def tiles(self, src, dst, rows):
        return [
            self.start(src.at[pl.ds(m * TILE_ROWS * COLS, TILE_ROWS * COLS)],
                       dst.at[pl.ds(m * TILE_ROWS * COLS, TILE_ROWS * COLS)])
            for m in range(rows // TILE_ROWS)
        ]

    def put_tile(self, src, dst, m):
        here = pl.ds(m * TILE_ROWS * COLS, TILE_ROWS * COLS)
        self.put(src.at[here], dst.at[here])

    def weights(self, pieces, place, dst):
        if len(pieces) == 1:
            return [self.start(pieces[0], dst)]
        copies = []
        count = pieces[0].shape[0] // PIECE
        for i, piece in enumerate(pieces):
            for k in range(count):
                row = pl.multiple_of(place[i * count + k], PIECE)
                copies.append(
                    self.start(piece.at[pl.ds(k * PIECE, PIECE)], dst.at[pl.ds(row, PIECE)])
                )
        return copies

    def finish(self):
        for copy in self.open:
            copy.wait()


def bring(io, ref, rest, count, rows):
    if len(rest) == count:
        return ref, [()] * (rows // TILE_ROWS), rest
    return rest[0], [(copy,) for copy in io.tiles(ref, rest[0], rows)], rest[1:]


def put_norms(norms, i, sums):
    norms[i : i + 1, :] = sums[2:3, :] + sums[3:4, :]
    norms[3 + i : 4 + i, :] = sums[0:1, :] + sums[1:2, :]


def settle(parts, dst):
    if len(parts) == 4:
        dst[...] = (parts[0][...] + parts[1][...]) + (parts[2][...] + parts[3][...])
    else:
        dst[...] = parts[0][...]
    return dst


def wait(*copies):
    for copy in copies:
        copy.wait()


def all_parts(channels, body):
    for c in range(channels // LANES):
        body(c)


def each_pair(m, channels, body):
    half = TILE_ROWS // 2
    loop(half, lambda i: all_parts(channels, lambda c: body(m * half + i, c)))


def each_row(m, channels, body):
    loop(TILE_ROWS, lambda r: all_parts(channels, lambda c: body(m * TILE_ROWS + r, c)))


def cast_kernel(pick, count, spot, *refs):
    sources, out, wide, sems = refs[:count], refs[-count - 2], refs[-count - 1 : -1], refs[-1]
    io = Copies(sems)
    rows, channels = out.shape[0], wide[0].shape[2]
    first = pl.multiple_of(spot[0] * rows, rows) if pick else 0
    reads = []
    for src, dst in zip(sources, wide):
        if len(src.shape) == 4:
            src = src.at[spot[1]]
        reads.append(io.start(src.at[:, pl.ds(first, rows), :], dst))
    start = 0
    for src, read in zip(wide, reads):
        read.wait()
        for t in range(src.shape[0]):
            out[:, start : start + channels] = src[t].astype(BF)
            start += channels


def conv_outputs(rows, info, w, z, zv, pay, quarter, taps, acc, io, w_reads):
    if quarter is not None:
        width = quarter.shape[2]
        io.put(taps.at[:, :, pl.ds(pl.multiple_of(info[7] * width, 128), width)], quarter)
    wait(*w_reads)
    for m in range(rows // TILE_ROWS):
        out = conv_tile(taps, w, m * TILE_ROWS, TILE_ROWS, False)
        zv[tile_at(m), :] = out
        io.put_tile(zv, z, m)
        add_sums(acc, 0, out)
        add_sums(acc, 1, out * out)
    put_edge(pay, zv, info, rows)
    put_sums(acc, info, pay, COLS)


def first_conv_kernel(rows, info, place, x, halo, pieces, z, zv, pay, quarter, xv, wv, taps, mk, acc, sems):
    io = Copies(sems)
    ch = x.shape[1]
    reads = io.tiles(x, xv, rows)
    w_reads = io.weights(pieces, place, wv)
    make_masks(mk, info)
    acc[...] = jnp.zeros_like(acc)
    for m, read in enumerate(reads):
        read.wait()
        each_row(
            m, ch, lambda r, c: put_row(part(taps, c), r + 1, part(xv, c)[row_at(r), :].astype(F32), mk)
        )
    put_halo(taps, lambda c: part(halo, c)[...].astype(F32), mk, info, rows)
    conv_outputs(rows, info, wv, z, zv, pay, quarter, taps, acc, io, w_reads)
    io.finish()


def conv_kernel(
    rows, which, info, cnt, place, params, x, recv, stats, pieces, z, zv, pay, quarter, kept, *rest
):
    io = Copies(rest[-1])
    x, reads, rest = bring(io, x, rest, 7, rows)
    sv, wv, taps, mk, acc, co, _ = rest
    w_reads = io.weights(pieces, place, wv)
    make_masks(mk, info)
    acc[...] = jnp.zeros_like(acc)
    norm_coefs(co, 0, settle(stats, sv), params, which, cnt, info)
    io.put(sv, kept)

    def act(ref, here, c):
        return silu(affine(part(ref, c)[here, :], part(co, c), 0, 1))

    for m, read in enumerate(reads):
        wait(*read)
        each_row(m, x.shape[1], lambda r, c: put_row(part(taps, c), r + 1, act(x, row_at(r), c), mk))
    put_halo(taps, lambda c: act(recv, slice(0, COLS), c), mk, info, rows)
    conv_outputs(rows, info, wv, z, zv, pay, quarter, taps, acc, io, w_reads)
    io.finish()


def enter_kernel(
    rows, which, info, cnt, params, x, recv, stats, w, low, pool, u, uv, pay, kept, *rest
):
    io = Copies(rest[-1])
    x, reads, rest = bring(io, x, rest, 8, rows)
    sv, wv, lowv, poolv, acc, co, buf, _ = rest
    w_read = io.start(w.at[:, pl.ds(0, wv.shape[1])], wv)
    acc[...] = jnp.zeros_like(acc)
    norm_coefs(co, 0, settle(stats, sv), params, which, cnt, info)
    io.put(sv, kept)
    half = COLS // 2
    ch = x.shape[1]

    def act(ref, here, c):
        return silu(affine(part(ref, c)[here, :], part(co, c), 0, 1))

    def pair(i, c):
        first, second = act(x, row_at(2 * i), c), act(x, row_at(2 * i + 1), c)
        part(lowv, c)[row_at(2 * i), :] = first.astype(BF)
        part(lowv, c)[row_at(2 * i + 1), :] = second.astype(BF)
        part(poolv, c)[pl.ds(pl.multiple_of(i * half, half), half), :] = pooled(
            buf.at[c], first + second
        ).astype(BF)

    for c in range(ch // LANES):
        part(lowv, c)[rows * COLS : (rows + 1) * COLS, :] = act(recv, slice(0, COLS), c).astype(BF)
    for m, read in enumerate(reads):
        wait(*read)
        each_pair(m, ch, pair)
        if m == 0:
            w_read.wait()
        out = lax.dot_general(lowv[tile_at(m), :], wv[...], NT, preferred_element_type=F32)
        uv[tile_at(m), :] = out
        io.put_tile(uv, u, m)
        add_sums(acc, 0, out)
        add_sums(acc, 1, out * out)
    io.put(lowv, low)
    io.put(poolv, pool)
    put_sums(acc, info, pay, 0)
    io.finish()


def mask_kernel(
    rows, which, info, cnt, params, u, stats, w, p, q, qv, pay, kept, sv, wv, ev, acc, co, sems
):
    io = Copies(sems)
    w_read = io.start(w.at[:, pl.ds(wv.shape[1], wv.shape[1])], wv)
    acc[...] = jnp.zeros_like(acc)
    norm_coefs(co, 0, settle(stats, sv), params, which, cnt, info)
    io.put(sv, kept)

    def each(r, c):
        part(ev, c)[row_at(r), :] = silu(affine(part(u, c)[row_at(r), :], part(co, c), 0, 1)).astype(BF)

    for m in range(rows // TILE_ROWS):
        each_row(m, u.shape[1], each)
        io.put_tile(ev, p, m)
        if m == 0:
            w_read.wait()
        out = lax.dot_general(ev[tile_at(m), :], wv[...], NT, preferred_element_type=F32)
        qv[tile_at(m), :] = out
        io.put_tile(qv, q, m)
        add_sums(acc, 0, out)
        add_sums(acc, 1, out * out)
    put_edge(pay, qv, info, rows)
    put_sums(acc, info, pay, COLS)
    io.finish()


def branch_conv_kernel(
    rows, which, info, cnt, params, low, q, recv, stats, w, y, yv, pay, wide_taps, kept, *rest
):
    io = Copies(rest[-1])
    q, reads, rest = bring(io, q, rest, 8, rows)
    lv, sv, wv, taps, mk, acc, co, _ = rest
    low_read = io.start(low, lv)
    w_read = io.start(w, wv)
    make_masks(mk, info)
    acc[...] = jnp.zeros_like(acc)
    norm_coefs(co, 0, settle(stats, sv), params, which, cnt, info)
    io.put(sv, kept)

    def masked(at, ref, here, c):
        gate = sigmoid(affine(part(ref, c)[here, :], part(co, c), 0, 1))
        return part(lv, c)[at, :].astype(F32) * gate

    low_read.wait()
    for m, read in enumerate(reads):
        wait(*read)
        each_row(
            m, q.shape[1],
            lambda r, c: put_row(part(taps, c), r + 1, masked(row_at(r), q, row_at(r), c), mk),
        )
    put_halo(
        taps, lambda c: masked(slice(rows * COLS, (rows + 1) * COLS), recv, slice(0, COLS), c), mk, info, rows
    )
    io.put(taps, wide_taps)
    conv_outputs(rows, info, wv, y, yv, pay, None, taps, acc, io, [w_read])
    io.finish()


def turn_kernel(
    rows, which, info, cnt, params, y, stats, cot, pool, g, pay, kept, gv, sv, cv, poolv, acc, co, buf, sems
):
    io = Copies(sems)
    cot_read = io.start(cot.at[info[9]], cv)
    acc[...] = jnp.zeros_like(acc)
    norm_coefs(co, 0, settle(stats, sv), params, which, cnt, info)
    io.put(sv, kept)
    half = COLS // 2

    def pair(i, c):
        here = pl.ds(pl.multiple_of(i * half, half), half)
        ct = spread(buf.at[c], part(cv, c)[here, :])
        total = None
        for k in range(2):
            at = row_at(2 * i + k)
            row = part(y, c)[at, :]
            v = affine(row, part(co, c), 0, 1)
            s = sigmoid(v)
            f = v * s
            total = f if total is None else total + f
            gr = ct * (s * (1.0 + v * (1.0 - s)))
            part(gv, c)[at, :] = gr
            add_sums(part(acc, c), 0, gr)
            add_sums(part(acc, c), 1, gr * affine(row, part(co, c), 2, 3))
        part(poolv, c)[here, :] = pooled(buf.at[c], total).astype(BF)

    cot_read.wait()
    for m in range(rows // TILE_ROWS):
        each_pair(m, y.shape[1], pair)
        io.put_tile(gv, g, m)
    io.put(poolv, pool)
    put_edge(pay, gv, info, rows)
    put_sums(acc, info, pay, COLS)
    io.finish()


def branch_back_kernel(
    rows, info, cnt, params, g, y, recv_g, recv_y, stats, sums, w, low, q, qstats,
    e, gv, gs, pay, norms, gin, yv, hv, sv, tv, qsv, lv, qv, ev, wv, taps, mk, acc, co, sems,
):
    io = Copies(sems)
    small = [io.start(stats, sv), io.start(qstats, qsv), io.start(recv_y, hv)]
    reads = list(zip(io.tiles(g, gin, rows), io.tiles(y, yv, rows)))
    w_read = io.start(w, wv)
    low_read = io.start(low.at[pl.ds(0, rows * COLS)], lv)
    q_read = io.start(q, qv)
    make_masks(mk, info)
    acc[...] = jnp.zeros_like(acc)
    wait(*small)
    norm_coefs(co, 0, sv, params, 5, cnt, info)
    grad_coefs(co, 4, 0, settle(sums, tv), cnt, info)
    norm_coefs(co, 6, qsv, params, 4, cnt, info)
    norms[...] = jnp.zeros_like(norms)
    put_norms(norms, 2, tv)

    ch = gv.shape[1]

    def grad(g_ref, y_ref, here, c):
        return grad_row(part(g_ref, c)[here, :], part(y_ref, c)[here, :], part(co, c), 0, 4)

    def each(r, c):
        row = grad(gin, yv, row_at(r), c)
        part(ev, c)[row_at(r), :] = row.astype(BF)
        put_row(part(taps, c), r + 1, row, mk)

    for m, pair in enumerate(reads):
        wait(*pair)
        each_row(m, ch, each)
        io.put_tile(ev, e, m)
    put_halo(taps, lambda c: grad(recv_g, hv, slice(0, COLS), c), mk, info, rows)
    wait(w_read, low_read, q_read)

    def post(r, c):
        here = row_at(r)
        value = part(gv, c)[here, :]
        row = part(qv, c)[here, :]
        gate = sigmoid(affine(row, part(co, c), 6, 7))
        value = value * gate
        part(yv, c)[here, :] = value
        out = value * part(lv, c)[here, :].astype(F32) * (1.0 - gate)
        part(gv, c)[here, :] = out
        add_sums(part(acc, c), 0, out)
        add_sums(part(acc, c), 1, out * affine(row, part(co, c), 8, 9))

    for m in range(rows // TILE_ROWS):
        gv[tile_at(m), :] = conv_tile(taps, wv, m * TILE_ROWS, TILE_ROWS, True)
        each_row(m, ch, post)
        io.put_tile(yv, gs, m)
    put_sums(acc, info, pay, 0)
    io.finish()


def mask_back_kernel(
    rows, info, cnt, params, g, q, stats, sums, w, u, ustats, before, e, gv, pay, norms,
    qv, uv, sv, tv, usv, wv, ev, acc, co, sems,
):
    io = Copies(sems)
    small = [io.start(stats, sv), io.start(ustats, usv)]
    reads = io.tiles(q, qv, rows)
    w_read = io.start(w.at[:, pl.ds(wv.shape[1], wv.shape[1])], wv)
    u_reads = io.tiles(u, uv, rows)
    acc[...] = jnp.zeros_like(acc)
    wait(*small)
    norm_coefs(co, 0, sv, params, 4, cnt, info)
    grad_coefs(co, 4, 0, settle(sums, tv), cnt, info)
    norm_coefs(co, 6, usv, params, 3, cnt, info)
    norms[...] = before[...]
    put_norms(norms, 1, tv)

    ch = g.shape[1]

    def each(r, c):
        here = row_at(r)
        part(ev, c)[here, :] = grad_row(
            part(g, c)[here, :], part(qv, c)[here, :], part(co, c), 0, 4
        ).astype(BF)

    def post(r, c):
        here = row_at(r)
        row = part(uv, c)[here, :]
        out = part(gv, c)[here, :] * silu_slope(affine(row, part(co, c), 6, 7))
        part(gv, c)[here, :] = out
        add_sums(part(acc, c), 0, out)
        add_sums(part(acc, c), 1, out * affine(row, part(co, c), 8, 9))

    for m, read in enumerate(reads):
        read.wait()
        each_row(m, ch, each)
        io.put_tile(ev, e, m)
        if m == 0:
            w_read.wait()
        gv[tile_at(m), :] = jnp.dot(ev[tile_at(m), :], wv[...], preferred_element_type=F32)
        u_reads[m].wait()
        each_row(m, ch, post)
    put_sums(acc, info, pay, 0)
    io.finish()


def leave_kernel(
    rows, info, cnt, params, g, u, stats, sums, w, gs, z, zstats, cot, before, e, out, pay, norms,
    gv, uv, sv, tv, zsv, wv, gsv, zv, cv, ev, ov, acc, co, buf, sems,
):
    io = Copies(sems)
    small = [io.start(stats, sv), io.start(zstats, zsv)]
    reads = io.tiles(u, uv, rows)
    w_read = io.start(w.at[:, pl.ds(0, wv.shape[1])], wv)
    later = list(zip(io.tiles(gs, gsv, rows), io.tiles(z, zv, rows)))
    cot_read = io.start(cot, cv)
    acc[...] = jnp.zeros_like(acc)
    wait(*small)
    norm_coefs(co, 0, sv, params, 3, cnt, info)
    grad_coefs(co, 4, 0, settle(sums, tv), cnt, info)
    norm_coefs(co, 6, zsv, params, 2, cnt, info)
    norms[...] = before[...]
    put_norms(norms, 0, tv)
    half = COLS // 2
    active = info[8] == 1

    ch = g.shape[1]

    def each(r, c):
        here = row_at(r)
        part(ev, c)[here, :] = grad_row(
            part(g, c)[here, :], part(uv, c)[here, :], part(co, c), 0, 4
        ).astype(BF)

    def post(i, c):
        ct = spread(buf.at[c], part(cv, c)[pl.ds(pl.multiple_of(i * half, half), half), :])
        for k in range(2):
            here = row_at(2 * i + k)
            grad = jnp.where(active, part(gv, c)[here, :] + part(gsv, c)[here, :], ct)
            part(ov, c)[here, :] = grad.astype(BF)
            row = part(zv, c)[here, :]
            grad = grad * silu_slope(affine(row, part(co, c), 6, 7))
            add_sums(part(acc, c), 0, grad)
            add_sums(part(acc, c), 1, grad * affine(row, part(co, c), 8, 9))

    for m, read in enumerate(reads):
        read.wait()
        each_row(m, ch, each)
        io.put_tile(ev, e, m)
        if m == 0:
            wait(w_read, cot_read)
        gv[tile_at(m), :] = jnp.dot(ev[tile_at(m), :], wv[...], preferred_element_type=F32)
        wait(*later[m])
        each_pair(m, ch, post)
        io.put_tile(ov, out, m)
    put_sums(acc, info, pay, 0)
    io.finish()


def trunk_back_kernel(
    rows, which, top, info, cnt, place, params, g, z, recv_g, recv_z, stats, sums, x, xstats, before, pieces,
    e, far, pay, norms, out, zv, kv, sv, tv, xv, xsv, ev, wv, taps, mk, co, acc, *rest
):
    io = Copies(rest[-1])
    small = [io.start(stats, sv), io.start(xstats, xsv), io.start(recv_z, kv)]
    gv = rest[:-1]
    reads = list(zip(*[io.tiles(a, b, rows) for a, b in zip((*g, z), (*gv, zv))]))
    w_reads = io.weights(pieces, place, wv)
    x_reads = io.tiles(x, xv, rows)
    acc[...] = jnp.zeros_like(acc)
    make_masks(mk, info)
    wait(*small)
    norm_coefs(co, 0, sv, params, which, cnt, info)
    grad_coefs(co, 4, 0, settle(sums, tv), cnt, info)
    norm_coefs(co, 6, xsv, params, which - 1, cnt, info)
    norms[...] = before[...]
    put_norms(norms, which, tv)

    ch = z.shape[1]

    def grad(g_refs, z_ref, here, c):
        g_row = part(g_refs[0], c)[here, :].astype(F32)
        for ref in g_refs[1:]:
            g_row = g_row + part(ref, c)[here, :].astype(F32)
        z_row = part(z_ref, c)[here, :]
        if top:
            g_row = g_row * silu_slope(affine(z_row, part(co, c), 0, 1))
        return grad_row(g_row, z_row, part(co, c), 0, 4)

    def each(r, c):
        row = grad(gv, zv, row_at(r), c)
        part(ev, c)[row_at(r), :] = row.astype(BF)
        put_row(part(taps, c), r + 1, row, mk)

    for m, pair in enumerate(reads):
        wait(*pair)
        each_row(m, ch, each)
        io.put_tile(ev, e, m)
    put_halo(taps, lambda c: grad((recv_g,), kv, slice(0, COLS), c), mk, info, rows)
    wait(*w_reads)

    def post(r, c):
        here = row_at(r)
        row = part(xv, c)[here, :]
        value = part(out, c)[here, :] * silu_slope(affine(row, part(co, c), 6, 7))
        part(out, c)[here, :] = value
        add_sums(part(acc, c), 0, value)
        add_sums(part(acc, c), 1, value * affine(row, part(co, c), 8, 9))

    for m in range(rows // TILE_ROWS):
        out[tile_at(m), :] = conv_tile(taps, wv, m * TILE_ROWS, TILE_ROWS, True)
        x_reads[m].wait()
        each_row(m, ch, post)
        io.put_tile(out, far, m)
    put_edge(pay, out, info, rows)
    put_sums(acc, info, pay, COLS)
    io.finish()


def wide_quarter(rows, quarter):
    width = rows * COLS
    return jnp.concatenate(
        [quarter[t % 3, (t // 3) * COLS : (t // 3) * COLS + width, :] for t in range(TAPS)], axis=1
    )


def last_grad_kernel(
    rows, info, place, cnt, params, g, z, recv_g, recv_z, stats, sums, quarter, before,
    e, gains, biases, mine, other, *rest
):
    io = Copies(rest[-1])
    g, g_reads, rest = bring(io, g, rest, 9, rows)
    zv, kv, sv, tv, av, ev, wv, co, _ = rest
    small = [io.start(stats, sv), io.start(recv_z, kv)]
    reads = io.tiles(z, zv, rows)
    a_read = io.start(quarter, av)
    wait(*small)
    norm_coefs(co, 0, sv, params, 0, cnt, info)
    grad_coefs(co, 4, 0, settle(sums, tv), cnt, info)
    gains[0:1, :] = tv[2:3, :] + tv[3:4, :]
    biases[0:1, :] = tv[0:1, :] + tv[1:2, :]
    gains[1:3, :] = before[1:3, :]
    biases[1:3, :] = before[4:6, :]

    def grad(g_ref, z_ref, here, c):
        return grad_row(part(g_ref, c)[here, :], part(z_ref, c)[here, :], part(co, c), 0, 4)

    def each(r, c):
        part(ev, c)[row_at(r + 1), :] = grad(g, zv, row_at(r), c).astype(BF)

    for m, read in enumerate(reads):
        wait(read, *g_reads[m])
        each_row(m, g.shape[1], each)
    for c in range(g.shape[1] // LANES):
        row = keep_large(grad(recv_g, kv, slice(0, COLS), c), info).astype(BF)
        part(ev, c)[row_at(jnp.where(info[6] == 1, 0, rows + 1)), :] = row
        part(ev, c)[row_at(jnp.where(info[6] == 1, rows + 1, 0)), :] = jnp.zeros_like(row)
    io.put(ev, e)
    a_read.wait()
    wv[...] = lax.dot_general(
        ev[COLS : (rows + 1) * COLS, :], wide_quarter(rows, av), TN, preferred_element_type=F32
    ).astype(BF)
    if other is None:
        io.put(wv, mine)
    else:
        size = mine.shape[0] // 4
        for k, mask in enumerate((0, 2, 1, 3)):
            for side, dst in ((0, mine), (1, other)):
                block = info[10] ^ (2 * mask + side)
                src = wv.at[pl.ds(pl.multiple_of(block * size, size), size)]
                io.put(src, dst.at[pl.ds(k * size, size)])
    io.finish()


def whole_last_grad_kernel(rows, *refs):
    last_grad_kernel(rows, *refs[:16], None, *refs[16:])


def last_conv_kernel(m, high, info, place, e, pieces, *refs):
    out, ev, ov, wv, taps, mk, sems = refs[-7:]
    io = Copies(sems)
    read = io.start(e.at[pl.ds(m * high * COLS, (high + 2) * COLS)], ev)
    w_reads = io.weights(pieces, place, wv)
    make_masks(mk, info)
    read.wait()
    loop(
        high + 2,
        lambda r: all_parts(
            ev.shape[1], lambda c: put_row(part(taps, c), r, part(ev, c)[row_at(r), :].astype(F32), mk)
        ),
    )
    wait(*w_reads)
    step = high // 3
    for k in range(3):
        here = pl.ds(k * step * COLS, step * COLS)
        ov[here, :] = conv_tile(taps, wv, k * step, step, True)
        io.put(ov.at[here], out.at[pl.ds((m * high + k * step) * COLS, step * COLS)])
    io.finish()


def trunk_wgrad_kernel(rows, place, quarter, e, *rest):
    parts, av, ev, ov, sems = rest[-5:]
    io = Copies(sems)
    reads = [io.start(quarter, av), io.start(e, ev)]
    wait(*reads)
    ov[...] = lax.dot_general(ev[...], wide_quarter(rows, av), TN, preferred_element_type=F32).astype(BF)
    width = ov.shape[1]
    io.put(ov, parts.at[:, pl.ds(place * width, width)])
    io.finish()


def branch_wgrad_kernel(rows, taps, ey, p, eq, low, eu, out, tv, yv, pv, qv, lv, uv, ov, sems):
    width = rows * COLS
    channels = ey.shape[1]
    io = Copies(sems)
    y_read = io.start(ey, yv)
    t_reads = [io.start(taps.at[k], tv.at[k]) for k in range(3)]
    reads = [io.start(p, pv), io.start(eq, qv), io.start(low.at[pl.ds(0, width)], lv), io.start(eu, uv)]
    y_read.wait()

    def emit(at, e, a):
        here = pl.ds(at * channels, channels)
        ov[:, here] = lax.dot_general(e, a, TN, preferred_element_type=F32).astype(BF)
        io.put(ov.at[:, here], out.at[:, here])

    for dj in range(3):
        t_reads[dj].wait()
        for di in range(3):
            emit(3 * di + dj, yv[...], tv[dj, di * COLS : di * COLS + width, :])
    wait(*reads)
    emit(TAPS, uv[...], lv[...])
    emit(TAPS + 1, qv[...], pv[...])
    io.finish()


def trunk_result_kernel(tasks, parts, *refs):
    outs = refs[:-1]
    quarter = parts[0].shape[1] // (TAPS * len(outs))
    for k in range(4):
        ref = parts[k]
        there = pl.ds(pl.multiple_of(tasks[k] * quarter, quarter), quarter)
        for layer, out in enumerate(outs):
            for t in range(TAPS):
                start = (layer * TAPS + t) * quarter
                out[t, :, there] = ref[:, start : start + quarter].astype(F32)


def branch_result_kernel(
    tasks, norm_tasks, parts, norms, features, out, in_out, mask_out, gains, biases, pools, fv, sems
):
    io = Copies(sems)
    read = io.start(features.at[pl.ds(0, TASKS)], fv)
    channels = in_out.shape[2]
    for k in range(4):
        ref = parts[k]
        task = tasks[k]

        @pl.when(task < TASKS)
        def _():
            for t in range(TAPS + 2):
                block = ref[:, t * channels : (t + 1) * channels].astype(F32)
                if t < TAPS:
                    out[task, t] = block
                elif t == TAPS:
                    in_out[task] = block
                else:
                    mask_out[task] = block

        @pl.when(norm_tasks[k] < TASKS)
        def _():
            gains[norm_tasks[k]] = norms[k][0:3, :]
            biases[norm_tasks[k]] = norms[k][3:6, :]

    read.wait()
    io.put(fv, pools)
    io.finish()


VMEM = pl.BlockSpec(memory_space=pltpu.VMEM)
VMEM_LIMIT = 28 * MIB


class Near:
    def __init__(self, value):
        self.value = value


class Far(Near):
    pass


class Free:
    def __init__(self, value):
        self.value = value


def frees(values):
    return [Free(value) for value in values]


def nears(values):
    return [Near(value) for value in values]


def bytes_of(a):
    return math.prod(a.shape) * jnp.dtype(a.dtype).itemsize


def run(kernel, ins, outs, scratch, flops=0, copies=64, near=False, deps=(), aliases=None):
    flat, specs, groups = [], [], []
    for item in ins:
        parts = list(item) if isinstance(item, (list, tuple)) else [item]
        groups.append(len(parts) if isinstance(item, (list, tuple)) else 0)
        for part in parts:
            kept, free = near or isinstance(part, Near), isinstance(part, Free)
            kept = kept and not isinstance(part, Far)
            part = part.value if isinstance(part, (Near, Free)) else part
            if part.ndim == 1:
                specs.append(SMEM)
                part = pltpu.with_memory_space_constraint(part, pltpu.HBM)
            elif free:
                specs.append(ANY)
            elif kept:
                specs.append(VMEM)
                if not near:
                    part = pltpu.with_memory_space_constraint(part, pltpu.VMEM)
            else:
                specs.append(HBM)
                part = pltpu.with_memory_space_constraint(part, pltpu.HBM)
            flat.append(part)
    shapes, out_specs = [], []
    for item in outs:
        kept = (near or isinstance(item, Near)) and not isinstance(item, Far)
        item = item.value if isinstance(item, Near) else item
        if not near:
            item = (pltpu.VMEM if kept else pltpu.HBM)(item.shape, item.dtype)
        shapes.append(item)
        out_specs.append(VMEM if kept else HBM)
    size = sum(bytes_of(a) for a in flat) + sum(bytes_of(o) for o in shapes)
    count = len(flat)

    def body(*refs):
        rest, args = list(refs[:count]), []
        for group in groups:
            if group:
                args.append(tuple(rest[:group]))
                rest = rest[group:]
            else:
                args.append(rest.pop(0))
        kernel(*args, *refs[count + len(deps) :])

    return pl.pallas_call(
        body,
        out_shape=shapes,
        in_specs=specs + [ANY if isinstance(d, Free) else HBM for d in deps],
        out_specs=out_specs,
        scratch_shapes=list(scratch) + [pltpu.SemaphoreType.DMA((copies,))],
        input_output_aliases=aliases or {},
        compiler_params=pltpu.CompilerParams(vmem_limit_bytes=VMEM_LIMIT),
        cost_estimate=pl.CostEstimate(flops=flops, bytes_accessed=size, transcendentals=0),
    )(*flat, *(d.value if isinstance(d, Free) else pltpu.with_memory_space_constraint(d, pltpu.HBM) for d in deps))


def after(value, *others):
    return pl.pallas_call(
        lambda *refs: None,
        out_shape=jax.ShapeDtypeStruct(value.shape, value.dtype),
        in_specs=[HBM] + [ANY] * len(others),
        out_specs=HBM,
        input_output_aliases={0: 0},
    )(value, *others)


def swap(value, axis, mask):
    pairs = [(i, i ^ mask) for i in range(lax.axis_size(axis))]
    return lax.ppermute(value, axis, pairs)


def cross(value, second):
    tasks, width = lax.axis_size("task"), lax.axis_size("dp")
    pairs = []
    for t in range(tasks):
        for d in range(width):
            mask = 1 if (d + second) % 2 == 0 else 2
            pairs.append((t * width + d, (t ^ mask) * width + d))
    return lax.ppermute(value, ("task", "dp"), pairs)


def all_of(value, axis, unit):
    if lax.axis_size(axis) == 4 * unit:
        return [value] + [swap(value, axis, unit * k) for k in (1, 2, 3)]
    mask = unit
    while mask < lax.axis_size(axis):
        value = value + swap(value, axis, mask)
        mask *= 2
    return [value]


def total(parts):
    return (parts[0] + parts[1]) + (parts[2] + parts[3]) if len(parts) == 4 else parts[0]


def sum_parts(pay):
    return all_of(pay + swap(pay, "dp", 1), "dp", 2)


def exchange(pay):
    recv = swap(pay, "dp", 1)
    return recv, all_of(pay[COLS:] + recv[COLS:], "dp", 2)


def join(*parts):
    return jnp.concatenate(parts, axis=0)


def gather_column(part, *others):
    far = swap(part, "dp", 6)
    return join(part, swap(part, "dp", 2), swap(part, "dp", 4), after(far, *others) if others else far)


def plane(part, *others):
    first, second = cross(part, 0), cross(part, 1)
    return [part, first, second, cross(after(first, *others) if others else first, 1)]


def gather_core(parts):
    return parts + [swap(part, "dp", 1) for part in parts]


def domain_counts(size_class, domain_tags):
    big_area = HEIGHT * WIDTH
    small_area = BAND * HALF_WIDTH
    ones_count = jnp.sum(
        jnp.where(
            size_class == 0, big_area * domain_tags[:, 0], small_area * jnp.sum(domain_tags, axis=1)
        )
    )
    all_count = size_class.shape[0] * big_area
    return jnp.maximum(jnp.stack([all_count - ones_count, ones_count]).astype(F32), 1.0)


def on_device(
    images,
    conv_first,
    conv_second,
    conv_third,
    trunk_gains,
    trunk_biases,
    attend_in,
    attend_mask,
    attend_out,
    branch_gains,
    branch_biases,
    size_class,
    domain_tags,
    trunk_cotangent,
    task_cotangent,
):
    rows, cols, ch = images.shape
    pixels = rows * cols
    position = lax.axis_index("dp")
    task_index = lax.axis_index("task")
    width = lax.axis_size("dp")
    task_count = lax.axis_size("task")
    quarter = ch // task_count
    own_out = ch // width
    by_permute = width == 8 and task_count == 4 and own_out == task_count * PIECE
    pair_index = position // 2
    bottom = position % 2
    local_class = lax.dynamic_slice_in_dim(size_class, pair_index * CANVAS, CANVAS, 0)
    local_tags = lax.dynamic_slice_in_dim(domain_tags, pair_index * CANVAS, CANVAS, 0)
    side = jnp.arange(GROUPS) % 2
    slot_class = jnp.repeat(local_class, 2)
    slot_tags = jnp.repeat(local_tags, 2, axis=0)
    which = jnp.where(slot_class == 1, bottom * 2 + side, 0)
    groups = jnp.sum(slot_tags * (jnp.arange(4)[None, :] == which[:, None]), axis=1)
    active = (task_index < TASKS).astype(jnp.int32)
    branch = jnp.minimum(task_index, TASKS - 1)
    info = jnp.concatenate(
        [groups, local_class, jnp.stack([bottom, task_index, active, branch, position])]
    ).astype(jnp.int32)
    cnt = domain_counts(size_class, domain_tags)

    def shape(dims, dtype=F32):
        return jax.ShapeDtypeStruct(dims, dtype)

    z_index, core = position // 2, position % 2
    masks_of = (jnp.where(core == 0, 1, 2), jnp.where(core == 0, 2, 1))
    places = []
    for side_core, (m1, m2) in ((core, masks_of), (1 - core, masks_of[::-1])):
        for t in (task_index, task_index ^ m1, task_index ^ m2, task_index ^ m1 ^ m2):
            for zz in (z_index, z_index ^ 1, z_index ^ 2, z_index ^ 3):
                places.append((2 * zz + side_core) * own_out + t * (own_out // task_count))
    place = jnp.stack(places).astype(jnp.int32)
    pieces_of_task = [task_index, task_index ^ masks_of[0], task_index ^ masks_of[1], task_index ^ 3]
    task_order = jnp.stack(pieces_of_task).astype(jnp.int32)
    norm_order = jnp.stack([task_index ^ k for k in range(4)]).astype(jnp.int32)
    spot = jnp.stack([task_index, branch]).astype(jnp.int32)

    def by_tap(kernel):
        kernel = jnp.swapaxes(kernel, -1, -2)
        tasks = kernel.shape[:1] if kernel.ndim % 2 else ()
        return kernel.reshape(tasks + (-1,) + kernel.shape[-2:])

    def cast(sources, out_rows, pick, deps=()):
        sources = [by_tap(k) for k in sources]
        taps_of = [k.shape[-3] for k in sources]
        (out,) = pl.pallas_call(
            functools.partial(cast_kernel, pick, len(sources)),
            out_shape=[shape((out_rows, sum(taps_of) * ch), BF)],
            in_specs=[SMEM] + [HBM] * len(sources) + [ANY] * len(deps),
            out_specs=[VMEM],
            scratch_shapes=[pltpu.VMEM((n, out_rows, ch), F32) for n in taps_of]
            + [pltpu.SemaphoreType.DMA((len(sources),))],
            compiler_params=pltpu.CompilerParams(vmem_limit_bytes=VMEM_LIMIT),
        )(spot, *(pltpu.with_memory_space_constraint(k, pltpu.HBM) for k in sources), *deps)
        return out

    def pick(values):
        return lax.dynamic_index_in_dim(values, branch, 0, keepdims=False)

    params = jnp.concatenate(
        [trunk_gains, pick(branch_gains), trunk_biases, pick(branch_biases), jnp.zeros((4, ch), F32)]
    )
    flat = images.reshape(pixels, ch)
    edge = jnp.where(bottom == 1, flat[:COLS], flat[pixels - COLS :])
    gather = functools.partial(lax.all_gather, axis_name="dp", axis=0, tiled=True)
    halo = swap(edge, "dp", 1)
    cast_pair = cast([attend_in, attend_mask], own_out, False)
    cast_out = cast([attend_out], own_out, False)
    early = [Free(halo)]
    if by_permute:
        casts = [cast([conv_third], PIECE, True), cast_pair, cast_out, halo]
        column_1 = gather_column(cast([conv_first], PIECE, True), *casts)
        first, second = cross(column_1, 0), cross(column_1, 1)
        plane_1 = [column_1, first, second, cross(after(first, second), 1)]
        weights_1 = gather_core(plane_1)
        weights_2 = [gather(after(cast([conv_second], own_out, False), column_1))]
    else:
        weights_1, weights_2, weights_3 = [
            [gather(cast([k], own_out, False))] for k in (conv_first, conv_second, conv_third)
        ]
    weights = [weights_1, weights_2, None]
    w_pair = gather(cast_pair)
    w_out = gather(cast_out)

    wide = shape((pixels, ch))
    low_wide = shape((pixels, ch), BF)
    pay_shape = shape((COLS + 8, ch))
    sums_shape = shape((8, ch))
    taps_dims = (3, pixels + 2 * COLS, ch)
    v_wide = pltpu.VMEM((pixels, ch), F32)
    v_pay = pltpu.VMEM((COLS + 8, ch), F32)
    v_low = pltpu.VMEM((pixels, ch), BF)
    v_sums = pltpu.VMEM((8, ch), F32)
    v_pool = pltpu.VMEM((pixels // 4, ch), BF)
    v_conv = pltpu.VMEM((ch, TAPS * ch), BF)
    v_dot = pltpu.VMEM((ch, ch), BF)
    v_quarter = pltpu.VMEM((3, pixels + 2 * COLS, quarter), BF)
    taps = pltpu.VMEM(taps_dims, BF)
    masks = pltpu.VMEM((2, COLS, 128), F32)
    acc = pltpu.VMEM((2, GROUPS, 8, ch), F32)
    buf = pltpu.VMEM((ch // 128, COLS, 128), F32)

    def coefs(blocks):
        return pltpu.VMEM((4 * blocks, ch), F32)

    conv_flops = 2 * TAPS * pixels * ch * ch
    dot_flops = 2 * pixels * ch * ch

    quarter_shape = shape((3, pixels + 2 * COLS, quarter), BF)
    z, recv, stats, quarters = [], [], [], []
    outs = [wide, Near(wide), Near(pay_shape), quarter_shape]
    near = None
    kept = []
    for layer in range(3):
        if layer == 0:
            values, near, pay, part = run(
                functools.partial(first_conv_kernel, rows),
                [info, place, flat, Near(halo), weights_1],
                outs, [v_low, v_conv, taps, masks, acc], conv_flops, deps=early,
            )
            if by_permute:
                column_3 = gather_column(after(casts[0], weights_1[4]), pay)
                first, second = cross(column_3, 0), cross(column_3, 1)
        else:
            values, near, pay, part, held = run(
                functools.partial(conv_kernel, rows, layer - 1),
                [info, cnt, place, Near(params), Near(near) if layer == 2 else z[-1], Near(recv[-1]), nears(stats[-1]), weights[layer]],
                outs + [sums_shape],
                ([] if layer == 2 else [v_wide]) + [v_sums, v_conv, taps, masks, acc, coefs(4)], conv_flops,
            )
            kept.append(held)
            if layer == 1:
                if by_permute:
                    plane_3 = [column_3, first, second, cross(after(first, second, pay), 1)]
                    weights[2] = gather_core(plane_3)
                else:
                    weights[2] = weights_3
        got, found = exchange(pay)
        z.append(values)
        recv.append(got)
        stats.append(found)
        quarters.append(part)

    low, trunk_pool, u, near, pay, held = run(
        functools.partial(enter_kernel, rows, 2),
        [info, cnt, Near(params), z[2], Near(recv[2]), nears(stats[2]), w_pair],
        [shape((pixels + COLS, ch), BF), shape((pixels // 4, ch), BF), wide, Near(wide), Near(sums_shape),
         sums_shape],
        [v_wide, v_sums, v_dot, pltpu.VMEM((pixels + COLS, ch), BF), v_pool, acc,
         coefs(4), buf], dot_flops,
    )
    kept.append(held)
    u_stats = sum_parts(pay)
    p, q, near, pay, u_kept = run(
        functools.partial(mask_kernel, rows, 3),
        [info, cnt, Near(params), Near(near), nears(u_stats), w_pair],
        [low_wide, wide, Near(wide), Near(pay_shape), sums_shape],
        [v_sums, v_dot, v_low, acc, coefs(4)], dot_flops,
    )
    q_recv, q_stats = exchange(pay)
    y, near, pay, masked_taps, q_kept = run(
        functools.partial(branch_conv_kernel, rows, 4),
        [info, cnt, Near(params), low, q, Near(q_recv), nears(q_stats), w_out],
        [wide, Near(wide), Near(pay_shape), shape(taps_dims, BF), sums_shape],
        [v_wide, pltpu.VMEM((pixels + COLS, ch), BF), v_sums, v_conv, taps, masks, acc, coefs(4)], conv_flops,
    )
    y_recv, y_stats = exchange(pay)

    branch_pool, near, pay, y_kept = run(
        functools.partial(turn_kernel, rows, 5),
        [info, cnt, Near(params), Near(near), nears(y_stats), task_cotangent.reshape(TASKS, pixels // 4, ch)],
        [shape((pixels // 4, ch), BF), wide, Near(pay_shape), sums_shape],
        [v_wide, v_sums, v_pool, v_pool, acc, coefs(4), buf],
    )
    task_features = lax.all_gather(branch_pool, "task")
    gy_recv, y_sums = exchange(pay)
    e_y, near, gs, pay, norms = run(
        functools.partial(branch_back_kernel, rows),
        [info, cnt, Near(params), near, y, Near(gy_recv), y_recv, y_kept, nears(y_sums), w_out, low, q,
         q_kept],
        [low_wide, Near(wide), wide, Near(sums_shape), Near(sums_shape)],
        [v_wide, v_wide, v_pay, v_sums, v_sums, v_sums, v_low, v_wide, v_low, v_conv,
         taps, masks, acc, coefs(10)], conv_flops,
    )
    q_sums = sum_parts(pay)
    e_q, near, pay, norms = run(
        functools.partial(mask_back_kernel, rows),
        [info, cnt, Near(params), Near(near), q, q_kept, nears(q_sums), w_pair, u, u_kept, Near(norms)],
        [low_wide, Near(wide), Near(sums_shape), Near(sums_shape)],
        [v_wide, v_wide, v_sums, v_sums, v_sums, v_dot, v_low, acc, coefs(10)], dot_flops,
    )
    u_sums = sum_parts(pay)
    e_u, grad_shared, pay, norms = run(
        functools.partial(leave_kernel, rows),
        [info, cnt, Near(params), Near(near), u, u_kept, nears(u_sums), w_pair, gs, z[2], kept[2],
         trunk_cotangent.reshape(pixels // 4, ch), Near(norms)],
        [low_wide, low_wide, Near(sums_shape), Near(sums_shape)],
        [v_wide, v_wide, v_sums, v_sums, v_sums, v_dot, v_wide, v_wide, v_pool, v_low, v_low, acc,
         coefs(10), buf], dot_flops,
    )
    sums = all_of(total(sum_parts(pay)), "task", 1)
    norm_parts = [norms] + [swap(norms, "task", k) for k in (1, 2, 3)]
    grad_half = grad_shared + after(cross(grad_shared, 0), *sums, *norm_parts, task_features)
    grad_rest = cross(grad_half, 1)
    (branch_part,) = run(
        functools.partial(branch_wgrad_kernel, rows),
        [masked_taps, e_y, p, e_q, low, e_u],
        [shape((ch, 11 * ch), BF)],
        [taps, v_low, v_low, v_low, v_low, v_low, pltpu.VMEM((ch, 11 * ch), BF)], conv_flops, deps=[grad_half],
    )
    branch_part = after(branch_part, grad_rest)
    branch_part = lax.psum_scatter(branch_part, "dp", scatter_dimension=0, tiled=True)

    edge = jnp.where(
        bottom == 1, grad_half[:COLS] + grad_rest[:COLS], grad_half[-COLS:] + grad_rest[-COLS:]
    )
    g, g_recv = [grad_half, grad_rest], swap(edge, "dp", 1)
    trunk_norms = jnp.zeros((8, ch), F32)
    for layer in (2, 1):
        top = layer == 2
        e, near, pay, trunk_norms = run(
            functools.partial(trunk_back_kernel, rows, layer, top),
            [info, cnt, place, Near(params), g, z[layer], Near(g_recv), recv[layer], kept[layer], nears(sums),
             z[layer - 1], kept[layer - 1], Near(trunk_norms), weights[layer]],
            [low_wide, wide, Near(pay_shape), Near(sums_shape)],
            [v_wide, v_wide, v_pay, v_sums, v_sums, v_wide, v_sums, v_low, v_conv, taps, masks, coefs(10), acc] + ([v_low, v_low] if top else [v_wide]), conv_flops,
            deps=() if top else [trunk_part],
        )
        g_recv, sums = exchange(pay)
        g = [near]
        (trunk_part,) = run(
            functools.partial(trunk_wgrad_kernel, rows, layer - 1),
            [quarters[layer], e] + ([] if top else [trunk_part]), [shape((ch, 2 * TAPS * quarter), BF)],
            [v_quarter, v_low, pltpu.VMEM((ch, TAPS * quarter), BF)], conv_flops // 4,
            deps=() if top else frees(sums[:2]), aliases=None if top else {2: 0},
        )

    later_part = lax.psum_scatter(trunk_part, "dp", scatter_dimension=0, tiled=True)
    half_out = shape((ch // 2, TAPS * quarter), BF)
    last_kernel = functools.partial(last_grad_kernel, rows)
    if not by_permute:
        last_kernel = functools.partial(whole_last_grad_kernel, rows)
    e, trunk_gains_grad, trunk_biases_grad, *halves = run(
        last_kernel,
        [info, place, cnt, Near(params), g[0], z[0], Near(g_recv), recv[0], kept[0], nears(sums), quarters[0],
         Near(trunk_norms)],
        [shape((pixels + 2 * COLS, ch), BF), Near(shape((3, ch))), Near(shape((3, ch)))]
        + ([half_out, half_out] if by_permute else [shape((ch, TAPS * quarter), BF)]),
        [v_wide, v_wide, v_pay, v_sums, v_sums, v_quarter, pltpu.VMEM((pixels + 2 * COLS, ch), BF),
         pltpu.VMEM((ch, TAPS * quarter), BF), coefs(10)], conv_flops // 4, deps=[trunk_part],
    )

    high = rows // 2
    tile = high * COLS

    def input_grad(m, before, deps):
        ins = [info, place, e, weights[0]] + before
        (out,) = run(
            functools.partial(last_conv_kernel, m, high), ins, [wide],
            [pltpu.VMEM((tile + 2 * COLS, ch), BF), pltpu.VMEM((tile, ch), F32), v_conv,
             pltpu.VMEM((3, tile + 2 * COLS, ch), BF), masks], conv_flops // 2, deps=deps,
            aliases={3 + len(weights[0]): 0} if before else None,
        )
        return [out]

    if by_permute:
        mine, other = halves
        half = mine.shape[0] // 2
        got = swap(other, "dp", 1)
        branch_part = after(branch_part, got)
        branch_first, branch_second = cross(branch_part, 0), cross(branch_part, 1)
        images_grad = input_grad(0, [], [Free(got)])
        send, keep = mine[half:] + got[half:], mine[:half] + got[:half]
        got = after(swap(send, "dp", 2), images_grad[0], branch_first, branch_second)
        images_grad = input_grad(1, images_grad, [Free(got)])
        branch_third = cross(branch_first, 1)
        half = half // 2
        send, keep = keep[half:] + got[half:], keep[:half] + got[:half]
        got = after(swap(send, "dp", 4), images_grad[0], branch_third)
        first_part = keep + got
        trunk_parts = plane(jnp.concatenate([first_part, later_part], axis=1))
        branch_parts = [branch_part, branch_first, branch_second, branch_third]
        result_deps = [Free(trunk_parts[1])]
    else:
        first_part = lax.psum_scatter(halves[0], "dp", scatter_dimension=0, tiled=True)
        images_grad, result_deps = [], []
        for m in range(2):
            images_grad = input_grad(m, images_grad, [])
        trunk_parts = plane(jnp.concatenate([first_part, later_part], axis=1))
        branch_parts = plane(branch_part)
    images_grad = images_grad[0]
    out_grad, in_grad, mask_grad, branch_gains_grad, branch_biases_grad, pools = run(
        branch_result_kernel,
        [task_order, norm_order, branch_parts, norm_parts,
         Far(task_features)],
        [shape((TASKS, TAPS, own_out, ch)), shape((TASKS, own_out, ch)), shape((TASKS, own_out, ch)),
         shape((TASKS, 3, ch)), shape((TASKS, 3, ch)), Far(shape((TASKS, pixels // 4, ch), BF))],
        [pltpu.VMEM((TASKS, pixels // 4, ch), BF)], near=True, deps=result_deps,
    )
    grad_shape = shape((TAPS, own_out, ch))
    grads = run(trunk_result_kernel, [task_order, trunk_parts], [grad_shape] * 3, [], near=True)
    kernel_grads = [
        jnp.swapaxes(k.reshape(3, 3, own_out, ch), 2, 3) for k in grads
    ]
    return (
        trunk_pool.reshape(rows // 2, cols // 2, ch),
        pools.reshape(TASKS, rows // 2, cols // 2, ch),
        images_grad.reshape(rows, cols, ch),
        *kernel_grads,
        trunk_gains_grad,
        trunk_biases_grad,
        jnp.swapaxes(in_grad, 1, 2),
        jnp.swapaxes(mask_grad, 1, 2),
        jnp.swapaxes(out_grad.reshape(TASKS, 3, 3, own_out, ch), 3, 4),
        branch_gains_grad,
        branch_biases_grad,
    )


def solution(mesh):
    in_specs = (
        P("dp", None, None),
        P(None, None, None, "dp"),
        P(None, None, None, "dp"),
        P(None, None, None, "dp"),
        P(),
        P(),
        P(None, None, "dp"),
        P(None, None, "dp"),
        P(None, None, None, None, "dp"),
        P(),
        P(),
        P(),
        P(),
        P("dp", None, None),
        P(None, "dp", None, None),
    )
    out_specs = (
        P("dp", None, None),
        P(None, "dp", None, None),
        P("dp", None, None),
        P(None, None, None, "dp"),
        P(None, None, None, "dp"),
        P(None, None, None, "dp"),
        P(),
        P(),
        P(None, None, "dp"),
        P(None, None, "dp"),
        P(None, None, None, None, "dp"),
        P(),
        P(),
    )
    return jax.shard_map(
        on_device, mesh=mesh, in_specs=in_specs, out_specs=out_specs, check_vma=False
    )
```

time: 537 us -> 521 us (0.970)
  starting transfers between devices: 106 us -> 87.2 us
  other arithmetic: 21.6 us -> 15.3 us
    ppermute x17 -> x14, waiting for transfers between devices: 35.5 us -> 53.2 us  [cross(): return lax.ppermute(value, ('task', 'dp'), pairs)]
    ppermute x73, starting transfers between devices: 87 us -> 70.9 us  [swap(): return lax.ppermute(value, axis, pairs)]
    ppermute x73, waiting for transfers between devices: 96.1 us -> 82.3 us  [swap(): return lax.ppermute(value, axis, pairs)]
    pallas_call x22 -> x20, Pallas kernels: 217 us -> 222 us  [run(): pl.pallas_call(body, out_shape=shapes, in_specs=specs + [ANY if isinstanc...]
    add x8, other arithmetic: 6.27 us -> 0.78 us  [exchange(): return (recv, all_of(pay[COLS:] + recv[COLS:], 'dp', 2))]
    ppermute x17 -> x14, starting transfers between devices: 18.3 us -> 16.1 us  [cross(): return lax.ppermute(value, ('task', 'dp'), pairs)]
    unnamed x215 -> x136, local copies, waits for them, and re-layouts: 23.5 us -> 23 us
  transfers between devices with their start and end apart: 96 -> 93, of which waited for: 48 -> 46; matrix products, arithmetic and copies ran while one was open for 4% -> 3% of each run, Pallas kernels for 36% -> 40%
where the time goes in v3:
time: 521 us; the launch traced here: 513 us
  Pallas kernels  232 us (45%)
  waiting for transfers between devices  137 us (26%)
  starting transfers between devices  87.2 us (17%)
  local copies, waits for them, and re-layouts  25.3 us (5%)
  between operations  16 us (3%)
  other arithmetic  15.3 us (3%)
    pallas_call x20, Pallas kernels, run(): pl.pallas_call(body, out_shape=shapes, in_specs=specs + [ANY if isinstanc...  222 us
    ppermute x73, waiting for transfers between devices, swap(): return lax.ppermute(value, axis, pairs)  82.3 us
    ppermute x73, starting transfers between devices, swap(): return lax.ppermute(value, axis, pairs)  70.9 us
    ppermute x14, waiting for transfers between devices, cross(): return lax.ppermute(value, ('task', 'dp'), pairs)  53.2 us
    unnamed x136, local copies, waits for them, and re-layouts  23 us
    ppermute x14, starting transfers between devices, cross(): return lax.ppermute(value, ('task', 'dp'), pairs)  16.1 us
  transfers between devices with their start and end apart: 93, of which 46 were waited for; matrix products, arithmetic and copies ran while one was open for 3% of the time, Pallas kernels for 40%

profile of v3, /device:TPU:0, one launch (start us, length us, event | category | flops | bytes accessed | tf_op | source)
XLA Modules:
  0.0 513.2 jit_solution(11833100187223865151)
XLA Ops:
  8.8 5.1 collective-permute-start.3
  17.8 2.7 shard_map.249.refs_3_
  20.5 1.9 shard_map.253.refs_0_
  23.3 2.2 shard_map.248.refs_2_
  26.8 1.8 pad_maximum_fusion.refs_4_.refs_1_.refs_3_
  33.4 12.2 %collective-permute-done.4.refs_5_.refs_4_ = bf16[64,4608]{1,0:T(8,128)(2,1)S(1)} collective-permute-done((bf16[64,4608]{1,0:T(8,128)(2,1)S(1)}, bf16[64,4608]{1,0:T(8,128)(2,1)S(1)}, u32[]{:S(2)}, u32[]{:S(2)}) %collective-permute-start.4) | collective-permute-done | bytes 589856 | tf_op jit(solution)/shard_map/ppermute | solution.py:992
  47.2 2.2 collective-permute-start.6
  49.9 7.7 %collective-permute-done.6.refs_7_.refs_6_ = bf16[64,4608]{1,0:T(8,128)(2,1)} collective-permute-done((bf16[64,4608]{1,0:T(8,128)(2,1)}, bf16[64,4608]{1,0:T(8,128)(2,1)}, u32[]{:S(2)}, u32[]{:S(2)}) %collective-permute-start.6) | collective-permute-done | bytes 589856 | tf_op jit(solution)/shard_map/ppermute | solution.py:992
  60.3 3.8 collective-permute-start.21
  64.7 15.5 %shard_map.252 = (f32[1728,512]{1,0:T(8,128)}, f32[1728,512]{1,0:T(8,128)}, f32[104,512]{1,0:T(8,128)S(1)}, bf16[3,1920,128]{2,1,0:T(8,128)(2,1)}) custom-call(s32[11]{0:T(128)} %concatenate.15.refs_0_, s32[32]{0:T(128)} %stack.196.refs_1_.refs_2_, bf16[1728,512]{1,0:T(8,128)(2,1)} %bitcast.102, bf16[96,512]{1,0:T(8,128)(2,1)S(1)} %copy-done.21, ...), custom_call_target="tpu_custom_call" | custom-call | flops 8153726976 | bytes 15351980 | tf_op jit(solution)/shard_map/pallas_call | solution.py:958
  81.6 10.0 %collective-permute-done.20 = bf16[16,4608]{1,0:T(8,128)(2,1)S(1)} collective-permute-done((bf16[16,4608]{1,0:T(8,128)(2,1)}, bf16[16,4608]{1,0:T(8,128)(2,1)S(1)}, u32[]{:S(2)}, u32[]{:S(2)}) %collective-permute-start.20) | collective-permute-done | bytes 147488 | tf_op jit(solution)/shard_map/ppermute | solution.py:982
  98.4 2.9 collective-permute-start.14
  102.7 1.8 collective-permute-start.23
  105.4 14.4 %shard_map.255 = (f32[1728,512]{1,0:T(8,128)}, f32[1728,512]{1,0:T(8,128)S(1)}, f32[104,512]{1,0:T(8,128)S(1)}, bf16[3,1920,128]{2,1,0:T(8,128)(2,1)}, f32[8,512]{1,0:T(8,128)}) custom-call(s32[11]{0:T(128)} %concatenate.15.refs_0_, f32[2]{0:T(128)} %fusion.6.refs_1_.refs_2_, s32[32]{0:T(128)} %stack.196.refs_1_.refs_2_, ...), custom_call_target="tpu_custom_call" | custom-call | flops 8153726976 | bytes 17350836 | tf_op jit(solution)/shard_map/pallas_call | solution.py:958
  120.5 1.8 copy-done.39
  124.2 9.1 %collective-permute-done.24.refs_13_.refs_20_ = bf16[64,4608]{1,0:T(8,128)(2,1)S(1)} collective-permute-done((bf16[64,4608]{1,0:T(8,128)(2,1)}, bf16[64,4608]{1,0:T(8,128)(2,1)S(1)}, u32[]{:S(2)}, u32[]{:S(2)}) %collective-permute-start.24) | collective-permute-done | bytes 589856 | tf_op jit(solution)/shard_map/ppermute | solution.py:992
  133.8 2.0 collective-permute-done.15.refs_5_.refs_7_
  135.8 1.8 collective-permute-start.17
  137.6 2.6 collective-permute-start.18
  141.3 2.2 collective-permute-done.18.refs_9_
  144.3 2.0 copy-done.40
  146.3 15.4 %shard_map.259 = (f32[1728,512]{1,0:T(8,128)}, f32[1728,512]{1,0:T(8,128)}, f32[104,512]{1,0:T(8,128)S(1)}, bf16[3,1920,128]{2,1,0:T(8,128)(2,1)}, f32[8,512]{1,0:T(8,128)}) custom-call(s32[11]{0:T(128)} %concatenate.15.refs_0_, f32[2]{0:T(128)} %fusion.6.refs_1_.refs_2_, s32[32]{0:T(128)} %stack.196.refs_1_.refs_2_, ...), custom_call_target="tpu_custom_call" | custom-call | flops 8153726976 | bytes 17350836 | tf_op jit(solution)/shard_map/pallas_call | solution.py:958
  164.1 2.4 collective-permute-start.31
  168.1 2.2 collective-permute-done.31.refs_7_
  172.0 7.5 %shard_map.260 = (bf16[1824,512]{1,0:T(8,128)(2,1)}, bf16[432,512]{1,0:T(8,128)(2,1)}, f32[1728,512]{1,0:T(8,128)}, f32[1728,512]{1,0:T(8,128)S(1)}, f32[8,512]{1,0:T(8,128)S(1)}, /*index=5*/f32[8,512]{1,0:T(8,128)}) custom-call(s32[11]{0:T(128)} %concatenate.15.refs_0_, f32[2]{0:T(128)} %fusion.6.refs_1_.refs_2_, ...), custom_call_target="tpu_custom_call" | custom-call | flops 905969664 | bytes 14319668 | tf_op jit(solution)/shard_map/pallas_call | solution.py:958
  182.5 2.7 collective-permute-start.36
  185.5 2.5 collective-permute-done.36.refs_7_
  188.0 7.5 %shard_map.261 = (bf16[1728,512]{1,0:T(8,128)(2,1)}, f32[1728,512]{1,0:T(8,128)}, f32[1728,512]{1,0:T(8,128)}, f32[104,512]{1,0:T(8,128)S(1)}, f32[8,512]{1,0:T(8,128)}) custom-call(s32[11]{0:T(128)} %concatenate.15.refs_0_, f32[2]{0:T(128)} %fusion.6.refs_1_.refs_2_, f32[16,512]{1,0:T(8,128)S(1)} %concatenate.16.refs_3_.refs_2_, ...), custom_call_target="tpu_custom_call" | custom-call | flops 905969664 | bytes 13762612 | tf_op jit(solution)/shard_map/pallas_call | solution.py:958
  197.1 3.2 collective-permute-start.39
  202.2 3.6 collective-permute-done.40.refs_9_
  205.8 15.7 %shard_map.262 = (f32[1728,512]{1,0:T(8,128)}, f32[1728,512]{1,0:T(8,128)S(1)}, f32[104,512]{1,0:T(8,128)S(1)}, bf16[3,1920,512]{2,1,0:T(8,128)(2,1)}, f32[8,512]{1,0:T(8,128)}) custom-call(s32[11]{0:T(128)} %concatenate.15.refs_0_, f32[2]{0:T(128)} %fusion.6.refs_1_.refs_2_, f32[16,512]{1,0:T(8,128)S(1)} %concatenate.16.refs_3_.refs_2_, ...), custom_call_target="tpu_custom_call" | custom-call | flops 8153726976 | bytes 23642164 | tf_op jit(solution)/shard_map/pallas_call | solution.py:958
  224.8 2.7 collective-permute-start.44
  227.8 2.5 collective-permute-done.44.refs_7_
  230.3 6.0 %shard_map.263 = (bf16[432,512]{1,0:T(8,128)(2,1)}, f32[1728,512]{1,0:T(8,128)}, f32[104,512]{1,0:T(8,128)S(1)}, f32[8,512]{1,0:T(8,128)}) custom-call(s32[11]{0:T(128)} %concatenate.15.refs_0_, f32[2]{0:T(128)} %fusion.6.refs_1_.refs_2_, f32[16,512]{1,0:T(8,128)S(1)} %concatenate.16.refs_3_.refs_2_, f32[1728,512]{1,0:T(8,128)S(1)} %get-tuple-element.92.refs_3_, ...), custom_call_target="tpu_custom_call" | custom-call | bytes 9175092 | tf_op jit(solution)/shard_map/pallas_call | solution.py:958
  237.8 3.2 collective-permute-start.47
  243.0 3.6 collective-permute-done.48.refs_11_
  246.6 20.4 %shard_map.264 = (bf16[1728,512]{1,0:T(8,128)(2,1)}, f32[1728,512]{1,0:T(8,128)S(1)}, f32[1728,512]{1,0:T(8,128)}, f32[8,512]{1,0:T(8,128)S(1)}, f32[8,512]{1,0:T(8,128)S(1)}) custom-call(s32[11]{0:T(128)} %concatenate.15.refs_0_, f32[2]{0:T(128)} %fusion.6.refs_1_.refs_2_, f32[16,512]{1,0:T(8,128)S(1)} %concatenate.16.refs_3_.refs_2_, ...), custom_call_target="tpu_custom_call" | custom-call | flops 8153726976 | bytes 26640436 | tf_op jit(solution)/shard_map/pallas_call | solution.py:958
  269.9 2.8 collective-permute-start.52
  273.0 2.4 collective-permute-done.52.refs_9_
  275.4 7.4 %shard_map.265 = (bf16[1728,512]{1,0:T(8,128)(2,1)}, f32[1728,512]{1,0:T(8,128)S(1)}, f32[8,512]{1,0:T(8,128)S(1)}, f32[8,512]{1,0:T(8,128)S(1)}) custom-call(s32[11]{0:T(128)} %concatenate.15.refs_0_, f32[2]{0:T(128)} %fusion.6.refs_1_.refs_2_, f32[16,512]{1,0:T(8,128)S(1)} %concatenate.16.refs_3_.refs_2_, f32[1728,512]{1,0:T(8,128)S(1)} %get-tuple-element.101.refs_3_, ...), custom_call_target="tpu_custom_call" | custom-call | flops 905969664 | bytes 17154100 | tf_op jit(solution)/shard_map/pallas_call | solution.py:958
  284.1 3.3 collective-permute-start.55
  289.3 3.7 collective-permute-done.56.refs_9_
  293.0 11.5 %shard_map.266 = (bf16[1728,512]{1,0:T(8,128)(2,1)}, bf16[1728,512]{1,0:T(8,128)(2,1)}, f32[8,512]{1,0:T(8,128)S(1)}, f32[8,512]{1,0:T(8,128)S(1)}) custom-call(s32[11]{0:T(128)} %concatenate.15.refs_0_, f32[2]{0:T(128)} %fusion.6.refs_1_.refs_2_, f32[16,512]{1,0:T(8,128)S(1)} %concatenate.16.refs_3_.refs_2_, f32[1728,512]{1,0:T(8,128)S(1)} %get-tuple-element.107.refs_3_, ...), custom_call_target="tpu_custom_call" | custom-call | flops 905969664 | bytes 19365940 | tf_op jit(solution)/shard_map/pallas_call | solution.py:958
  306.3 2.1 collective-permute-start.61
  314.9 13.1 %collective-permute-done.65.refs_6_.refs_7_ = f32[8,512]{1,0:T(8,128)S(1)} collective-permute-done((f32[8,512]{1,0:T(8,128)S(1)}, f32[8,512]{1,0:T(8,128)S(1)}, u32[]{:S(2)}, u32[]{:S(2)}) %collective-permute-start.65) | collective-permute-done | bytes 16416 | tf_op jit(solution)/shard_map/ppermute | solution.py:982
  335.1 2.0 add.312.refs_6_.refs_4_
  338.7 14.8 %shard_map.268.refs_0_ = bf16[512,5632]{1,0:T(8,128)(2,1)} custom-call(bf16[3,1920,512]{2,1,0:T(8,128)(2,1)} %get-tuple-element.91.refs_0_, bf16[1728,512]{1,0:T(8,128)(2,1)} %get-tuple-element.99.refs_1_, bf16[1728,512]{1,0:T(8,128)(2,1)} %get-tuple-element.100.refs_2_, bf16[1728,512]{1,0:T(8,128)(2,1)} %get-tuple-element.106.refs_3_, ...), custom_call_target="tpu_custom_call" | custom-call | flops 8153726976 | bytes 20611072 | tf_op jit(solution)/shard_map/pallas_call | solution.py:958
  353.5 6.2 %collective-permute-done.68.refs_1_.refs_5_ = bf16[1728,512]{1,0:T(8,128)(2,1)S(1)} collective-permute-done((bf16[1728,512]{1,0:T(8,128)(2,1)S(1)}, bf16[1728,512]{1,0:T(8,128)(2,1)S(1)}, u32[]{:S(2)}, u32[]{:S(2)}) %collective-permute-start.68) | collective-permute-done | bytes 1769504 | tf_op jit(solution)/shard_map/ppermute | solution.py:992
  363.4 19.7 %shard_map.270 = (bf16[1728,512]{1,0:T(8,128)(2,1)}, f32[1728,512]{1,0:T(8,128)}, f32[104,512]{1,0:T(8,128)S(1)}, f32[8,512]{1,0:T(8,128)S(1)}) custom-call(s32[11]{0:T(128)} %concatenate.15.refs_0_, f32[2]{0:T(128)} %fusion.6.refs_1_.refs_2_, s32[32]{0:T(128)} %stack.196.refs_1_.refs_2_, f32[16,512]{1,0:T(8,128)S(1)} %concatenate.16.refs_3_.refs_2_, ...), custom_call_target="tpu_custom_call" | custom-call | flops 8153726976 | bytes 21332148 | tf_op jit(solution)/shard_map/pallas_call | solution.py:958
  384.7 2.8 collective-permute-start.72
  389.0 6.2 %shard_map.271.refs_17_.refs_2_ = bf16[512,2304]{1,0:T(8,128)(2,1)} custom-call(bf16[3,1920,128]{2,1,0:T(8,128)(2,1)} %get-tuple-element.123.refs_0_, bf16[1728,512]{1,0:T(8,128)(2,1)} %get-tuple-element.124.refs_1_), custom_call_target="tpu_custom_call" | custom-call | flops 2038431744 | bytes 5603328 | tf_op jit(solution)/shard_map/pallas_call | solution.py:958
  395.3 18.4 %shard_map.272 = (bf16[1728,512]{1,0:T(8,128)(2,1)}, f32[1728,512]{1,0:T(8,128)}, f32[104,512]{1,0:T(8,128)S(1)}, f32[8,512]{1,0:T(8,128)S(1)}) custom-call(s32[11]{0:T(128)} %concatenate.15.refs_0_, f32[2]{0:T(128)} %fusion.6.refs_1_.refs_2_, s32[32]{0:T(128)} %stack.196.refs_1_.refs_2_, f32[16,512]{1,0:T(8,128)S(1)} %concatenate.16.refs_3_.refs_2_, ...), custom_call_target="tpu_custom_call" | custom-call | flops 8153726976 | bytes 21446836 | tf_op jit(solution)/shard_map/pallas_call | solution.py:958
  415.2 4.2 collective-permute-done.75.refs_4_.refs_10_
  419.4 6.2 %shard_map.273.refs_15_ = bf16[512,2304]{1,0:T(8,128)(2,1)} custom-call(bf16[3,1920,128]{2,1,0:T(8,128)(2,1)} %get-tuple-element.129.refs_0_, bf16[1728,512]{1,0:T(8,128)(2,1)} %get-tuple-element.130.refs_1_, bf16[512,2304]{1,0:T(8,128)(2,1)} %shard_map.271.refs_17_.refs_2_, ...), custom_call_target="tpu_custom_call", output_to_operand_aliasing={{}: (2, {})} | custom-call | flops 2038431744 | bytes 7962624 | tf_op jit(solution)/shard_map/pallas_call | solution.py:958
  426.4 1.8 collective-permute-start.77
  428.2 2.1 collective-permute-done.76.refs_11_
  432.1 8.4 %shard_map.274 = (bf16[1920,512]{1,0:T(8,128)(2,1)}, f32[3,512]{1,0:T(4,128)S(1)}, f32[3,512]{1,0:T(4,128)S(1)}, bf16[256,1152]{1,0:T(8,128)(2,1)}, bf16[256,1152]{1,0:T(8,128)(2,1)}) custom-call(s32[11]{0:T(128)} %concatenate.15.refs_0_, s32[32]{0:T(128)} %stack.196.refs_1_.refs_2_, f32[2]{0:T(128)} %fusion.6.refs_1_.refs_2_, ...), custom_call_target="tpu_custom_call" | custom-call | flops 2038431744 | bytes 12267700 | tf_op jit(solution)/shard_map/pallas_call | solution.py:958
  440.6 2.3 collective-permute-done.78.refs_1_.refs_11_
  446.7 9.0 %shard_map.276.refs_1_.refs_11_ = f32[1728,512]{1,0:T(8,128)} custom-call(s32[11]{0:T(128)} %concatenate.15.refs_0_, s32[32]{0:T(128)} %stack.196.refs_1_.refs_2_, bf16[1920,512]{1,0:T(8,128)(2,1)} %get-tuple-element.133.refs_2_, bf16[64,4608]{1,0:T(8,128)(2,1)} %pad_maximum_fusion.refs_4_.refs_1_.refs_3_, bf16[64,4608]{1,0:T(8,128)(2,1)} %copy-done.51, ...), custom_call_target="tpu_custom_call" | custom-call | flops 4076863488 | bytes 10223788 | tf_op jit(solution)/shard_map/pallas_call | solution.py:958
  455.7 7.1 %collective-permute-done.79.refs_2_.refs_3_ = bf16[64,5632]{1,0:T(8,128)(2,1)S(1)} collective-permute-done((bf16[64,5632]{1,0:T(8,128)(2,1)}, bf16[64,5632]{1,0:T(8,128)(2,1)S(1)}, u32[]{:S(2)}, u32[]{:S(2)}) %collective-permute-start.79) | collective-permute-done | bytes 720928 | tf_op jit(solution)/shard_map/ppermute | solution.py:992
  468.0 8.9 %shard_map.278.refs_1_ = f32[1728,512]{1,0:T(8,128)} custom-call(s32[11]{0:T(128)} %concatenate.15.refs_0_, s32[32]{0:T(128)} %stack.196.refs_1_.refs_2_, bf16[1920,512]{1,0:T(8,128)(2,1)} %get-tuple-element.133.refs_2_, bf16[64,4608]{1,0:T(8,128)(2,1)} %pad_maximum_fusion.refs_4_.refs_1_.refs_3_, ...), custom_call_target="tpu_custom_call", output_to_operand_aliasing={{}: (11, {})} | custom-call | flops 4076863488 | bytes 13762732 | tf_op jit(solution)/shard_map/pallas_call | solution.py:958
  482.8 10.5 %collective-permute-done.84.refs_11_.refs_2_ = bf16[64,3456]{1,0:T(8,128)(2,1)} collective-permute-done((bf16[64,3456]{1,0:T(8,128)(2,1)S(1)}, bf16[64,3456]{1,0:T(8,128)(2,1)}, u32[]{:S(2)}, u32[]{:S(2)}) %collective-permute-start.84) | collective-permute-done | bytes 442400 | tf_op jit(solution)/shard_map/ppermute | solution.py:992
  495.9 5.7 %shard_map.280 = (f32[3,9,64,512]{3,2,1,0:T(8,128)}, f32[3,64,512]{2,1,0:T(8,128)}, f32[3,64,512]{2,1,0:T(8,128)}, f32[3,3,512]{2,1,0:T(4,128)}, f32[3,3,512]{2,1,0:T(4,128)}, /*index=5*/bf16[3,432,512]{2,1,0:T(8,128)(2,1)}) custom-call(s32[4]{0:T(128)} %add_add_fusion.1.refs_0_, s32[4]{0:T(128)} %add_add_fusion.2.refs_1_, bf16[64,5632]{1,0:T(8,128)(2,1)S(1)} %copy-done.3, ...), custom_call_target="tpu_custom_call" | custom-call | bytes 10407968 | tf_op jit(solution)/shard_map/pallas_call | solution.py:958
  502.0 4.0 shard_map.281
  (340 shorter events, 103.9 us)
Async XLA Ops:
  7.2 98.3 %all-gather.6.cloned.1.call-start = ((), (), s32[]{:S(2)}) async-start(), calls=%async_computation.2 | async-start | bytes 5308416 | tf_op jit(solution)/shard_map/all_gather | solution.py:1144
  8.8 16.7 %collective-permute-start.3 = (bf16[16,4608]{1,0:T(8,128)(2,1)S(1)}, bf16[16,4608]{1,0:T(8,128)(2,1)S(1)}, u32[]{:S(2)}, u32[]{:S(2)}) collective-permute-start(bf16[16,4608]{1,0:T(8,128)(2,1)S(1)} %shard_map.246), channel_id=1, source_target_pairs={{0,6},{1,7},{2,4},{3,5},{4,2},{5,3},{6,0},{7,1},{8,14},{9,15},{10,... | collective-permute-start | bytes 442376 | tf_op jit(solution)/shard_map/ppermute | solution.py:982
  14.0 12.8 %collective-permute-start.2 = (bf16[16,4608]{1,0:T(8,128)(2,1)S(1)}, bf16[16,4608]{1,0:T(8,128)(2,1)S(1)}, u32[]{:S(2)}, u32[]{:S(2)}) collective-permute-start(bf16[16,4608]{1,0:T(8,128)(2,1)S(1)} %shard_map.246), channel_id=1, source_target_pairs={{0,4},{1,5},{2,6},{3,7},{4,0},{5,1},{6,2},{7,3},{8,12},{9,13},{10,... | collective-permute-start | bytes 442376 | tf_op jit(solution)/shard_map/ppermute | solution.py:982
  14.0 12.8 %collective-permute-start.1 = (bf16[16,4608]{1,0:T(8,128)(2,1)S(1)}, bf16[16,4608]{1,0:T(8,128)(2,1)S(1)}, u32[]{:S(2)}, u32[]{:S(2)}) collective-permute-start(bf16[16,4608]{1,0:T(8,128)(2,1)S(1)} %shard_map.246), channel_id=1, source_target_pairs={{0,2},{1,3},{2,0},{3,1},{4,6},{5,7},{6,4},{7,5},{8,10},{9,11},{10,... | collective-permute-start | bytes 442376 | tf_op jit(solution)/shard_map/ppermute | solution.py:982
  15.6 9.9 %collective-permute-start = (bf16[96,512]{1,0:T(8,128)(2,1)S(1)}, bf16[96,512]{1,0:T(8,128)(2,1)S(1)}, u32[]{:S(2)}, u32[]{:S(2)}) collective-permute-start(bf16[96,512]{1,0:T(8,128)(2,1)S(1)} %select_bitcast_fusion), channel_id=1, source_target_pairs={{0,1},{1,0},{2,3},{3,2},{4,5},{5,4},{6,7},{7,6},{8,9},{9,8},{10,11... | collective-permute-start | bytes 294920 | tf_op jit(solution)/shard_map/ppermute | solution.py:982
  28.6 139.0 %all-gather.8.cloned.1.call-start = ((), (), s32[]{:S(2)}) async-start(), calls=%async_computation.3 | async-start | bytes 1179648 | tf_op jit(solution)/shard_map/all_gather | solution.py:1150
  29.4 172.1 %all-gather.10.cloned.1.call-start = ((), (), s32[]{:S(2)}) async-start(), calls=%async_computation.4 | async-start | bytes 5308416 | tf_op jit(solution)/shard_map/all_gather | solution.py:1151
  30.1 302.9 %all-gather.12.cloned.1.call-start = ((), (), s32[]{:S(2)}) async-start(), calls=%async_computation.7 | async-start | bytes 2211840 | tf_op jit(solution)/shard_map/all_gather | solution.py:1243
  30.2 15.4 %collective-permute-start.4 = (bf16[64,4608]{1,0:T(8,128)(2,1)S(1)}, bf16[64,4608]{1,0:T(8,128)(2,1)S(1)}, u32[]{:S(2)}, u32[]{:S(2)}) collective-permute-start(bf16[64,4608]{1,0:T(8,128)(2,1)S(1)} %copy-done.41), channel_id=1, source_target_pairs={{0,8},{1,17},{2,10},{3,19},{4,12},{5,21},{6,14},{7,23},{8,0},{9,25... | collective-permute-start | bytes 1769480 | tf_op jit(solution)/shard_map/ppermute | solution.py:992
  31.9 14.5 %collective-permute-start.5 = (bf16[64,4608]{1,0:T(8,128)(2,1)S(1)}, bf16[64,4608]{1,0:T(8,128)(2,1)S(1)}, u32[]{:S(2)}, u32[]{:S(2)}) collective-permute-start(bf16[64,4608]{1,0:T(8,128)(2,1)S(1)} %copy-done.41), channel_id=1, source_target_pairs={{0,16},{1,9},{2,18},{3,11},{4,20},{5,13},{6,22},{7,15},{8,24},{9,1... | collective-permute-start | bytes 1769480 | tf_op jit(solution)/shard_map/ppermute | solution.py:992
  47.2 10.3 %collective-permute-start.6 = (bf16[64,4608]{1,0:T(8,128)(2,1)}, bf16[64,4608]{1,0:T(8,128)(2,1)}, u32[]{:S(2)}, u32[]{:S(2)}) collective-permute-start(bf16[64,4608]{1,0:T(8,128)(2,1)} %shard_map.251), channel_id=1, source_target_pairs={{0,16},{1,9},{2,18},{3,11},{4,20},{5,13},{6,22},{7,15},{8,24},{9,1... | collective-permute-start | bytes 1769480 | tf_op jit(solution)/shard_map/ppermute | solution.py:992
  49.4 10.1 %collective-permute-start.7 = (bf16[64,4608]{1,0:T(8,128)(2,1)S(1)}, bf16[64,4608]{1,0:T(8,128)(2,1)S(1)}, u32[]{:S(2)}, u32[]{:S(2)}) collective-permute-start(bf16[64,4608]{1,0:T(8,128)(2,1)S(1)} %copy-done.41), channel_id=1, source_target_pairs={{0,1},{1,0},{2,3},{3,2},{4,5},{5,4},{6,7},{7,6},{8,9},{9,8},{10,11... | collective-permute-start | bytes 1769480 | tf_op jit(solution)/shard_map/ppermute | solution.py:982
  49.4 14.7 %collective-permute-start.8 = (bf16[64,4608]{1,0:T(8,128)(2,1)S(1)}, bf16[64,4608]{1,0:T(8,128)(2,1)}, u32[]{:S(2)}, u32[]{:S(2)}) collective-permute-start(bf16[64,4608]{1,0:T(8,128)(2,1)S(1)} %collective-permute-done.4.refs_5_.refs_4_), channel_id=1, source_target_pairs={{0,1},{1,0},{2,3},{3,2},{4,5},{5,4},{6,7},{7,6},{8,9},{9,8},{10,11... | collective-permute-start | bytes 1769480 | tf_op jit(solution)/shard_map/ppermute | solution.py:982
  49.9 14.8 %collective-permute-start.9 = (bf16[64,4608]{1,0:T(8,128)(2,1)}, bf16[64,4608]{1,0:T(8,128)(2,1)}, u32[]{:S(2)}, u32[]{:S(2)}) collective-permute-start(bf16[64,4608]{1,0:T(8,128)(2,1)} %copy-done.47), channel_id=1, source_target_pairs={{0,1},{1,0},{2,3},{3,2},{4,5},{5,4},{6,7},{7,6},{8,9},{9,8},{10,11... | collective-permute-start | bytes 1769480 | tf_op jit(solution)/shard_map/ppermute | solution.py:982
  57.6 7.1 %collective-permute-start.10 = (bf16[64,4608]{1,0:T(8,128)(2,1)}, bf16[64,4608]{1,0:T(8,128)(2,1)}, u32[]{:S(2)}, u32[]{:S(2)}) collective-permute-start(bf16[64,4608]{1,0:T(8,128)(2,1)} %collective-permute-done.6.refs_7_.refs_6_), channel_id=1, source_target_pairs={{0,1},{1,0},{2,3},{3,2},{4,5},{5,4},{6,7},{7,6},{8,9},{9,8},{10,11... | collective-permute-start | bytes 1769480 | tf_op jit(solution)/shard_map/ppermute | solution.py:982
  60.3 20.6 %collective-permute-start.21 = (bf16[16,4608]{1,0:T(8,128)(2,1)}, bf16[16,4608]{1,0:T(8,128)(2,1)S(1)}, u32[]{:S(2)}, u32[]{:S(2)}) collective-permute-start(bf16[16,4608]{1,0:T(8,128)(2,1)} %shard_map.256), channel_id=1, source_target_pairs={{0,6},{1,7},{2,4},{3,5},{4,2},{5,3},{6,0},{7,1},{8,14},{9,15},{10,... | collective-permute-start | bytes 442376 | tf_op jit(solution)/shard_map/ppermute | solution.py:982
  64.1 27.5 %collective-permute-start.20 = (bf16[16,4608]{1,0:T(8,128)(2,1)}, bf16[16,4608]{1,0:T(8,128)(2,1)S(1)}, u32[]{:S(2)}, u32[]{:S(2)}) collective-permute-start(bf16[16,4608]{1,0:T(8,128)(2,1)} %shard_map.256), channel_id=1, source_target_pairs={{0,4},{1,5},{2,6},{3,7},{4,0},{5,1},{6,2},{7,3},{8,12},{9,13},{10,... | collective-permute-start | bytes 442376 | tf_op jit(solution)/shard_map/ppermute | solution.py:982
  64.1 27.5 %collective-permute-start.19 = (bf16[16,4608]{1,0:T(8,128)(2,1)}, bf16[16,4608]{1,0:T(8,128)(2,1)S(1)}, u32[]{:S(2)}, u32[]{:S(2)}) collective-permute-start(bf16[16,4608]{1,0:T(8,128)(2,1)} %shard_map.256), channel_id=1, source_target_pairs={{0,2},{1,3},{2,0},{3,1},{4,6},{5,7},{6,4},{7,5},{8,10},{9,11},{10,... | collective-permute-start | bytes 442376 | tf_op jit(solution)/shard_map/ppermute | solution.py:982
  92.5 12.1 %collective-permute-start.22 = (bf16[64,4608]{1,0:T(8,128)(2,1)S(1)}, bf16[64,4608]{1,0:T(8,128)(2,1)S(1)}, u32[]{:S(2)}, u32[]{:S(2)}) collective-permute-start(bf16[64,4608]{1,0:T(8,128)(2,1)S(1)} %pad_maximum_fusion.1.refs_10_.refs_17_), channel_id=1, source_target_pairs={{0,8},{1,17},{2,10},{3,19},{4,12},{5,21},{6,14},{7,23},{8,0},{9,25... | collective-permute-start | bytes 1769480 | tf_op jit(solution)/shard_map/ppermute | solution.py:992
  96.9 8.5 %collective-permute-start.12 = (f32[8,512]{1,0:T(8,128)S(1)}, f32[8,512]{1,0:T(8,128)S(1)}, u32[]{:S(2)}, u32[]{:S(2)}) collective-permute-start(f32[8,512]{1,0:T(8,128)S(1)} %slice_add_fusion.13.refs_6_), channel_id=1, source_target_pairs={{0,2},{1,3},{2,0},{3,1},{4,6},{5,7},{6,4},{7,5},{8,10},{9,11},{10,... | collective-permute-start | bytes 49160 | tf_op jit(solution)/shard_map/ppermute | solution.py:982
  96.9 8.5 %collective-permute-start.13 = (f32[8,512]{1,0:T(8,128)S(1)}, f32[8,512]{1,0:T(8,128)S(1)}, u32[]{:S(2)}, u32[]{:S(2)}) collective-permute-start(f32[8,512]{1,0:T(8,128)S(1)} %slice_add_fusion.13.refs_6_), channel_id=1, source_target_pairs={{0,4},{1,5},{2,6},{3,7},{4,0},{5,1},{6,2},{7,3},{8,12},{9,13},{10,... | collective-permute-start | bytes 49160 | tf_op jit(solution)/shard_map/ppermute | solution.py:982
  98.4 7.0 %collective-permute-start.14 = (f32[8,512]{1,0:T(8,128)S(1)}, f32[8,512]{1,0:T(8,128)S(1)}, u32[]{:S(2)}, u32[]{:S(2)}) collective-permute-start(f32[8,512]{1,0:T(8,128)S(1)} %slice_add_fusion.13.refs_6_), channel_id=1, source_target_pairs={{0,6},{1,7},{2,4},{3,5},{4,2},{5,3},{6,0},{7,1},{8,14},{9,15},{10,... | collective-permute-start | bytes 49160 | tf_op jit(solution)/shard_map/ppermute | solution.py:982
  102.7 19.7 %collective-permute-start.23 = (bf16[64,4608]{1,0:T(8,128)(2,1)S(1)}, bf16[64,4608]{1,0:T(8,128)(2,1)S(1)}, u32[]{:S(2)}, u32[]{:S(2)}) collective-permute-start(bf16[64,4608]{1,0:T(8,128)(2,1)S(1)} %pad_maximum_fusion.1.refs_10_.refs_17_), channel_id=1, source_target_pairs={{0,16},{1,9},{2,18},{3,11},{4,20},{5,13},{6,22},{7,15},{8,24},{9,1... | collective-permute-start | bytes 1769480 | tf_op jit(solution)/shard_map/ppermute | solution.py:992
  123.2 10.1 %collective-permute-start.24 = (bf16[64,4608]{1,0:T(8,128)(2,1)}, bf16[64,4608]{1,0:T(8,128)(2,1)S(1)}, u32[]{:S(2)}, u32[]{:S(2)}) collective-permute-start(bf16[64,4608]{1,0:T(8,128)(2,1)} %shard_map.258), channel_id=1, source_target_pairs={{0,16},{1,9},{2,18},{3,11},{4,20},{5,13},{6,22},{7,15},{8,24},{9,1... | collective-permute-start | bytes 1769480 | tf_op jit(solution)/shard_map/ppermute | solution.py:992
  123.6 12.2 %collective-permute-start.25 = (bf16[64,4608]{1,0:T(8,128)(2,1)S(1)}, bf16[64,4608]{1,0:T(8,128)(2,1)S(1)}, u32[]{:S(2)}, u32[]{:S(2)}) collective-permute-start(bf16[64,4608]{1,0:T(8,128)(2,1)S(1)} %pad_maximum_fusion.1.refs_10_.refs_17_), channel_id=1, source_target_pairs={{0,1},{1,0},{2,3},{3,2},{4,5},{5,4},{6,7},{7,6},{8,9},{9,8},{10,11... | collective-permute-start | bytes 1769480 | tf_op jit(solution)/shard_map/ppermute | solution.py:982
  123.6 14.0 %collective-permute-start.26 = (bf16[64,4608]{1,0:T(8,128)(2,1)S(1)}, bf16[64,4608]{1,0:T(8,128)(2,1)S(1)}, u32[]{:S(2)}, u32[]{:S(2)}) collective-permute-start(bf16[64,4608]{1,0:T(8,128)(2,1)S(1)} %collective-permute-done.22.refs_11_.refs_18_), channel_id=1, source_target_pairs={{0,1},{1,0},{2,3},{3,2},{4,5},{5,4},{6,7},{7,6},{8,9},{9,8},{10,11... | collective-permute-start | bytes 1769480 | tf_op jit(solution)/shard_map/ppermute | solution.py:982
  124.1 16.1 %collective-permute-start.27 = (bf16[64,4608]{1,0:T(8,128)(2,1)}, bf16[64,4608]{1,0:T(8,128)(2,1)S(1)}, u32[]{:S(2)}, u32[]{:S(2)}) collective-permute-start(bf16[64,4608]{1,0:T(8,128)(2,1)} %copy-done.55), channel_id=1, source_target_pairs={{0,1},{1,0},{2,3},{3,2},{4,5},{5,4},{6,7},{7,6},{8,9},{9,8},{10,11... | collective-permute-start | bytes 1769480 | tf_op jit(solution)/shard_map/ppermute | solution.py:982
  133.3 10.2 %collective-permute-start.28 = (bf16[64,4608]{1,0:T(8,128)(2,1)S(1)}, bf16[64,4608]{1,0:T(8,128)(2,1)S(1)}, u32[]{:S(2)}, u32[]{:S(2)}) collective-permute-start(bf16[64,4608]{1,0:T(8,128)(2,1)S(1)} %collective-permute-done.24.refs_13_.refs_20_), channel_id=1, source_target_pairs={{0,1},{1,0},{2,3},{3,2},{4,5},{5,4},{6,7},{7,6},{8,9},{9,8},{10,11... | collective-permute-start | bytes 1769480 | tf_op jit(solution)/shard_map/ppermute | solution.py:982
  135.8 5.2 %collective-permute-start.16 = (f32[8,512]{1,0:T(8,128)S(1)}, f32[8,512]{1,0:T(8,128)S(1)}, u32[]{:S(2)}, u32[]{:S(2)}) collective-permute-start(f32[8,512]{1,0:T(8,128)S(1)} %slice_add_fusion.12.refs_6_), channel_id=1, source_target_pairs={{0,2},{1,3},{2,0},{3,1},{4,6},{5,7},{6,4},{7,5},{8,10},{9,11},{10,... | collective-permute-start | bytes 49160 | tf_op jit(solution)/shard_map/ppermute | solution.py:982
  135.8 5.4 %collective-permute-start.17 = (f32[8,512]{1,0:T(8,128)S(1)}, f32[8,512]{1,0:T(8,128)S(1)}, u32[]{:S(2)}, u32[]{:S(2)}) collective-permute-start(f32[8,512]{1,0:T(8,128)S(1)} %slice_add_fusion.12.refs_6_), channel_id=1, source_target_pairs={{0,4},{1,5},{2,6},{3,7},{4,0},{5,1},{6,2},{7,3},{8,12},{9,13},{10,... | collective-permute-start | bytes 49160 | tf_op jit(solution)/shard_map/ppermute | solution.py:982
  137.6 5.9 %collective-permute-start.18 = (f32[8,512]{1,0:T(8,128)S(1)}, f32[8,512]{1,0:T(8,128)S(1)}, u32[]{:S(2)}, u32[]{:S(2)}) collective-permute-start(f32[8,512]{1,0:T(8,128)S(1)} %slice_add_fusion.12.refs_6_), channel_id=1, source_target_pairs={{0,6},{1,7},{2,4},{3,5},{4,2},{5,3},{6,0},{7,1},{8,14},{9,15},{10,... | collective-permute-start | bytes 49160 | tf_op jit(solution)/shard_map/ppermute | solution.py:982
  164.1 6.2 %collective-permute-start.31 = (f32[8,512]{1,0:T(8,128)S(1)}, f32[8,512]{1,0:T(8,128)S(1)}, u32[]{:S(2)}, u32[]{:S(2)}) collective-permute-start(f32[8,512]{1,0:T(8,128)S(1)} %slice_add_fusion.11.refs_5_), channel_id=1, source_target_pairs={{0,4},{1,5},{2,6},{3,7},{4,0},{5,1},{6,2},{7,3},{8,12},{9,13},{10,... | collective-permute-start | bytes 49160 | tf_op jit(solution)/shard_map/ppermute | solution.py:982
  166.5 5.5 %collective-permute-start.32 = (f32[8,512]{1,0:T(8,128)S(1)}, f32[8,512]{1,0:T(8,128)S(1)}, u32[]{:S(2)}, u32[]{:S(2)}) collective-permute-start(f32[8,512]{1,0:T(8,128)S(1)} %slice_add_fusion.11.refs_5_), channel_id=1, source_target_pairs={{0,6},{1,7},{2,4},{3,5},{4,2},{5,3},{6,0},{7,1},{8,14},{9,15},{10,... | collective-permute-start | bytes 49160 | tf_op jit(solution)/shard_map/ppermute | solution.py:982
  182.5 5.5 %collective-permute-start.36 = (f32[8,512]{1,0:T(8,128)S(1)}, f32[8,512]{1,0:T(8,128)S(1)}, u32[]{:S(2)}, u32[]{:S(2)}) collective-permute-start(f32[8,512]{1,0:T(8,128)S(1)} %add.302.refs_4_), channel_id=1, source_target_pairs={{0,6},{1,7},{2,4},{3,5},{4,2},{5,3},{6,0},{7,1},{8,14},{9,15},{10,... | collective-permute-start | bytes 49160 | tf_op jit(solution)/shard_map/ppermute | solution.py:982
  197.1 5.1 collective-permute-start.39
  200.3 5.5 %collective-permute-start.40 = (f32[8,512]{1,0:T(8,128)S(1)}, f32[8,512]{1,0:T(8,128)S(1)}, u32[]{:S(2)}, u32[]{:S(2)}) collective-permute-start(f32[8,512]{1,0:T(8,128)S(1)} %slice_add_fusion.10.refs_6_), channel_id=1, source_target_pairs={{0,6},{1,7},{2,4},{3,5},{4,2},{5,3},{6,0},{7,1},{8,14},{9,15},{10,... | collective-permute-start | bytes 49160 | tf_op jit(solution)/shard_map/ppermute | solution.py:982
  224.8 5.5 %collective-permute-start.44 = (f32[8,512]{1,0:T(8,128)S(1)}, f32[8,512]{1,0:T(8,128)S(1)}, u32[]{:S(2)}, u32[]{:S(2)}) collective-permute-start(f32[8,512]{1,0:T(8,128)S(1)} %slice_add_fusion.9.refs_4_), channel_id=1, source_target_pairs={{0,6},{1,7},{2,4},{3,5},{4,2},{5,3},{6,0},{7,1},{8,14},{9,15},{10,... | collective-permute-start | bytes 49160 | tf_op jit(solution)/shard_map/ppermute | solution.py:982
  237.8 5.1 collective-permute-start.47
  241.1 5.5 %collective-permute-start.48 = (f32[8,512]{1,0:T(8,128)S(1)}, f32[8,512]{1,0:T(8,128)S(1)}, u32[]{:S(2)}, u32[]{:S(2)}) collective-permute-start(f32[8,512]{1,0:T(8,128)S(1)} %slice_add_fusion.8.refs_8_), channel_id=1, source_target_pairs={{0,6},{1,7},{2,4},{3,5},{4,2},{5,3},{6,0},{7,1},{8,14},{9,15},{10,... | collective-permute-start | bytes 49160 | tf_op jit(solution)/shard_map/ppermute | solution.py:982
  242.3 200.6 %reduce-scatter.3.cloned.1.call-start = ((), (), s32[]{:S(2)}) async-start(), calls=%async_computation.5 | async-start | bytes 6488064 | tf_op jit(solution)/shard_map/reduce_scatter | solution.py:1280
  269.9 5.5 %collective-permute-start.52 = (f32[8,512]{1,0:T(8,128)S(1)}, f32[8,512]{1,0:T(8,128)S(1)}, u32[]{:S(2)}, u32[]{:S(2)}) collective-permute-start(f32[8,512]{1,0:T(8,128)S(1)} %add.306.refs_6_), channel_id=1, source_target_pairs={{0,6},{1,7},{2,4},{3,5},{4,2},{5,3},{6,0},{7,1},{8,14},{9,15},{10,... | collective-permute-start | bytes 49160 | tf_op jit(solution)/shard_map/ppermute | solution.py:982
  284.1 5.2 %collective-permute-start.55 = (f32[8,512]{1,0:T(8,128)S(1)}, f32[8,512]{1,0:T(8,128)S(1)}, u32[]{:S(2)}, u32[]{:S(2)}) collective-permute-start(f32[8,512]{1,0:T(8,128)S(1)} %add.307.refs_6_), channel_id=1, source_target_pairs={{0,4},{1,5},{2,6},{3,7},{4,0},{5,1},{6,2},{7,3},{8,12},{9,13},{10,... | collective-permute-start | bytes 49160 | tf_op jit(solution)/shard_map/ppermute | solution.py:982
  287.4 5.5 %collective-permute-start.56 = (f32[8,512]{1,0:T(8,128)S(1)}, f32[8,512]{1,0:T(8,128)S(1)}, u32[]{:S(2)}, u32[]{:S(2)}) collective-permute-start(f32[8,512]{1,0:T(8,128)S(1)} %add.307.refs_6_), channel_id=1, source_target_pairs={{0,6},{1,7},{2,4},{3,5},{4,2},{5,3},{6,0},{7,1},{8,14},{9,15},{10,... | collective-permute-start | bytes 49160 | tf_op jit(solution)/shard_map/ppermute | solution.py:982
  304.4 28.6 %collective-permute-start.57 = (bf16[1728,512]{1,0:T(8,128)(2,1)}, bf16[1728,512]{1,0:T(8,128)(2,1)}, u32[]{:S(2)}, u32[]{:S(2)}) collective-permute-start(bf16[1728,512]{1,0:T(8,128)(2,1)} %get-tuple-element.113), channel_id=1, source_target_pairs={{0,8},{1,17},{2,10},{3,19},{4,12},{5,21},{6,14},{7,23},{8,0},{9,25... | collective-permute-start | bytes 5308424 | tf_op jit(solution)/shard_map/ppermute | solution.py:992
  306.3 5.9 %collective-permute-start.61 = (f32[8,512]{1,0:T(8,128)S(1)}, f32[8,512]{1,0:T(8,128)S(1)}, u32[]{:S(2)}, u32[]{:S(2)}) collective-permute-start(f32[8,512]{1,0:T(8,128)S(1)} %add.308), channel_id=1, source_target_pairs={{0,6},{1,7},{2,4},{3,5},{4,2},{5,3},{6,0},{7,1},{8,14},{9,15},{10,... | collective-permute-start | bytes 49160 | tf_op jit(solution)/shard_map/ppermute | solution.py:982
  308.4 5.4 %collective-permute-start.59 = (f32[8,512]{1,0:T(8,128)S(1)}, f32[8,512]{1,0:T(8,128)S(1)}, u32[]{:S(2)}, u32[]{:S(2)}) collective-permute-start(f32[8,512]{1,0:T(8,128)S(1)} %add.308), channel_id=1, source_target_pairs={{0,2},{1,3},{2,0},{3,1},{4,6},{5,7},{6,4},{7,5},{8,10},{9,11},{10,... | collective-permute-start | bytes 49160 | tf_op jit(solution)/shard_map/ppermute | solution.py:982
  309.8 18.1 %collective-permute-start.65 = (f32[8,512]{1,0:T(8,128)S(1)}, f32[8,512]{1,0:T(8,128)S(1)}, u32[]{:S(2)}, u32[]{:S(2)}) collective-permute-start(f32[8,512]{1,0:T(8,128)S(1)} %get-tuple-element.115.refs_5_.refs_6_), channel_id=1, source_target_pairs={{0,8},{8,0},{16,24},{24,16},{1,9},{9,1},{17,25},{25,17},{2,10},{10... | collective-permute-start | bytes 49160 | tf_op jit(solution)/shard_map/ppermute | solution.py:982
  311.3 17.1 %collective-permute-start.66 = (f32[8,512]{1,0:T(8,128)S(1)}, f32[8,512]{1,0:T(8,128)S(1)}, u32[]{:S(2)}, u32[]{:S(2)}) collective-permute-start(f32[8,512]{1,0:T(8,128)S(1)} %get-tuple-element.115.refs_5_.refs_6_), channel_id=1, source_target_pairs={{0,16},{8,24},{16,0},{24,8},{1,17},{9,25},{17,1},{25,9},{2,18},{10... | collective-permute-start | bytes 49160 | tf_op jit(solution)/shard_map/ppermute | solution.py:982
  312.2 17.9 %collective-permute-start.67 = (f32[8,512]{1,0:T(8,128)S(1)}, f32[8,512]{1,0:T(8,128)S(1)}, u32[]{:S(2)}, u32[]{:S(2)}) collective-permute-start(f32[8,512]{1,0:T(8,128)S(1)} %get-tuple-element.115.refs_5_.refs_6_), channel_id=1, source_target_pairs={{0,24},{8,16},{16,8},{24,0},{1,25},{9,17},{17,9},{25,1},{2,26},{10... | collective-permute-start | bytes 49160 | tf_op jit(solution)/shard_map/ppermute | solution.py:982
  313.9 16.2 %collective-permute-start.62 = (f32[8,512]{1,0:T(8,128)S(1)}, f32[8,512]{1,0:T(8,128)S(1)}, u32[]{:S(2)}, u32[]{:S(2)}) collective-permute-start(f32[8,512]{1,0:T(8,128)S(1)} %add_add_fusion.refs_1_.refs_10_), channel_id=1, source_target_pairs={{0,8},{8,0},{16,24},{24,16},{1,9},{9,1},{17,25},{25,17},{2,10},{10... | collective-permute-start | bytes 49160 | tf_op jit(solution)/shard_map/ppermute | solution.py:982
  337.1 22.6 %collective-permute-start.68 = (bf16[1728,512]{1,0:T(8,128)(2,1)S(1)}, bf16[1728,512]{1,0:T(8,128)(2,1)S(1)}, u32[]{:S(2)}, u32[]{:S(2)}) collective-permute-start(bf16[1728,512]{1,0:T(8,128)(2,1)S(1)} %add.312.refs_6_.refs_4_), channel_id=1, source_target_pairs={{0,16},{1,9},{2,18},{3,11},{4,20},{5,13},{6,22},{7,15},{8,24},{9,1... | collective-permute-start | bytes 5308424 | tf_op jit(solution)/shard_map/ppermute | solution.py:992
  360.9 118.8 %reduce-scatter.5.cloned.1.call-start = ((), (), s32[]{:S(2)}) async-start(), calls=%async_computation.6 | async-start | bytes 2654208 | tf_op jit(solution)/shard_map/reduce_scatter | solution.py:1306
  384.6 10.6 %collective-permute-start.71 = (f32[8,512]{1,0:T(8,128)S(1)}, f32[8,512]{1,0:T(8,128)S(1)}, u32[]{:S(2)}, u32[]{:S(2)}) collective-permute-start(f32[8,512]{1,0:T(8,128)S(1)} %slice_add_fusion.7.refs_9_), channel_id=1, source_target_pairs={{0,2},{1,3},{2,0},{3,1},{4,6},{5,7},{6,4},{7,5},{8,10},{9,11},{10,... | collective-permute-start | bytes 49160 | tf_op jit(solution)/shard_map/ppermute | solution.py:982
  384.7 10.6 %collective-permute-start.72 = (f32[8,512]{1,0:T(8,128)S(1)}, f32[8,512]{1,0:T(8,128)S(1)}, u32[]{:S(2)}, u32[]{:S(2)}) collective-permute-start(f32[8,512]{1,0:T(8,128)S(1)} %slice_add_fusion.7.refs_9_), channel_id=1, source_target_pairs={{0,4},{1,5},{2,6},{3,7},{4,0},{5,1},{6,2},{7,3},{8,12},{9,13},{10,... | collective-permute-start | bytes 49160 | tf_op jit(solution)/shard_map/ppermute | solution.py:982
  387.5 7.8 %collective-permute-start.73 = (f32[8,512]{1,0:T(8,128)S(1)}, f32[8,512]{1,0:T(8,128)S(1)}, u32[]{:S(2)}, u32[]{:S(2)}) collective-permute-start(f32[8,512]{1,0:T(8,128)S(1)} %slice_add_fusion.7.refs_9_), channel_id=1, source_target_pairs={{0,6},{1,7},{2,4},{3,5},{4,2},{5,3},{6,0},{7,1},{8,14},{9,15},{10,... | collective-permute-start | bytes 49160 | tf_op jit(solution)/shard_map/ppermute | solution.py:982
  426.4 5.6 %collective-permute-start.77 = (f32[8,512]{1,0:T(8,128)S(1)}, f32[8,512]{1,0:T(8,128)S(1)}, u32[]{:S(2)}, u32[]{:S(2)}) collective-permute-start(f32[8,512]{1,0:T(8,128)S(1)} %slice_add_fusion.6.refs_3_.refs_9_), channel_id=1, source_target_pairs={{0,6},{1,7},{2,4},{3,5},{4,2},{5,3},{6,0},{7,1},{8,14},{9,15},{10,... | collective-permute-start | bytes 49160 | tf_op jit(solution)/shard_map/ppermute | solution.py:982
  443.6 19.2 %collective-permute-start.79 = (bf16[64,5632]{1,0:T(8,128)(2,1)}, bf16[64,5632]{1,0:T(8,128)(2,1)S(1)}, u32[]{:S(2)}, u32[]{:S(2)}) collective-permute-start(bf16[64,5632]{1,0:T(8,128)(2,1)} %shard_map.275.refs_2_), channel_id=1, source_target_pairs={{0,8},{1,17},{2,10},{3,19},{4,12},{5,21},{6,14},{7,23},{8,0},{9,25... | collective-permute-start | bytes 2162696 | tf_op jit(solution)/shard_map/ppermute | solution.py:992
  444.5 19.3 %collective-permute-start.80 = (bf16[64,5632]{1,0:T(8,128)(2,1)}, bf16[64,5632]{1,0:T(8,128)(2,1)S(1)}, u32[]{:S(2)}, u32[]{:S(2)}) collective-permute-start(bf16[64,5632]{1,0:T(8,128)(2,1)} %shard_map.275.refs_2_), channel_id=1, source_target_pairs={{0,16},{1,9},{2,18},{3,11},{4,20},{5,13},{6,22},{7,15},{8,24},{9,1... | collective-permute-start | bytes 2162696 | tf_op jit(solution)/shard_map/ppermute | solution.py:992
  446.3 17.5 %collective-permute-start.82 = (bf16[128,1152]{1,0:T(8,128)(2,1)S(1)}, bf16[128,1152]{1,0:T(8,128)(2,1)S(1)}, u32[]{:S(2)}, u32[]{:S(2)}) collective-permute-start(bf16[128,1152]{1,0:T(8,128)(2,1)S(1)} %get-tuple-element.148), channel_id=1, source_target_pairs={{0,2},{1,3},{2,0},{3,1},{4,6},{5,7},{6,4},{7,5},{8,10},{9,11},{10,... | collective-permute-start | bytes 884744 | tf_op jit(solution)/shard_map/ppermute | solution.py:982
  462.9 14.1 %collective-permute-start.81 = (bf16[64,5632]{1,0:T(8,128)(2,1)S(1)}, bf16[64,5632]{1,0:T(8,128)(2,1)S(1)}, u32[]{:S(2)}, u32[]{:S(2)}) collective-permute-start(bf16[64,5632]{1,0:T(8,128)(2,1)S(1)} %collective-permute-done.79.refs_2_.refs_3_), channel_id=1, source_target_pairs={{0,16},{1,9},{2,18},{3,11},{4,20},{5,13},{6,22},{7,15},{8,24},{9,1... | collective-permute-start | bytes 2162696 | tf_op jit(solution)/shard_map/ppermute | solution.py:992
  466.3 10.7 %collective-permute-start.83 = (bf16[64,1152]{1,0:T(8,128)(2,1)S(1)}, bf16[64,1152]{1,0:T(8,128)(2,1)S(1)}, u32[]{:S(2)}, u32[]{:S(2)}) collective-permute-start(bf16[64,1152]{1,0:T(8,128)(2,1)S(1)} %slice_add_fusion.2), channel_id=1, source_target_pairs={{0,4},{1,5},{2,6},{3,7},{4,0},{5,1},{6,2},{7,3},{8,12},{9,13},{10,... | collective-permute-start | bytes 442376 | tf_op jit(solution)/shard_map/ppermute | solution.py:982
  480.7 12.7 %collective-permute-start.84 = (bf16[64,3456]{1,0:T(8,128)(2,1)S(1)}, bf16[64,3456]{1,0:T(8,128)(2,1)}, u32[]{:S(2)}, u32[]{:S(2)}) collective-permute-start(bf16[64,3456]{1,0:T(8,128)(2,1)S(1)} %pad_maximum_fusion.2.refs_1_), channel_id=1, source_target_pairs={{0,8},{1,17},{2,10},{3,19},{4,12},{5,21},{6,14},{7,23},{8,0},{9,25... | collective-permute-start | bytes 1327112 | tf_op jit(solution)/shard_map/ppermute | solution.py:992
  481.2 20.4 %collective-permute-start.85 = (bf16[64,3456]{1,0:T(8,128)(2,1)S(1)}, bf16[64,3456]{1,0:T(8,128)(2,1)}, u32[]{:S(2)}, u32[]{:S(2)}) collective-permute-start(bf16[64,3456]{1,0:T(8,128)(2,1)S(1)} %pad_maximum_fusion.2.refs_1_), channel_id=1, source_target_pairs={{0,16},{1,9},{2,18},{3,11},{4,20},{5,13},{6,22},{7,15},{8,24},{9,1... | collective-permute-start | bytes 1327112 | tf_op jit(solution)/shard_map/ppermute | solution.py:992
  493.4 8.6 %collective-permute-start.86 = (bf16[64,3456]{1,0:T(8,128)(2,1)}, bf16[64,3456]{1,0:T(8,128)(2,1)}, u32[]{:S(2)}, u32[]{:S(2)}) collective-permute-start(bf16[64,3456]{1,0:T(8,128)(2,1)} %collective-permute-done.84.refs_11_.refs_2_), channel_id=1, source_target_pairs={{0,16},{1,9},{2,18},{3,11},{4,20},{5,13},{6,22},{7,15},{8,24},{9,1... | collective-permute-start | bytes 1327112 | tf_op jit(solution)/shard_map/ppermute | solution.py:992
  (95 other events, 706.4 us)
Sparse Core Ops, SparseCore 0:
  28.7 65.6 all-gather.5
  96.0 20.8 all-gather.7
  119.1 53.8 all-gather.9
  242.4 31.7 all-gather.11
  361.1 65.1 reduce-scatter.2
  428.4 39.4 reduce-scatter.4
